TPU v7x, 128 devices: a whole 4x4x4 slice. The times are simulated.
128 devices in a mesh: space: 16 (over z_hi, y, core), filt: 8 (over z_lo, x).
Axes of the slice: x: 4, y: 4, z: 4 (z_hi: 2, z_lo: 2; z = z_hi * 2 + z_lo), core: 2. Of those that a mesh axis runs over, the one named last changes fastest.
Arguments:
- volume: bfloat16 [4, 128, 32, 1024], P(None, None, 'space'), may hold values from -6 to 6
- kernel: bfloat16 [3, 3, 3, 256, 128], P(None, None, None, 'filt'), may hold values from -0.109375 to 0.109375
- out_grad: bfloat16 [4, 256, 16, 256], P(None, 'filt', 'space'), may hold values from -6 to 6
Outputs:
- output: bfloat16 [4, 256, 16, 256], P(None, 'filt', 'space')
- input_grad: bfloat16 [4, 128, 32, 1024], P(None, None, 'space', 'filt')
- kernel_grad: float32 [3, 3, 3, 256, 128], P(None, None, None, 'filt')
All inputs are finite; a program needn't handle non-finite values.
Results may differ from a plain program's by a relative error of at most 0.0034.
Values may be sent and summed in bfloat16 or wider, within the bound.
No kernel may reach another device: no remote copies, remote signals or barrier semaphores. Data moves between devices by JAX's collectives and lax.ppermute only.
A program may use at most 256 MiB of HBM per device.

v0:
```python
import jax
import jax.numpy as jnp
from jax import lax
from jax.sharding import PartitionSpec as P

EDGE = 32
HALF = 16


def conv_forward(volume_in, weights, padding):
    return lax.conv_general_dilated(
        volume_in,
        weights,
        (2, 2, 2),
        padding,
        dimension_numbers=("NCDHW", "DHWOI", "NCDHW"),
        preferred_element_type=jnp.float32,
    )


def conv_back_input(grads_in, weights, padding):
    flipped = weights[::-1, ::-1, ::-1]
    return lax.conv_general_dilated(
        grads_in,
        flipped,
        (1, 1, 1),
        padding,
        lhs_dilation=(2, 2, 2),
        dimension_numbers=("NCDHW", "DHWIO", "NCDHW"),
        preferred_element_type=jnp.float32,
    )


def conv_back_kernel(volume_in, grads_in, padding):
    return lax.conv_general_dilated(
        volume_in,
        grads_in,
        (1, 1, 1),
        padding,
        rhs_dilation=(2, 2, 2),
        dimension_numbers=("CNDHW", "IODHW", "DHWCN"),
        preferred_element_type=jnp.float32,
    )


def spread(values_in, side_len):
    return values_in.reshape(
        values_in.shape[0],
        values_in.shape[1],
        values_in.shape[2],
        values_in.shape[3] // side_len,
        side_len,
    )


def flatten(values_in):
    return values_in.reshape(
        values_in.shape[0],
        values_in.shape[1],
        values_in.shape[2],
        values_in.shape[3] * values_in.shape[4],
    )


def body(volume, kernel, out_grad):
    position = lax.axis_index("space")
    block_width = kernel.shape[4] // lax.axis_size("space")
    own_channels = spread(
        lax.all_to_all(volume, "space", split_axis=1, concat_axis=2, tiled=True), EDGE
    )
    ker_block = lax.dynamic_slice_in_dim(kernel, position * block_width, block_width, 4)
    partial_out = flatten(conv_forward(own_channels, ker_block, ((1, 0), (1, 0), (1, 0))))
    output = lax.psum_scatter(partial_out, "space", scatter_dimension=2, tiled=True).astype(
        jnp.bfloat16
    )
    grad_whole = spread(lax.all_gather(out_grad, "space", axis=2, tiled=True), HALF)
    vol_term = flatten(conv_back_input(grad_whole, ker_block, ((1, 2), (1, 2), (1, 2))))
    summed = lax.psum_scatter(vol_term, "filt", scatter_dimension=3, tiled=True).astype(
        jnp.bfloat16
    )
    input_grad = lax.all_to_all(summed, "space", split_axis=2, concat_axis=1, tiled=True)
    ker_term = conv_back_kernel(own_channels, grad_whole, ((1, 0), (1, 0), (1, 0)))
    kernel_grad = lax.all_gather(ker_term, "space", axis=4, tiled=True)
    return (output, input_grad, kernel_grad)


def solution(mesh):
    return jax.shard_map(
        body,
        mesh=mesh,
        in_specs=(
            P(None, None, "space", None),
            P(None, None, None, "filt", None),
            P(None, "filt", "space", None),
        ),
        out_specs=(
            P(None, "filt", "space", None),
            P(None, None, "space", "filt"),
            P(None, None, None, "filt", None),
        ),
        check_vma=False,
    )
```

profile of v0, /device:TPU:1, one launch (start us, length us, event | category | flops | bytes accessed | tf_op | source)
XLA Modules:
  0.0 659.2 jit_solution(842129894069244331)
XLA Ops:
  7.9 5.3 copy.46
  13.2 9.3 %all-to-all-start = ((bf16[4,128,2,1024]{3,2,0,1:T(2,128)(2,1)}), bf16[4,128,2,1024]{3,2,0,1:T(2,128)(2,1)S(1)}, u32[]{:S(2)}, u32[]{:S(2)}) async-start(bf16[4,128,2,1024]{3,2,0,1:T(2,128)(2,1)} %copy.46), calls=%async_computation | async-start | bytes 4194304 | tf_op jit(solution)/shard_map/all_to_all | solution.py:69
  22.7 44.9 %all-gather.2.cloned.1.call-done = bf16[4,32,16,256]{3,1,2,0:T(8,128)(2,1)} async-done(((bf16[4,32,1,256]{3,1,2,0:T(8,128)(2,1)}), bf16[4,32,16,256]{3,1,2,0:T(8,128)(2,1)}) %all-gather.2.cloned.1.call-update) | async-done | bytes 1048592 | tf_op jit(solution)/shard_map/all_gather | solution.py:76
  67.6 6.7 %copy.55 = bf16[4,32,16,256]{1,0,3,2:T(4,128)(2,1)} copy(bf16[4,32,16,256]{3,1,2,0:T(8,128)(2,1)} %all-gather.2.cloned.1.call-done) | data formatting | bytes 2097152 | tf_op jit(solution)/shard_map/all_gather | solution.py:76
  74.3 4.7 pad.2
  81.3 91.6 %broadcast_select_fusion = f32[32,32,32,6,8]{2,4,3,1,0:T(8,128)} fusion(pred[32,6]{0,1:T(8,128)(4,1)S(1)} %copy-done.2, bf16[32,16,16,4,7,1]{0,4,3,5,2,1:T(8,128)(2,1)S(1)} %slice.6, bf16[32,16,16,4,8,3]{0,4,3,5,2,1:T(8,128)(2,1)S(1)} %copy.57, bf16[3,3,3,32,8]{4,3,2,1,0:T(8,128)(2,1)S(1)} %fusion.33), kind=kOutput, calls=%fused_computation.6 | convolution fusion | flops 333594624 | bytes 8337088 | tf_op jit(solution)/shard_map/conv_general_dilated | solution.py:23
  172.9 26.7 %copy.58 = f32[32,32,32,6,8]{1,4,3,2,0:T(8,128)} copy(f32[32,32,32,6,8]{2,4,3,1,0:T(8,128)} %broadcast_select_fusion) | data formatting | bytes 12582912 | tf_op jit(solution)/shard_map/conv_general_dilated | solution.py:23
  199.6 11.6 %slice_bitcast_fusion = f32[4,8,32,32,32]{3,1,4,0,2:T(8,128)} fusion(f32[32,32,4,48,8]{1,4,3,2,0:T(8,128)} %bitcast.46), kind=kLoop, calls=%fused_computation.3 | loop fusion | bytes 8388608 | tf_op jit(solution)/shard_map/conv_general_dilated | solution.py:23
  211.2 17.4 %copy.59 = f32[4,8,32,32,32]{4,3,2,1,0:T(8,128)} copy(f32[4,8,32,32,32]{3,1,4,0,2:T(8,128)} %slice_bitcast_fusion) | data formatting | bytes 8388608 | tf_op jit(solution)/shard_map/conv_general_dilated | solution.py:23
  228.6 13.7 %reshape.22 = f32[4,8,32,1024]{3,2,1,0:T(8,128)} reshape(f32[4,8,32,32,32]{4,3,2,1,0:T(8,128)} %copy.59) | data formatting | bytes 8388608 | tf_op jit(solution)/shard_map/reshape | solution.py:57
  242.5 34.8 %copy.47 = bf16[4,16,8,2,1024]{2,0,4,3,1:T(4,128)(2,1)} copy(bf16[4,16,8,2,1024]{4,3,0,2,1:T(2,128)(2,1)S(1)} %bitcast.53) | data formatting | bytes 4194304 | tf_op jit(solution)/shard_map/all_to_all | solution.py:69
  277.4 38.9 %pad = bf16[8,32,32,4,48]{0,3,4,2,1:T(4,128)(2,1)} pad(bf16[8,32,32,4,32]{0,3,4,2,1:T(4,128)(2,1)} %bitcast.44, bf16[]{:T(256)} %constant.14), padding=0_0x0_0x0_0x0_0x1_15 | pad | bytes 5242882 | tf_op jit(solution)/shard_map/reshape | solution.py:47
  316.3 80.4 %copy.49 = bf16[8,32,32,4,8,6]{2,5,4,3,1,0:T(8,128)(2,1)} copy(bf16[8,32,32,4,8,6]{0,3,5,4,2,1:T(4,128)(2,1)} %bitcast.43) | data formatting | bytes 6291456 | tf_op jit(solution)/shard_map/conv_general_dilated | solution.py:11
  396.7 6.3 slice.4
  403.0 17.5 %fusion.1 = bf16[8,32,32,4,8,8]{2,5,4,3,1,0:T(8,128)(2,1)} fusion(bf16[8,32,32,4,7,2]{2,5,4,3,1,0:T(2,128)(2,1)S(1)} %slice.4, bf16[8,32,32,4,8,6]{2,5,4,3,1,0:T(8,128)(2,1)} %copy.49), kind=kLoop, calls=%fused_computation.2 | loop fusion | flops 12582912 | bytes 8257536 | tf_op jit(solution)/shard_map/conv_general_dilated | solution.py:11
  420.5 36.8 %copy.51 = bf16[8,32,32,32,8]{3,0,4,2,1:T(8,128)(2,1)} copy(bf16[8,32,32,32,8]{2,4,3,1,0:T(8,128)(2,1)} %bitcast.47) | data formatting | bytes 8388608 | tf_op jit(solution)/shard_map/conv_general_dilated | solution.py:11
  457.3 69.3 %broadcast_select_fusion.1 = f32[16,16,32,3,32]{4,2,3,1,0:T(8,128)} fusion(pred[32,3]{0,1:T(4,128)(4,1)S(1)} %copy-done.3, bf16[8,32,32,32,8]{3,0,4,2,1:T(8,128)(2,1)} %copy.51, bf16[3,3,3,32,8]{4,3,2,1,0:T(8,128)(2,1)S(1)} %fusion.35), kind=kOutput, calls=%fused_computation.14 | convolution fusion | flops 326516736 | bytes 7353952 | tf_op jit(solution)/shard_map/conv_general_dilated | solution.py:11
  526.6 18.8 %copy.52 = f32[16,16,32,3,32]{4,1,3,2,0:T(8,128)} copy(f32[16,16,32,3,32]{4,2,3,1,0:T(8,128)} %broadcast_select_fusion.1) | data formatting | bytes 6291456 | tf_op jit(solution)/shard_map/conv_general_dilated | solution.py:11
  545.4 3.9 slice_bitcast_fusion.1
  549.3 7.3 %copy.53 = f32[4,32,16,16,16]{1,4,3,2,0:T(8,128)} copy(f32[4,32,16,16,16]{1,3,4,0,2:T(8,128)S(1)} %slice_bitcast_fusion.1) | data formatting | bytes 4194304 | tf_op jit(solution)/shard_map/conv_general_dilated | solution.py:11
  556.6 6.2 copy.54
  562.9 49.9 %fusion.20 = f32[3,3,3,32,8]{3,4,2,1,0:T(8,128)S(1)} fusion(bf16[4,8,32,32,32]{1,0,4,3,2:T(4,128)(2,1)} %bitcast.45, bf16[4,32,16,16,16]{1,0,4,3,2:T(4,128)(2,1)} %bitcast.52), kind=kOutput, calls=%fused_computation.25 | convolution fusion | flops 212629504 | bytes 3173376 | tf_op jit(solution)/shard_map/conv_general_dilated | solution.py:35
  614.7 4.0 all-to-all-start.1
  618.7 29.9 %all_gather.7 = f32[3,3,3,32,128]{3,4,2,1,0:T(8,128)S(1)} all-gather(f32[3,3,3,32,8]{3,4,2,1,0:T(8,128)S(1)} %fusion.20), channel_id=1, replica_groups=mesh['space'=16,'filt'=8] {'space'}, dimensions={4}, use_global_device_ids=true | all-gather | bytes 470016 | tf_op jit(solution)/shard_map/all_gather | solution.py:83
  (28 shorter events, 9.1 us)
Async XLA Ops:
  7.2 15.4 %copy-start = (bf16[3,3,3,32,128]{4,3,2,1,0:T(8,128)(2,1)S(1)}, bf16[3,3,3,32,128]{4,3,2,1,0:T(8,128)(2,1)}, u32[]{:S(2)}) copy-start(bf16[3,3,3,32,128]{4,3,2,1,0:T(8,128)(2,1)} %param.4) | copy-start | bytes 663556
  7.2 60.4 %all-gather.2.cloned.1.call-start = ((), (), s32[]{:S(2)}) async-start(), calls=%async_computation.5 | async-start | bytes 1114112 | tf_op jit(solution)/shard_map/all_gather | solution.py:76
  13.2 229.3 %all-to-all-start = ((bf16[4,128,2,1024]{3,2,0,1:T(2,128)(2,1)}), bf16[4,128,2,1024]{3,2,0,1:T(2,128)(2,1)S(1)}, u32[]{:S(2)}, u32[]{:S(2)}) async-start(bf16[4,128,2,1024]{3,2,0,1:T(2,128)(2,1)} %copy.46), calls=%async_computation | async-start | bytes 4194304 | tf_op jit(solution)/shard_map/all_to_all | solution.py:69
  22.5 590.3 %reduce-scatter.5.cloned.1.call-start = ((), (), s32[]{:S(2)}) async-start(), calls=%async_computation.6 | async-start | bytes 4718592 | tf_op jit(solution)/shard_map/reduce_scatter | solution.py:78
  74.3 7.0 %copy-start.2 = (pred[32,6]{0,1:T(8,128)(4,1)S(1)}, pred[32,6]{0,1:T(8,128)(4,1)}, u32[]{:S(2)}) copy-start(pred[32,6]{0,1:T(8,128)(4,1)} %constant.23) | copy-start | bytes 580
  242.3 407.6 %reduce-scatter.3.cloned.1.call-start = ((), (), s32[]{:S(2)}) async-start(), calls=%async_computation.4 | async-start | bytes 2228224 | tf_op jit(solution)/shard_map/reduce_scatter | solution.py:73
  420.5 36.8 %copy-start.3 = (pred[32,3]{0,1:T(4,128)(4,1)S(1)}, pred[32,3]{0,1:T(4,128)(4,1)}, u32[]{:S(2)}) copy-start(pred[32,3]{0,1:T(4,128)(4,1)} %constant.22) | copy-start | bytes 292
  562.9 89.6 %copy-start.1 = (bf16[3,3,3,32,128]{4,3,2,1,0:T(8,128)(2,1)S(1)}, bf16[3,3,3,32,128]{4,3,2,1,0:T(8,128)(2,1)}, u32[]{:S(2)}) copy-start(bf16[3,3,3,32,128]{4,3,2,1,0:T(8,128)(2,1)} %param.4) | copy-start | bytes 663556
  614.7 36.8 %all-to-all-start.1 = ((bf16[4,8,32,128]{3,1,0,2:T(8,128)(2,1)}), bf16[4,8,32,128]{3,1,0,2:T(8,128)(2,1)S(1)}, u32[]{:S(2)}, u32[]{:S(2)}) async-start(bf16[4,8,32,128]{3,1,0,2:T(8,128)(2,1)} %copy.60), calls=%async_computation.3 | async-start | bytes 524288 | tf_op jit(solution)/shard_map/all_to_all | solution.py:81
Sparse Core Ops, SparseCore 0:
  10.5 57.0 all-gather.1
  242.5 51.2 reduce-scatter.4
  563.0 69.6 reduce-scatter.2
where the time goes:
time: 668 us; the launch traced here: 659 us
  local copies, waits for them, and re-layouts  325 us (49%)
  matrix products  211 us (32%)
  waiting for transfers between devices  45.6 us (7%)
  blocking collectives  29.9 us (4%)
  other arithmetic  20.1 us (3%)
  between operations  14.1 us (2%)
  starting transfers between devices  13.5 us (2%)
    conv_general_dilated x7, local copies, waits for them, and re-layouts, conv_forward(): lax.conv_general_dilated(volume_in, weights, (2, 2, 2), padding, dimensio...  154 us
    conv_general_dilated x1, matrix products, conv_back_input(): lax.conv_general_dilated(grads_in, flipped, (1, 1, 1), padding, lhs_dilat...  91.6 us
    conv_general_dilated x1, matrix products, conv_forward(): lax.conv_general_dilated(volume_in, weights, (2, 2, 2), padding, dimensio...  69.3 us
    conv_general_dilated x6, local copies, waits for them, and re-layouts, conv_back_input(): lax.conv_general_dilated(grads_in, flipped, (1, 1, 1), padding, lhs_dilat...  58.1 us
    conv_general_dilated x1, matrix products, conv_back_kernel(): lax.conv_general_dilated(volume_in, grads_in, (1, 1, 1), padding, rhs_dil...  49.9 us
    all_gather x1, waiting for transfers between devices, body(): lax.all_gather(out_grad, 'space', axis=2, tiled=True)  44.9 us
    reshape x2, local copies, waits for them, and re-layouts, spread(): values_in.reshape(values_in.shape[0], values_in.shape[1], values_in.shape...  43.6 us
    all_to_all x1, local copies, waits for them, and re-layouts, body(): lax.all_to_all(volume, 'space', split_axis=1, concat_axis=2, tiled=True)  34.8 us
  transfers between devices with their start and end apart: 5, of which 1 were waited for; matrix products, arithmetic and copies ran while one was open for 84% of the time, Pallas kernels for 0%

commit v1 on v0

v1 whole, which is shorter than its diff:
```python
import jax
import jax.numpy as jnp
from jax import lax
from jax.experimental import pallas as pl
from jax.experimental.pallas import tpu as pltpu
from jax.sharding import PartitionSpec as P

B = 4
CIN = 128
EDGE = 32
HALF = 16
F32 = jnp.float32
BF16 = jnp.bfloat16
NT = (((1,), (1,)), ((), ()))
ROWS = 896


def iota(shape, axis):
    return lax.broadcasted_iota(jnp.int32, shape, axis)


def conv_kernel(vol_ref, ker_ref, g_ref, gn_ref, own_ref, send_ref, dw_ref,
                perm, select, planes, cols):
    step = pl.program_id(0)

    @pl.when(step == 0)
    def _():
        row, col = iota((256, 256), 0), iota((256, 256), 1)
        source = (row & 15) * 16 + ((row >> 4) & 7) * 2 + (row >> 7)
        perm[...] = jnp.where(col == source, 1.0, 0.0).astype(BF16)
        row, col = iota((192, 128), 0), iota((192, 128), 1)
        depth = (row & 15) * 2 + (row >> 6) - 1
        wanted = (col == ((row >> 4) & 3) * 32 + depth) & (depth >= 0)
        select[...] = jnp.where(wanted, 1.0, 0.0).astype(BF16)
        dw_ref[...] = jnp.zeros_like(dw_ref)
        for x in range(2):
            for k in range(3):
                planes[x, k, 0] = jnp.zeros((HALF, CIN), BF16)

    for group in range(8):
        block = vol_ref[0, group * 256:(group + 1) * 256, :]
        moved = jnp.dot(perm[...], block, preferred_element_type=F32).astype(BF16)
        for x in range(2):
            for lt in range(8):
                start = (x * 8 + lt) * 16
                cols[lt, x * 128 + group * 16:x * 128 + group * 16 + 16, :] = moved[start:start + 16]
    for lt in range(8):
        turned = lax.dot_general(select[...], cols[lt], NT, preferred_element_type=F32).astype(BF16)
        for k in range(3):
            for y in range(4):
                start = k * 64 + y * 16
                for x in range(2):
                    planes[x, k, 1 + 4 * lt + y] = turned[start:start + 16, x * 128:(x + 1) * 128]

    def columns(x):
        parts = []
        for j in range(3):
            for k in range(3):
                rows = [planes[x, k, 2 * q + j] for q in range(HALF)]
                parts.append(jnp.concatenate(rows, 0))
        return jnp.concatenate(parts, 1)

    def weights(i):
        return jnp.concatenate([ker_ref[i * 9 + t] for t in range(9)], 1)

    grad = g_ref[0]
    pair = jnp.concatenate([grad, gn_ref[0]], 0)
    even = columns(0)
    here = lax.dot_general(weights(1), even, NT, preferred_element_type=F32)
    back_even = jnp.dot(grad, even, preferred_element_type=F32)
    odd = columns(1)
    both = lax.dot_general(
        jnp.concatenate([weights(2), weights(0)], 0), odd, NT, preferred_element_type=F32
    )
    back_odd = jnp.dot(pair, odd, preferred_element_type=F32)
    own_ref[0] = here + both[:32]
    send_ref[0] = both[32:]
    for t in range(9):
        lanes = slice(t * 128, (t + 1) * 128)
        dw_ref[t * 32:(t + 1) * 32] += back_odd[32:, lanes]
        dw_ref[(9 + t) * 32:(10 + t) * 32] += back_even[:, lanes]
        dw_ref[(18 + t) * 32:(19 + t) * 32] += back_odd[:32, lanes]


def conv_local(vol, ker, g, gn):
    per_sample = lambda *shape: pl.BlockSpec((1,) + shape, lambda b: (b,) + (0,) * len(shape))
    whole = lambda *shape: pl.BlockSpec(shape, lambda b: (0,) * len(shape))
    return pl.pallas_call(
        conv_kernel,
        grid=(B,),
        in_specs=[per_sample(2048, 128), whole(27, 32, CIN), per_sample(32, 256), per_sample(32, 256)],
        out_specs=[per_sample(32, 256), per_sample(32, 256), whole(ROWS, CIN)],
        out_shape=[
            jax.ShapeDtypeStruct((B, 32, 256), F32),
            jax.ShapeDtypeStruct((B, 32, 256), F32),
            jax.ShapeDtypeStruct((ROWS, CIN), F32),
        ],
        scratch_shapes=[
            pltpu.VMEM((256, 256), BF16),
            pltpu.VMEM((192, 128), BF16),
            pltpu.VMEM((2, 3, EDGE + 1, HALF, CIN), BF16),
            pltpu.VMEM((8, 256, 128), BF16),
        ],
        compiler_params=pltpu.CompilerParams(vmem_limit_bytes=40 * 1024 * 1024),
        cost_estimate=pl.CostEstimate(flops=6_000_000_000, bytes_accessed=4_000_000, transcendentals=0),
        name="conv_local",
    )(vol, ker, g, gn)


def spread_kernel(g_ref, gn_ref, out_ref):
    for b in range(B):
        for f in range(8):
            parts = []
            for ref in (g_ref, gn_ref):
                whole = jnp.concatenate([ref[b], jnp.zeros((32, 128), BF16)], 1)
                parts.append(whole[:, 32 * f:32 * f + 64])
            out_ref[f, b] = jnp.concatenate(parts, 1)


def spread(g, gn):
    return pl.pallas_call(
        spread_kernel,
        out_shape=jax.ShapeDtypeStruct((8, B, 32, 128), BF16),
        name="spread",
    )(g, gn)


def input_grad_kernel(ker_ref, g_ref, out_ref, grads, mixed, paired):
    last = (iota((128, 256), 0) & 15) == 15
    for b in range(B):
        block = g_ref[:, b].reshape(256, 128).astype(F32)
        turned = jnp.transpose(block)
        later = jnp.where(last, 0.0, pltpu.roll(turned, 127, 0))
        for shift, value in enumerate((turned, later)):
            low = value.astype(BF16)
            for p in range(2):
                for q in range(3):
                    start = p * 64 + q * 16
                    grads[p, shift, q, b] = low[start:start + 16]

    def lhs(p, qs, rs):
        rows = [grads[p, rs, qs + q, b] for q in range(2) for b in range(B)]
        return jnp.concatenate(rows, 0)

    def tap(i, j, k):
        return ker_ref[:, i * 9 + j * 3 + k].reshape(256, CIN)

    choices = (((1, 0),), ((2, 0), (0, 1)))
    for py in range(2):
        for pz in range(2):
            total = jnp.zeros((128, 256), F32)
            extra = jnp.zeros((128, 128), F32)
            for j, qs in choices[py]:
                for k, rs in choices[pz]:
                    two = jnp.concatenate([tap(1, j, k), tap(2, j, k)], 1)
                    total += jnp.dot(lhs(0, qs, rs), two, preferred_element_type=F32)
                    extra += jnp.dot(lhs(1, qs, rs), tap(0, j, k), preferred_element_type=F32)
            values = (total[:, :128], total[:, 128:] + extra)
            for px in range(2):
                for q in range(2):
                    for b in range(B):
                        start = (q * B + b) * 16
                        mixed[px, b, pl.ds((2 * q + py) * 32 + pz, 16, stride=2), :] = (
                            values[px][start:start + 16]
                        )
    for b in range(B):
        for px in range(2):
            paired[b, pl.ds(px, CIN, stride=2), :] = jnp.transpose(mixed[px, b])
        out_ref[b] = paired[b].astype(BF16)


def input_grad_local(ker_all, g_all):
    return pl.pallas_call(
        input_grad_kernel,
        out_shape=jax.ShapeDtypeStruct((B, 2 * CIN, 128), BF16),
        scratch_shapes=[
            pltpu.VMEM((2, 2, 3, B, HALF, 256), BF16),
            pltpu.VMEM((2, B, 128, CIN), F32),
            pltpu.VMEM((B, 2 * CIN, 128), F32),
        ],
        compiler_params=pltpu.CompilerParams(vmem_limit_bytes=40 * 1024 * 1024),
        cost_estimate=pl.CostEstimate(flops=2_000_000_000, bytes_accessed=3_000_000, transcendentals=0),
        name="input_grad_local",
    )(ker_all, g_all)


def sum_kernel(parts_ref, out_ref):
    total = parts_ref[0]
    for i in range(1, 16):
        total = total + parts_ref[i]
    for i in range(16):
        out_ref[i] = total


def sum_and_copy(parts):
    return pl.pallas_call(
        sum_kernel,
        out_shape=jax.ShapeDtypeStruct(parts.shape, parts.dtype),
        name="sum_and_copy",
    )(parts)


def swap(values, axis):
    return lax.all_to_all(values, axis, split_axis=0, concat_axis=0, tiled=True)


def body(volume, kernel, out_grad):
    spaces = lax.axis_size("space")
    g = out_grad.reshape(B, 32, 256)
    ker = kernel.reshape(27, 32, CIN)
    g_next = lax.ppermute(g, "space", [(i + 1, i) for i in range(spaces - 1)])
    ker_all = swap(jnp.broadcast_to(ker[None], (8, 27, 32, CIN)), "filt")
    g_all = swap(spread(g, g_next), "filt")
    vol = volume.reshape(B, CIN, 2, 8, 128).transpose(0, 1, 3, 2, 4).reshape(B, 2048, 128)
    own, send, dw = conv_local(vol, ker, g, g_next)
    came = lax.ppermute(send, "space", [(i, i + 1) for i in range(spaces - 1)])
    dw_mine = sum_and_copy(swap(dw.reshape(16, 56, CIN), "space"))
    dw_all = swap(dw_mine, "space").reshape(ROWS, CIN)
    output = (own + came).astype(BF16).reshape(B, 32, 1, 256)
    input_grad = input_grad_local(ker_all, g_all).reshape(B, CIN, 2, 128)
    kernel_grad = dw_all[:864].reshape(3, 3, 3, 32, CIN)
    return (output, input_grad, kernel_grad)


def solution(mesh):
    return jax.shard_map(
        body,
        mesh=mesh,
        in_specs=(
            P(None, None, "space", None),
            P(None, None, None, "filt", None),
            P(None, "filt", "space", None),
        ),
        out_specs=(
            P(None, "filt", "space", None),
            P(None, None, "space", "filt"),
            P(None, None, None, "filt", None),
        ),
        check_vma=False,
    )
```

time: 668 us -> 96.4 us (0.14); the launches traced: 659 us -> 95.3 us
  local copies, waits for them, and re-layouts: 325 us -> 5.66 us
  matrix products: 211 us -> 0 us
  other arithmetic: 20.1 us -> 0.64 us
  blocking collectives: 29.9 us -> 16.4 us
  between operations: 14.1 us -> 0.67 us
  Pallas kernels: 0 us -> 13 us
  waiting for transfers between devices: 45.6 us -> 36.7 us
  starting transfers between devices: 13.5 us -> 22.3 us
    conv_general_dilated x13 -> x0, local copies, waits for them, and re-layouts: 212 us -> none  [the longest x7 154 us: conv_forward(): lax.conv_general_dilated(volume_in, weights, (2, 2, 2), padding, dimensio...]
    conv_general_dilated x3 -> x0, matrix products: 211 us -> none  [the longest x1 91.6 us: conv_back_input(): lax.conv_general_dilated(grads_in, flipped, (1, 1, 1), padding, lhs_dilat...]
    reshape x4 -> x0, local copies, waits for them, and re-layouts: 63.5 us -> none  [the longest x2 43.6 us: spread(): values_in.reshape(values_in.shape[0], values_in.shape[1], values_in.shape...]
    all_gather x1 -> x0, waiting for transfers between devices: 44.9 us -> none  [body(): lax.all_gather(out_grad, 'space', axis=2, tiled=True)]
    all_to_all x2 -> x0, local copies, waits for them, and re-layouts: 34.9 us -> none  [the longest x1 34.8 us: body(): lax.all_to_all(volume, 'space', split_axis=1, concat_axis=2, tiled=True)]
    all_to_all x2 -> x3, waiting for transfers between devices: 0.01 us -> 31.3 us  [swap(): return lax.all_to_all(values, axis, split_axis=0, concat_axis=0, tiled=True)]
    all_gather x1 -> x0, blocking collectives: 29.9 us -> none  [body(): kernel_grad = lax.all_gather(ker_term, 'space', axis=4, tiled=True)]
    conv_general_dilated x1 -> x0, other arithmetic: 17.5 us -> none  [conv_forward(): lax.conv_general_dilated(volume_in, weights, (2, 2, 2), padding, dimensio...]
  transfers between devices with their start and end apart: 5 -> 5, of which waited for: 1 -> 5; matrix products, arithmetic and copies ran while one was open for 84% -> 2% of each run, Pallas kernels for 0% -> 4%
where the time goes in v1:
time: 96.4 us; the launch traced here: 95.3 us
  waiting for transfers between devices  36.7 us (38%)
  starting transfers between devices  22.3 us (23%)
  blocking collectives  16.4 us (17%)
  Pallas kernels  13 us (13%)
  local copies, waits for them, and re-layouts  5.66 us (6%)
    all_to_all x3, waiting for transfers between devices, swap(): return lax.all_to_all(values, axis, split_axis=0, concat_axis=0, tiled=True)  31.3 us
    all_to_all x3, starting transfers between devices, swap(): return lax.all_to_all(values, axis, split_axis=0, concat_axis=0, tiled=True)  17 us
    all_to_all x1, blocking collectives, swap(): return lax.all_to_all(values, axis, split_axis=0, concat_axis=0, tiled=True)  16.4 us
    pallas_call x1, Pallas kernels, conv_local(): pl.pallas_call(conv_kernel, grid=(B,), in_specs=[per_sample(2048, 128), w...  7.91 us
    ppermute x1, waiting for transfers between devices, body(): g_next = lax.ppermute(g, 'space', [(i + 1, i) for i in range(spaces - 1)])  3.41 us
    unnamed x12, local copies, waits for them, and re-layouts  3.4 us
    ppermute x1, starting transfers between devices, body(): g_next = lax.ppermute(g, 'space', [(i + 1, i) for i in range(spaces - 1)])  3.33 us
  transfers between devices with their start and end apart: 5, of which 5 were waited for; matrix products, arithmetic and copies ran while one was open for 2% of the time, Pallas kernels for 4%

profile of v1, /device:TPU:1, one launch (start us, length us, event | category | flops | bytes accessed | tf_op | source)
XLA Modules:
  0.0 95.3 jit_solution(7812100441920291663)
XLA Ops:
  0.6 3.3 %collective-permute-start = (bf16[4,32,256]{2,1,0:T(8,128)(2,1)}, bf16[4,32,256]{2,1,0:T(8,128)(2,1)S(1)}, u32[]{:S(2)}, u32[]{:S(2)}) collective-permute-start(bf16[4,32,256]{2,1,0:T(8,128)(2,1)} %bitcast.17), channel_id=1, source_target_pairs={{8,0},{16,8},{24,16},{32,24},{40,32},{48,40},{56,48},{64,56},{72,6... | collective-permute-start | bytes 196616 | tf_op jit(solution)/shard_map/ppermute | solution.py:211
  4.0 3.4 %collective-permute-done.gn_ref = bf16[4,32,256]{2,1,0:T(8,128)(2,1)S(1)} collective-permute-done((bf16[4,32,256]{2,1,0:T(8,128)(2,1)}, bf16[4,32,256]{2,1,0:T(8,128)(2,1)S(1)}, u32[]{:S(2)}, u32[]{:S(2)}) %collective-permute-start) | collective-permute-done | bytes 65568 | tf_op jit(solution)/shard_map/ppermute | solution.py:211
  7.4 1.0 %copy-done = bf16[3,3,3,32,128]{4,3,2,1,0:T(8,128)(2,1)S(1)} copy-done((bf16[3,3,3,32,128]{4,3,2,1,0:T(8,128)(2,1)S(1)}, bf16[3,3,3,32,128]{4,3,2,1,0:T(8,128)(2,1)}, u32[]{:S(2)}) %copy-start) | copy-done | bytes 221208
  8.3 0.8 copy-done.2
  9.2 1.6 %copy-done.4 = bf16[4,128,2,1024]{3,2,1,0:T(2,128)(2,1)S(1)} copy-done((bf16[4,128,2,1024]{3,2,1,0:T(2,128)(2,1)S(1)}, bf16[4,128,2,1024]{3,2,1,0:T(2,128)(2,1)}, u32[]{:S(2)}) %copy-start.4) | copy-done | bytes 2097176
  10.8 7.9 %conv_local.1 = (f32[4,32,256]{2,1,0:T(8,128)S(1)}, f32[4,32,256]{2,1,0:T(8,128)S(1)}, f32[896,128]{1,0:T(8,128)}) custom-call(bf16[4,2048,128]{2,1,0:T(8,128)(2,1)S(1)} %bitcast.20, bf16[27,32,128]{2,1,0:T(8,128)(2,1)S(1)} %bitcast.15, bf16[4,32,256]{2,1,0:T(8,128)(2,1)S(1)} %bitcast.19, bf16[4,32,256]{2,1,0:T(8,128)(2,1)S(1)} %collective-permute-done.gn_ref), custom_call_target="tpu_custom_call" | custom-call | flops 6000000000 | bytes 4000000 | tf_op jit(solution)/shard_map/conv_local/pallas_call | solution.py:88
  18.7 0.0 copy-done.3
  18.7 8.0 %all-to-all-start.2 = ((f32[16,56,128]{2,1,0:T(8,128)}), f32[16,56,128]{2,1,0:T(8,128)S(1)}, u32[]{:S(2)}, u32[]{:S(2)}) async-start(f32[16,56,128]{2,1,0:T(8,128)} %bitcast.8), calls=%async_computation.2 | async-start | bytes 917504 | tf_op jit(solution)/shard_map/all_to_all | solution.py:204
  26.7 1.8 %spread.1 = bf16[8,4,32,128]{3,2,1,0:T(8,128)(2,1)} custom-call(bf16[4,32,256]{2,1,0:T(8,128)(2,1)} %bitcast.18, bf16[4,32,256]{2,1,0:T(8,128)(2,1)} %copy-done.3), custom_call_target="tpu_custom_call" | custom-call | tf_op jit(solution)/shard_map/spread/pallas_call | solution.py:121
  28.5 8.7 %all-to-all-done.2.parts_ref = f32[16,56,128]{2,1,0:T(8,128)S(1)} async-done(((f32[16,56,128]{2,1,0:T(8,128)}), f32[16,56,128]{2,1,0:T(8,128)S(1)}, u32[]{:S(2)}, u32[]{:S(2)}) %all-to-all-start.2) | async-done | bytes 458784 | tf_op jit(solution)/shard_map/all_to_all | solution.py:204
  37.2 5.4 %all-to-all-start.1 = ((bf16[8,4,32,128]{3,2,1,0:T(8,128)(2,1)}), bf16[8,4,32,128]{3,2,1,0:T(8,128)(2,1)S(1)}, u32[]{:S(2)}, u32[]{:S(2)}) async-start(bf16[8,4,32,128]{3,2,1,0:T(8,128)(2,1)} %spread.1), calls=%async_computation.1 | async-start | bytes 524288 | tf_op jit(solution)/shard_map/all_to_all | solution.py:204
  42.5 0.0 copy-done.5
  42.5 1.8 %sum_and_copy.1 = f32[16,56,128]{2,1,0:T(8,128)} custom-call(f32[16,56,128]{2,1,0:T(8,128)} %copy-done.5), custom_call_target="tpu_custom_call" | custom-call | tf_op jit(solution)/shard_map/sum_and_copy/pallas_call | solution.py:196
  44.4 4.5 %all-to-all-done.1.g_ref = bf16[8,4,32,128]{3,2,1,0:T(8,128)(2,1)S(1)} async-done(((bf16[8,4,32,128]{3,2,1,0:T(8,128)(2,1)}), bf16[8,4,32,128]{3,2,1,0:T(8,128)(2,1)S(1)}, u32[]{:S(2)}, u32[]{:S(2)}) %all-to-all-start.1) | async-done | bytes 262176 | tf_op jit(solution)/shard_map/all_to_all | solution.py:204
  48.9 16.4 %all_to_all.20 = f32[16,56,128]{2,1,0:T(8,128)S(1)} all-to-all(f32[16,56,128]{2,1,0:T(8,128)} %sum_and_copy.1), channel_id=1, replica_groups=mesh['space'=16,'filt'=8] {'space'}, dimensions={0} | all-to-all | bytes 917504 | tf_op jit(solution)/shard_map/all_to_all | solution.py:204
  65.3 0.0 copy-done.1
  65.3 1.5 %broadcast_in_dim.2 = bf16[8,27,32,128]{3,2,1,0:T(8,128)(2,1)} broadcast(bf16[27,32,128]{2,1,0:T(8,128)(2,1)S(1)} %bitcast.16), dimensions={1,2,3} | broadcast | bytes 1990656 | tf_op jit(solution)/shard_map/broadcast_in_dim | solution.py:212
  66.8 3.6 %all-to-all-start = ((bf16[8,27,32,128]{3,2,1,0:T(8,128)(2,1)}), bf16[8,27,32,128]{3,2,1,0:T(8,128)(2,1)S(1)}, u32[]{:S(2)}, u32[]{:S(2)}) async-start(bf16[8,27,32,128]{3,2,1,0:T(8,128)(2,1)} %broadcast_in_dim.2), calls=%async_computation | async-start | bytes 3538944 | tf_op jit(solution)/shard_map/all_to_all | solution.py:204
  70.4 1.9 %collective-permute-start.1 = (f32[4,32,256]{2,1,0:T(8,128)S(1)}, f32[4,32,256]{2,1,0:T(8,128)S(1)}, u32[]{:S(2)}, u32[]{:S(2)}) collective-permute-start(f32[4,32,256]{2,1,0:T(8,128)S(1)} %get-tuple-element.7), channel_id=1, source_target_pairs={{0,8},{8,16},{16,24},{24,32},{32,40},{40,48},{48,56},{56,64},{64,7... | collective-permute-start | bytes 393224 | tf_op jit(solution)/shard_map/ppermute | solution.py:216
  72.3 1.9 %collective-permute-done.1 = f32[4,32,256]{2,1,0:T(8,128)S(1)} collective-permute-done((f32[4,32,256]{2,1,0:T(8,128)S(1)}, f32[4,32,256]{2,1,0:T(8,128)S(1)}, u32[]{:S(2)}, u32[]{:S(2)}) %collective-permute-start.1) | collective-permute-done | bytes 131104 | tf_op jit(solution)/shard_map/ppermute | solution.py:216
  74.2 0.6 fusion
  74.9 0.8 slice.4
  75.7 18.2 %all-to-all-done.ker_ref = bf16[8,27,32,128]{3,2,1,0:T(8,128)(2,1)S(1)} async-done(((bf16[8,27,32,128]{3,2,1,0:T(8,128)(2,1)}), bf16[8,27,32,128]{3,2,1,0:T(8,128)(2,1)S(1)}, u32[]{:S(2)}, u32[]{:S(2)}) %all-to-all-start) | async-done | bytes 1769504 | tf_op jit(solution)/shard_map/all_to_all | solution.py:204
  93.8 1.5 %input_grad_local.1 = bf16[4,256,128]{2,1,0:T(8,128)(2,1)} custom-call(bf16[8,27,32,128]{3,2,1,0:T(8,128)(2,1)S(1)} %all-to-all-done.ker_ref, bf16[8,4,32,128]{3,2,1,0:T(8,128)(2,1)S(1)} %all-to-all-done.1.g_ref), custom_call_target="tpu_custom_call" | custom-call | flops 2000000000 | bytes 3000000 | tf_op jit(solution)/shard_map/input_grad_local/pallas_call | solution.py:173
  (6 shorter events, 0.0 us)
Async XLA Ops:
  0.6 6.8 %collective-permute-start = (bf16[4,32,256]{2,1,0:T(8,128)(2,1)}, bf16[4,32,256]{2,1,0:T(8,128)(2,1)S(1)}, u32[]{:S(2)}, u32[]{:S(2)}) collective-permute-start(bf16[4,32,256]{2,1,0:T(8,128)(2,1)} %bitcast.17), channel_id=1, source_target_pairs={{8,0},{16,8},{24,16},{32,24},{40,32},{48,40},{56,48},{64,56},{72,6... | collective-permute-start | bytes 196616 | tf_op jit(solution)/shard_map/ppermute | solution.py:211
  7.4 11.3 %copy-start.3 = (bf16[4,32,256]{2,1,0:T(8,128)(2,1)}, bf16[4,32,256]{2,1,0:T(8,128)(2,1)S(1)}, u32[]{:S(2)}) copy-start(bf16[4,32,256]{2,1,0:T(8,128)(2,1)S(1)} %collective-permute-done.gn_ref) | copy-start | bytes 196612
  7.4 1.0 %copy-start = (bf16[3,3,3,32,128]{4,3,2,1,0:T(8,128)(2,1)S(1)}, bf16[3,3,3,32,128]{4,3,2,1,0:T(8,128)(2,1)}, u32[]{:S(2)}) copy-start(bf16[3,3,3,32,128]{4,3,2,1,0:T(8,128)(2,1)} %param.4) | copy-start | bytes 663556
  8.3 0.8 copy-start.2
  9.2 1.6 %copy-start.4 = (bf16[4,128,2,1024]{3,2,1,0:T(2,128)(2,1)S(1)}, bf16[4,128,2,1024]{3,2,1,0:T(2,128)(2,1)}, u32[]{:S(2)}) copy-start(bf16[4,128,2,1024]{3,2,1,0:T(2,128)(2,1)} %param.3) | copy-start | bytes 6291460
  18.7 46.6 %copy-start.1 = (bf16[3,3,3,32,128]{4,3,2,1,0:T(8,128)(2,1)S(1)}, bf16[3,3,3,32,128]{4,3,2,1,0:T(8,128)(2,1)}, u32[]{:S(2)}) copy-start(bf16[3,3,3,32,128]{4,3,2,1,0:T(8,128)(2,1)} %param.4) | copy-start | bytes 663556
  18.7 18.5 %all-to-all-start.2 = ((f32[16,56,128]{2,1,0:T(8,128)}), f32[16,56,128]{2,1,0:T(8,128)S(1)}, u32[]{:S(2)}, u32[]{:S(2)}) async-start(f32[16,56,128]{2,1,0:T(8,128)} %bitcast.8), calls=%async_computation.2 | async-start | bytes 917504 | tf_op jit(solution)/shard_map/all_to_all | solution.py:204
  37.2 5.4 %copy-start.5 = (f32[16,56,128]{2,1,0:T(8,128)}, f32[16,56,128]{2,1,0:T(8,128)S(1)}, u32[]{:S(2)}) copy-start(f32[16,56,128]{2,1,0:T(8,128)S(1)} %all-to-all-done.2.parts_ref) | copy-start | bytes 1376260
  37.2 11.7 %all-to-all-start.1 = ((bf16[8,4,32,128]{3,2,1,0:T(8,128)(2,1)}), bf16[8,4,32,128]{3,2,1,0:T(8,128)(2,1)S(1)}, u32[]{:S(2)}, u32[]{:S(2)}) async-start(bf16[8,4,32,128]{3,2,1,0:T(8,128)(2,1)} %spread.1), calls=%async_computation.1 | async-start | bytes 524288 | tf_op jit(solution)/shard_map/all_to_all | solution.py:204
  66.8 27.1 %all-to-all-start = ((bf16[8,27,32,128]{3,2,1,0:T(8,128)(2,1)}), bf16[8,27,32,128]{3,2,1,0:T(8,128)(2,1)S(1)}, u32[]{:S(2)}, u32[]{:S(2)}) async-start(bf16[8,27,32,128]{3,2,1,0:T(8,128)(2,1)} %broadcast_in_dim.2), calls=%async_computation | async-start | bytes 3538944 | tf_op jit(solution)/shard_map/all_to_all | solution.py:204
  70.4 3.9 %collective-permute-start.1 = (f32[4,32,256]{2,1,0:T(8,128)S(1)}, f32[4,32,256]{2,1,0:T(8,128)S(1)}, u32[]{:S(2)}, u32[]{:S(2)}) collective-permute-start(f32[4,32,256]{2,1,0:T(8,128)S(1)} %get-tuple-element.7), channel_id=1, source_target_pairs={{0,8},{8,16},{16,24},{24,32},{32,40},{40,48},{48,56},{56,64},{64,7... | collective-permute-start | bytes 393224 | tf_op jit(solution)/shard_map/ppermute | solution.py:216

commit v2 on v1

--- a/solution.py
+++ b/solution.py
@@ -12,6 +12,8 @@
 F32 = jnp.float32
 BF16 = jnp.bfloat16
 NT = (((1,), (1,)), ((), ()))
+TAPS = 14
+PACKED = TAPS * 32 + 64
 ROWS = 896
 
 
@@ -107,43 +109,52 @@
     )(vol, ker, g, gn)
 
 
-def spread_kernel(g_ref, gn_ref, out_ref):
+def pack_kernel(ker_ref, g_ref, out_ref):
+    core = lax.rem(lax.axis_index("space"), 2)
+    half = ker_ref[pl.ds(core * 13, TAPS)].reshape(TAPS * 32, CIN)
+    for f in range(8):
+        out_ref[f, :TAPS * 32] = half
     for b in range(B):
+        whole = jnp.concatenate([g_ref[b], jnp.zeros((32, 128), BF16)], 1)
+        start, lane = TAPS * 32 + (b // 2) * 32, (b % 2) * 64
         for f in range(8):
-            parts = []
-            for ref in (g_ref, gn_ref):
-                whole = jnp.concatenate([ref[b], jnp.zeros((32, 128), BF16)], 1)
-                parts.append(whole[:, 32 * f:32 * f + 64])
-            out_ref[f, b] = jnp.concatenate(parts, 1)
-
-
-def spread(g, gn):
-    return pl.pallas_call(
-        spread_kernel,
-        out_shape=jax.ShapeDtypeStruct((8, B, 32, 128), BF16),
-        name="spread",
-    )(g, gn)
-
-
-def input_grad_kernel(ker_ref, g_ref, out_ref, grads, mixed, paired):
+            out_ref[f, start:start + 32, lane:lane + 64] = whole[:, 32 * f:32 * f + 64]
+
+
+def pack(ker, g):
+    return pl.pallas_call(
+        pack_kernel,
+        out_shape=jax.ShapeDtypeStruct((8, PACKED, 128), BF16),
+        name="pack",
+    )(ker, g)
+
+
+def input_grad_kernel(mine_ref, other_ref, next_ref, out_ref, halves, grads, mixed, paired):
+    core = lax.rem(lax.axis_index("space"), 2)
+    halves[core] = mine_ref[:, :TAPS * 32]
+    halves[1 - core] = other_ref[:, :TAPS * 32]
     last = (iota((128, 256), 0) & 15) == 15
-    for b in range(B):
-        block = g_ref[:, b].reshape(256, 128).astype(F32)
-        turned = jnp.transpose(block)
-        later = jnp.where(last, 0.0, pltpu.roll(turned, 127, 0))
-        for shift, value in enumerate((turned, later)):
-            low = value.astype(BF16)
-            for p in range(2):
-                for q in range(3):
-                    start = p * 64 + q * 16
-                    grads[p, shift, q, b] = low[start:start + 16]
+    for p, (ref, first) in enumerate(((mine_ref, TAPS * 32), (next_ref, 0))):
+        for two in range(B // 2):
+            start = first + two * 32
+            block = ref[:, start:start + 32].reshape(256, 128).astype(F32)
+            turned = jnp.transpose(block)
+            later = jnp.where(last, 0.0, pltpu.roll(turned, 127, 0))
+            for shift, value in enumerate((turned, later)):
+                low = value.astype(BF16)
+                for b in range(2):
+                    for q in range(3):
+                        start = b * 64 + q * 16
+                        grads[p, shift, q, 2 * two + b] = low[start:start + 16]
 
     def lhs(p, qs, rs):
         rows = [grads[p, rs, qs + q, b] for q in range(2) for b in range(B)]
         return jnp.concatenate(rows, 0)
 
     def tap(i, j, k):
-        return ker_ref[:, i * 9 + j * 3 + k].reshape(256, CIN)
+        t = i * 9 + j * 3 + k
+        half, place = (0, t) if t < TAPS else (1, t - 13)
+        return halves[half, :, place * 32:place * 32 + 32].reshape(256, CIN)
 
     choices = (((1, 0),), ((2, 0), (0, 1)))
     for py in range(2):
@@ -169,11 +180,12 @@
         out_ref[b] = paired[b].astype(BF16)
 
 
-def input_grad_local(ker_all, g_all):
+def input_grad_local(mine, other, following):
     return pl.pallas_call(
         input_grad_kernel,
         out_shape=jax.ShapeDtypeStruct((B, 2 * CIN, 128), BF16),
         scratch_shapes=[
+            pltpu.VMEM((2, 8, TAPS * 32, CIN), BF16),
             pltpu.VMEM((2, 2, 3, B, HALF, 256), BF16),
             pltpu.VMEM((2, B, 128, CIN), F32),
             pltpu.VMEM((B, 2 * CIN, 128), F32),
@@ -181,7 +193,7 @@
         compiler_params=pltpu.CompilerParams(vmem_limit_bytes=40 * 1024 * 1024),
         cost_estimate=pl.CostEstimate(flops=2_000_000_000, bytes_accessed=3_000_000, transcendentals=0),
         name="input_grad_local",
-    )(ker_all, g_all)
+    )(mine, other, following)
 
 
 def sum_kernel(parts_ref, out_ref):
@@ -189,13 +201,13 @@
     for i in range(1, 16):
         total = total + parts_ref[i]
     for i in range(16):
-        out_ref[i] = total
+        out_ref[i] = total.astype(BF16)
 
 
 def sum_and_copy(parts):
     return pl.pallas_call(
         sum_kernel,
-        out_shape=jax.ShapeDtypeStruct(parts.shape, parts.dtype),
+        out_shape=jax.ShapeDtypeStruct(parts.shape, BF16),
         name="sum_and_copy",
     )(parts)
 
@@ -208,17 +220,22 @@
     spaces = lax.axis_size("space")
     g = out_grad.reshape(B, 32, 256)
     ker = kernel.reshape(27, 32, CIN)
-    g_next = lax.ppermute(g, "space", [(i + 1, i) for i in range(spaces - 1)])
-    ker_all = swap(jnp.broadcast_to(ker[None], (8, 27, 32, CIN)), "filt")
-    g_all = swap(spread(g, g_next), "filt")
+    to_previous = [(i + 1, i) for i in range(spaces - 1)]
+    to_next = [(i, i + 1) for i in range(spaces - 1)]
+    to_other_core = [(i, i ^ 1) for i in range(spaces)]
+    g_next = lax.ppermute(g, "space", to_previous)
+    mine = swap(pack(ker, g), "filt")
     vol = volume.reshape(B, CIN, 2, 8, 128).transpose(0, 1, 3, 2, 4).reshape(B, 2048, 128)
     own, send, dw = conv_local(vol, ker, g, g_next)
-    came = lax.ppermute(send, "space", [(i, i + 1) for i in range(spaces - 1)])
+    dw, mine = lax.optimization_barrier((dw, mine))
+    came = lax.ppermute(send, "space", to_next)
+    other = lax.ppermute(mine, "space", to_other_core)
+    following = lax.ppermute(mine[:, TAPS * 32:], "space", to_previous)
     dw_mine = sum_and_copy(swap(dw.reshape(16, 56, CIN), "space"))
     dw_all = swap(dw_mine, "space").reshape(ROWS, CIN)
     output = (own + came).astype(BF16).reshape(B, 32, 1, 256)
-    input_grad = input_grad_local(ker_all, g_all).reshape(B, CIN, 2, 128)
-    kernel_grad = dw_all[:864].reshape(3, 3, 3, 32, CIN)
+    input_grad = input_grad_local(mine, other, following).reshape(B, CIN, 2, 128)
+    kernel_grad = dw_all[:864].astype(F32).reshape(3, 3, 3, 32, CIN)
     return (output, input_grad, kernel_grad)
 
 

time: 96.4 us -> 62.4 us (0.65)
  waiting for transfers between devices: 36.7 us -> 16.2 us
  blocking collectives: 16.4 us -> 0 us
  starting transfers between devices: 22.3 us -> 27.4 us
  local copies, waits for them, and re-layouts: 5.66 us -> 2.4 us
    all_to_all x3, waiting for transfers between devices: 31.3 us -> 12.8 us  [swap(): return lax.all_to_all(values, axis, split_axis=0, concat_axis=0, tiled=True)]
    all_to_all x1 -> x0, blocking collectives: 16.4 us -> none  [swap(): return lax.all_to_all(values, axis, split_axis=0, concat_axis=0, tiled=True)]
    ppermute x2 -> x4, starting transfers between devices: 5.25 us -> 9.14 us  [the longest x1 3.53 us: body(): came = lax.ppermute(send, 'space', to_next)]
    ppermute x2 -> x4, waiting for transfers between devices: 5.34 us -> 3.42 us  [the longest x1 3.41 us: body(): g_next = lax.ppermute(g, 'space', to_previous)]
    broadcast_in_dim x1 -> x0, local copies, waits for them, and re-layouts: 1.47 us -> none  [body(): ker_all = swap(jnp.broadcast_to(ker[None], (8, 27, 32, CIN)), 'filt')]
    all_to_all x3, starting transfers between devices: 17 us -> 18.3 us  [swap(): return lax.all_to_all(values, axis, split_axis=0, concat_axis=0, tiled=True)]
    unnamed x12 -> x8, local copies, waits for them, and re-layouts: 3.4 us -> 2.37 us
  transfers between devices with their start and end apart: 5 -> 7, of which waited for: 5 -> 3; matrix products, arithmetic and copies ran while one was open for 2% -> 2% of each run, Pallas kernels for 4% -> 16%
where the time goes in v2:
time: 62.4 us; the launch traced here: 61.9 us
  starting transfers between devices  27.4 us (44%)
  waiting for transfers between devices  16.2 us (26%)
  Pallas kernels  13.6 us (22%)
  local copies, waits for them, and re-layouts  2.4 us (4%)
  other arithmetic  1.46 us (2%)
  between operations  0.7 us (1%)
    all_to_all x3, starting transfers between devices, swap(): return lax.all_to_all(values, axis, split_axis=0, concat_axis=0, tiled=True)  18.3 us
    all_to_all x3, waiting for transfers between devices, swap(): return lax.all_to_all(values, axis, split_axis=0, concat_axis=0, tiled=True)  12.8 us
    pallas_call x1, Pallas kernels, conv_local(): pl.pallas_call(conv_kernel, grid=(B,), in_specs=[per_sample(2048, 128), w...  7.94 us
    ppermute x1, starting transfers between devices, body(): came = lax.ppermute(send, 'space', to_next)  3.53 us
    ppermute x1, waiting for transfers between devices, body(): g_next = lax.ppermute(g, 'space', to_previous)  3.41 us
    ppermute x1, starting transfers between devices, body(): g_next = lax.ppermute(g, 'space', to_previous)  2.86 us
    unnamed x8, local copies, waits for them, and re-layouts  2.37 us
    pallas_call x1, Pallas kernels, pack(): pl.pallas_call(pack_kernel, out_shape=jax.ShapeDtypeStruct((8, PACKED, 12...  2.2 us
  transfers between devices with their start and end apart: 7, of which 3 were waited for; matrix products, arithmetic and copies ran while one was open for 2% of the time, Pallas kernels for 16%

profile of v2, /device:TPU:1, one launch (start us, length us, event | category | flops | bytes accessed | tf_op | source)
XLA Modules:
  0.0 61.9 jit_solution(9306421457288490082)
XLA Ops:
  0.6 0.0 copy-start.1
  0.6 0.0 copy-start
  0.7 2.2 %pack.1 = bf16[8,512,128]{2,1,0:T(8,128)(2,1)} custom-call(bf16[27,32,128]{2,1,0:T(8,128)(2,1)} %bitcast.16, bf16[4,32,256]{2,1,0:T(8,128)(2,1)} %bitcast.18), custom_call_target="tpu_custom_call" | custom-call | tf_op jit(solution)/shard_map/pack/pallas_call | solution.py:125
  2.9 6.2 %all-to-all-start = ((bf16[8,512,128]{2,1,0:T(8,128)(2,1)}), bf16[8,512,128]{2,1,0:T(8,128)(2,1)S(1)}, u32[]{:S(2)}, u32[]{:S(2)}) async-start(bf16[8,512,128]{2,1,0:T(8,128)(2,1)} %pack.1), calls=%async_computation | async-start | bytes 2097152 | tf_op jit(solution)/shard_map/all_to_all | solution.py:216
  9.1 2.9 %collective-permute-start = (bf16[4,32,256]{2,1,0:T(8,128)(2,1)S(1)}, bf16[4,32,256]{2,1,0:T(8,128)(2,1)S(1)}, u32[]{:S(2)}, u32[]{:S(2)}) collective-permute-start(bf16[4,32,256]{2,1,0:T(8,128)(2,1)S(1)} %bitcast.19), channel_id=1, source_target_pairs={{8,0},{16,8},{24,16},{32,24},{40,32},{48,40},{56,48},{64,56},{72,6... | collective-permute-start | bytes 196616 | tf_op jit(solution)/shard_map/ppermute | solution.py:226
  11.9 3.4 %collective-permute-done.gn_ref = bf16[4,32,256]{2,1,0:T(8,128)(2,1)S(1)} collective-permute-done((bf16[4,32,256]{2,1,0:T(8,128)(2,1)S(1)}, bf16[4,32,256]{2,1,0:T(8,128)(2,1)S(1)}, u32[]{:S(2)}, u32[]{:S(2)}) %collective-permute-start) | collective-permute-done | bytes 65568 | tf_op jit(solution)/shard_map/ppermute | solution.py:226
  15.4 1.6 %copy-done.2 = bf16[4,128,2,1024]{3,2,1,0:T(2,128)(2,1)S(1)} copy-done((bf16[4,128,2,1024]{3,2,1,0:T(2,128)(2,1)S(1)}, bf16[4,128,2,1024]{3,2,1,0:T(2,128)(2,1)}, u32[]{:S(2)}) %copy-start.2) | copy-done | bytes 2097176
  16.9 7.9 %conv_local.1 = (f32[4,32,256]{2,1,0:T(8,128)S(1)}, f32[4,32,256]{2,1,0:T(8,128)S(1)}, f32[896,128]{1,0:T(8,128)}) custom-call(bf16[4,2048,128]{2,1,0:T(8,128)(2,1)S(1)} %bitcast.21, bf16[27,32,128]{2,1,0:T(8,128)(2,1)S(1)} %bitcast.17, bf16[4,32,256]{2,1,0:T(8,128)(2,1)S(1)} %bitcast.20, bf16[4,32,256]{2,1,0:T(8,128)(2,1)S(1)} %collective-permute-done.gn_ref), custom_call_target="tpu_custom_call" | custom-call | flops 6000000000 | bytes 4000000 | tf_op jit(solution)/shard_map/conv_local/pallas_call | solution.py:90
  24.9 0.0 all-to-all-done.mine_ref
  24.9 0.8 %collective-permute-start.2 = (bf16[8,512,128]{2,1,0:T(8,128)(2,1)S(1)}, bf16[8,512,128]{2,1,0:T(8,128)(2,1)S(1)}, u32[]{:S(2)}, u32[]{:S(2)}) collective-permute-start(bf16[8,512,128]{2,1,0:T(8,128)(2,1)S(1)} %all-to-all-done.mine_ref), channel_id=1, source_target_pairs={{0,8},{8,0},{16,24},{24,16},{32,40},{40,32},{48,56},{56,48},{64,72... | collective-permute-start | bytes 3145736 | tf_op jit(solution)/shard_map/ppermute | solution.py:232
  25.7 7.6 %all-to-all-start.1 = ((f32[16,56,128]{2,1,0:T(8,128)}), f32[16,56,128]{2,1,0:T(8,128)S(1)}, u32[]{:S(2)}, u32[]{:S(2)}) async-start(f32[16,56,128]{2,1,0:T(8,128)} %bitcast.8), calls=%async_computation.1 | async-start | bytes 917504 | tf_op jit(solution)/shard_map/all_to_all | solution.py:216
  33.3 3.5 %collective-permute-start.1 = (f32[4,32,256]{2,1,0:T(8,128)S(1)}, f32[4,32,256]{2,1,0:T(8,128)S(1)}, u32[]{:S(2)}, u32[]{:S(2)}) collective-permute-start(f32[4,32,256]{2,1,0:T(8,128)S(1)} %get-tuple-element.9), channel_id=1, source_target_pairs={{0,8},{8,16},{16,24},{24,32},{32,40},{40,48},{48,56},{56,64},{64,7... | collective-permute-start | bytes 393224 | tf_op jit(solution)/shard_map/ppermute | solution.py:231
  36.9 1.9 %collective-permute-start.3 = (bf16[8,64,128]{2,1,0:T(8,128)(2,1)S(1)}, bf16[8,64,128]{2,1,0:T(8,128)(2,1)S(1)}, u32[]{:S(2)}, u32[]{:S(2)}) collective-permute-start(bf16[8,64,128]{2,1,0:T(8,128)(2,1)S(1)} %slice.6), channel_id=1, source_target_pairs={{8,0},{16,8},{24,16},{32,24},{40,32},{48,40},{56,48},{64,56},{72,6... | collective-permute-start | bytes 393224 | tf_op jit(solution)/shard_map/ppermute | solution.py:233
  38.8 5.0 %all-to-all-done.1.parts_ref = f32[16,56,128]{2,1,0:T(8,128)S(1)} async-done(((f32[16,56,128]{2,1,0:T(8,128)}), f32[16,56,128]{2,1,0:T(8,128)S(1)}, u32[]{:S(2)}, u32[]{:S(2)}) %all-to-all-start.1) | async-done | bytes 458784 | tf_op jit(solution)/shard_map/all_to_all | solution.py:216
  43.8 0.8 %copy-done.3 = f32[16,56,128]{2,1,0:T(8,128)} copy-done((f32[16,56,128]{2,1,0:T(8,128)}, f32[16,56,128]{2,1,0:T(8,128)S(1)}, u32[]{:S(2)}) %copy-start.3) | copy-done | bytes 458776
  44.5 1.7 %sum_and_copy.1 = bf16[16,56,128]{2,1,0:T(8,128)(2,1)} custom-call(f32[16,56,128]{2,1,0:T(8,128)} %copy-done.3), custom_call_target="tpu_custom_call" | custom-call | tf_op jit(solution)/shard_map/sum_and_copy/pallas_call | solution.py:208
  46.3 4.5 %all-to-all-start.2 = ((bf16[16,56,128]{2,1,0:T(8,128)(2,1)}), bf16[16,56,128]{2,1,0:T(8,128)(2,1)S(1)}, u32[]{:S(2)}, u32[]{:S(2)}) async-start(bf16[16,56,128]{2,1,0:T(8,128)(2,1)} %sum_and_copy.1), calls=%async_computation.2 | async-start | bytes 458752 | tf_op jit(solution)/shard_map/all_to_all | solution.py:216
  50.8 0.0 collective-permute-done.1
  50.8 0.6 %fusion = bf16[4,32,1,256]{3,1,2,0:T(8,128)(2,1)} fusion(f32[4,32,256]{2,1,0:T(8,128)S(1)} %get-tuple-element.8, f32[4,32,256]{2,1,0:T(8,128)S(1)} %collective-permute-done.1), kind=kLoop, calls=%fused_computation.1 | loop fusion | flops 65536 | bytes 327680
  51.4 7.9 %all-to-all-done.2 = bf16[16,56,128]{2,1,0:T(8,128)(2,1)S(1)} async-done(((bf16[16,56,128]{2,1,0:T(8,128)(2,1)}), bf16[16,56,128]{2,1,0:T(8,128)(2,1)S(1)}, u32[]{:S(2)}, u32[]{:S(2)}) %all-to-all-start.2) | async-done | bytes 229408 | tf_op jit(solution)/shard_map/all_to_all | solution.py:216
  59.3 0.8 %convert.1 = f32[3,3,3,32,128]{4,3,2,1,0:T(8,128)} convert(bf16[3,3,3,32,128]{4,3,2,1,0:T(8,128)(2,1)S(1)} %bitcast.23) | non-fusion elementwise | flops 110592 | bytes 663552 | tf_op jit(solution)/shard_map/reshape | solution.py:238
  60.1 0.0 collective-permute-done.3.next_ref
  60.1 0.0 collective-permute-done.2.other_ref
  60.1 1.8 %input_grad_local.1 = bf16[4,256,128]{2,1,0:T(8,128)(2,1)} custom-call(bf16[8,512,128]{2,1,0:T(8,128)(2,1)S(1)} %all-to-all-done.mine_ref, bf16[8,512,128]{2,1,0:T(8,128)(2,1)S(1)} %collective-permute-done.2.other_ref, bf16[8,64,128]{2,1,0:T(8,128)(2,1)S(1)} %collective-permute-done.3.next_ref), custom_call_target="tpu_custom_call" | custom-call | flops 2000000000 | bytes 3000000 | tf_op jit(solution)/shard_map/input_grad_local/pallas_call | solution.py:184
  (6 shorter events, 0.0 us)
Async XLA Ops:
  0.6 8.4 %copy-start.1 = (bf16[4,32,1,256]{3,1,2,0:T(8,128)(2,1)S(1)}, bf16[4,32,1,256]{3,1,2,0:T(8,128)(2,1)}, u32[]{:S(2)}) copy-start(bf16[4,32,1,256]{3,1,2,0:T(8,128)(2,1)} %param.5) | copy-start | bytes 196612
  0.6 14.7 %copy-start = (bf16[3,3,3,32,128]{4,3,2,1,0:T(8,128)(2,1)S(1)}, bf16[3,3,3,32,128]{4,3,2,1,0:T(8,128)(2,1)}, u32[]{:S(2)}) copy-start(bf16[3,3,3,32,128]{4,3,2,1,0:T(8,128)(2,1)} %param.4) | copy-start | bytes 663556
  2.9 22.0 %all-to-all-start = ((bf16[8,512,128]{2,1,0:T(8,128)(2,1)}), bf16[8,512,128]{2,1,0:T(8,128)(2,1)S(1)}, u32[]{:S(2)}, u32[]{:S(2)}) async-start(bf16[8,512,128]{2,1,0:T(8,128)(2,1)} %pack.1), calls=%async_computation | async-start | bytes 2097152 | tf_op jit(solution)/shard_map/all_to_all | solution.py:216
  9.1 6.3 %collective-permute-start = (bf16[4,32,256]{2,1,0:T(8,128)(2,1)S(1)}, bf16[4,32,256]{2,1,0:T(8,128)(2,1)S(1)}, u32[]{:S(2)}, u32[]{:S(2)}) collective-permute-start(bf16[4,32,256]{2,1,0:T(8,128)(2,1)S(1)} %bitcast.19), channel_id=1, source_target_pairs={{8,0},{16,8},{24,16},{32,24},{40,32},{48,40},{56,48},{64,56},{72,6... | collective-permute-start | bytes 196616 | tf_op jit(solution)/shard_map/ppermute | solution.py:226
  15.3 1.6 %copy-start.2 = (bf16[4,128,2,1024]{3,2,1,0:T(2,128)(2,1)S(1)}, bf16[4,128,2,1024]{3,2,1,0:T(2,128)(2,1)}, u32[]{:S(2)}) copy-start(bf16[4,128,2,1024]{3,2,1,0:T(2,128)(2,1)} %param.3) | copy-start | bytes 6291460
  24.9 35.2 %collective-permute-start.2 = (bf16[8,512,128]{2,1,0:T(8,128)(2,1)S(1)}, bf16[8,512,128]{2,1,0:T(8,128)(2,1)S(1)}, u32[]{:S(2)}, u32[]{:S(2)}) collective-permute-start(bf16[8,512,128]{2,1,0:T(8,128)(2,1)S(1)} %all-to-all-done.mine_ref), channel_id=1, source_target_pairs={{0,8},{8,0},{16,24},{24,16},{32,40},{40,32},{48,56},{56,48},{64,72... | collective-permute-start | bytes 3145736 | tf_op jit(solution)/shard_map/ppermute | solution.py:232
  25.7 18.1 %all-to-all-start.1 = ((f32[16,56,128]{2,1,0:T(8,128)}), f32[16,56,128]{2,1,0:T(8,128)S(1)}, u32[]{:S(2)}, u32[]{:S(2)}) async-start(f32[16,56,128]{2,1,0:T(8,128)} %bitcast.8), calls=%async_computation.1 | async-start | bytes 917504 | tf_op jit(solution)/shard_map/all_to_all | solution.py:216
  33.3 17.4 %collective-permute-start.1 = (f32[4,32,256]{2,1,0:T(8,128)S(1)}, f32[4,32,256]{2,1,0:T(8,128)S(1)}, u32[]{:S(2)}, u32[]{:S(2)}) collective-permute-start(f32[4,32,256]{2,1,0:T(8,128)S(1)} %get-tuple-element.9), channel_id=1, source_target_pairs={{0,8},{8,16},{16,24},{24,32},{32,40},{40,48},{48,56},{56,64},{64,7... | collective-permute-start | bytes 393224 | tf_op jit(solution)/shard_map/ppermute | solution.py:231
  36.9 23.2 %collective-permute-start.3 = (bf16[8,64,128]{2,1,0:T(8,128)(2,1)S(1)}, bf16[8,64,128]{2,1,0:T(8,128)(2,1)S(1)}, u32[]{:S(2)}, u32[]{:S(2)}) collective-permute-start(bf16[8,64,128]{2,1,0:T(8,128)(2,1)S(1)} %slice.6), channel_id=1, source_target_pairs={{8,0},{16,8},{24,16},{32,24},{40,32},{48,40},{56,48},{64,56},{72,6... | collective-permute-start | bytes 393224 | tf_op jit(solution)/shard_map/ppermute | solution.py:233
  43.8 0.8 %copy-start.3 = (f32[16,56,128]{2,1,0:T(8,128)}, f32[16,56,128]{2,1,0:T(8,128)S(1)}, u32[]{:S(2)}) copy-start(f32[16,56,128]{2,1,0:T(8,128)S(1)} %all-to-all-done.1.parts_ref) | copy-start | bytes 1376260
  46.3 13.0 %all-to-all-start.2 = ((bf16[16,56,128]{2,1,0:T(8,128)(2,1)}), bf16[16,56,128]{2,1,0:T(8,128)(2,1)S(1)}, u32[]{:S(2)}, u32[]{:S(2)}) async-start(bf16[16,56,128]{2,1,0:T(8,128)(2,1)} %sum_and_copy.1), calls=%async_computation.2 | async-start | bytes 458752 | tf_op jit(solution)/shard_map/all_to_all | solution.py:216

commit v3 on v2

v3 whole, which is shorter than its diff:
```python
import jax
import jax.numpy as jnp
from jax import lax
from jax.experimental import pallas as pl
from jax.experimental.pallas import tpu as pltpu
from jax.sharding import PartitionSpec as P

B = 4
CIN = 128
EDGE = 32
HALF = 16
F32 = jnp.float32
BF16 = jnp.bfloat16
NT = (((1,), (1,)), ((), ()))
FULL = 63_000_000
TAPS = 14
PACKED = TAPS + 2
ROWS = 896
OWN = 56


def iota(shape, axis):
    return lax.broadcasted_iota(jnp.int32, shape, axis)


def columns(plane):
    parts = []
    for j in range(3):
        for k in range(3):
            parts.append(jnp.concatenate([plane(k, 2 * q + j) for q in range(HALF)], 0))
    return jnp.concatenate(parts, 1)


def conv_kernel(vol_ref, ker_ref, g_ref, own_ref, send_ref, dw_ref, odd_ref,
                total, raw, arrived, ker_in, grads_in, perm, select, planes, cols):
    step = pl.program_id(0)

    def fetch(b):
        return pltpu.make_async_copy(vol_ref.at[b], raw.at[b], arrived.at[b])

    others = [
        pltpu.make_async_copy(ker_ref, ker_in, arrived.at[B]),
        pltpu.make_async_copy(g_ref, grads_in, arrived.at[B + 1]),
    ]

    @pl.when(step == 0)
    def _():
        fetch(0).start()
        for copy in others:
            copy.start()
        for b in range(1, B):
            fetch(b).start()

    @pl.when(step == 0)
    def _():
        row, col = iota((256, 256), 0), iota((256, 256), 1)
        source = (row & 15) * 16 + ((row >> 4) & 7) * 2 + (row >> 7)
        perm[...] = jnp.where(col == source, 1.0, 0.0).astype(BF16)
        row, col = iota((192, 128), 0), iota((192, 128), 1)
        depth = (row & 15) * 2 + (row >> 6) - 1
        wanted = (col == ((row >> 4) & 3) * 32 + depth) & (depth >= 0)
        select[...] = jnp.where(wanted, 1.0, 0.0).astype(BF16)
        total[...] = jnp.zeros_like(total)
        dw_ref[...] = jnp.zeros_like(dw_ref)
        for k in range(3):
            planes[k, 0] = jnp.zeros((HALF, CIN), BF16)

    fetch(step).wait()
    wide = jnp.concatenate([raw[step, g * 256:(g + 1) * 256] for g in range(8)], 1)
    moved = jnp.dot(perm[...], wide, preferred_element_type=F32).astype(BF16)
    for lt in range(8):
        for x in range(2):
            start = (x * 8 + lt) * 16
            for g in range(8):
                cols[lt, x * 128 + g * 16:x * 128 + g * 16 + 16, :] = (
                    moved[start:start + 16, g * 128:(g + 1) * 128]
                )
    for k in range(3):
        odd_ref[0, k, 0] = jnp.zeros((HALF, CIN), BF16)
    for lt in range(8):
        turned = lax.dot_general(select[...], cols[lt], NT, preferred_element_type=F32).astype(BF16)
        for k in range(3):
            for y in range(4):
                start = k * 64 + y * 16
                planes[k, 1 + 4 * lt + y] = turned[start:start + 16, :128]
                odd_ref[0, k, 1 + 4 * lt + y] = turned[start:start + 16, 128:]

    @pl.when(step == 0)
    def _():
        for copy in others:
            copy.wait()

    def weights(i):
        return jnp.concatenate([ker_in[i * 9 + t] for t in range(9)], 1)

    grad = grads_in[step]
    even = columns(lambda k, y: planes[k, y])
    here = lax.dot_general(weights(1), even, NT, preferred_element_type=F32)
    back_even = jnp.dot(grad, even, preferred_element_type=F32)
    odd = columns(lambda k, y: odd_ref[0, k, y])
    both = lax.dot_general(
        jnp.concatenate([weights(2), weights(0)], 0), odd, NT, preferred_element_type=F32
    )
    back_odd = jnp.dot(grad, odd, preferred_element_type=F32)
    own_ref[0] = here + both[:32]
    send_ref[0] = both[32:]
    for t in range(9):
        lanes = slice(t * 128, (t + 1) * 128)
        total[t * 32:(t + 1) * 32] += back_even[:, lanes]
        total[(9 + t) * 32:(10 + t) * 32] += back_odd[:, lanes]

    @pl.when(step == B - 1)
    def _():
        dw_ref[288:864] = total[...].astype(BF16)


def conv_local(vol, ker, g):
    per_sample = lambda *shape: pl.BlockSpec((1,) + shape, lambda b: (b,) + (0,) * len(shape))
    whole = lambda *shape: pl.BlockSpec(shape, lambda b: (0,) * len(shape))
    return pl.pallas_call(
        conv_kernel,
        grid=(B,),
        in_specs=[pl.BlockSpec(memory_space=pltpu.HBM)] * 3,
        out_specs=[per_sample(32, 256), per_sample(32, 256), whole(ROWS, CIN), per_sample(3, EDGE + 1, HALF, CIN)],
        out_shape=[
            jax.ShapeDtypeStruct((B, 32, 256), F32),
            jax.ShapeDtypeStruct((B, 32, 256), F32),
            jax.ShapeDtypeStruct((ROWS, CIN), BF16),
            jax.ShapeDtypeStruct((B, 3, EDGE + 1, HALF, CIN), BF16),
        ],
        scratch_shapes=[
            pltpu.VMEM((576, CIN), F32),
            pltpu.VMEM((B, 2048, 128), BF16),
            pltpu.SemaphoreType.DMA((B + 2,)),
            pltpu.VMEM((27, 32, CIN), BF16),
            pltpu.VMEM((B, 32, 256), BF16),
            pltpu.VMEM((256, 256), BF16),
            pltpu.VMEM((192, 128), BF16),
            pltpu.VMEM((3, EDGE + 1, HALF, CIN), BF16),
            pltpu.VMEM((8, 256, 128), BF16),
        ],
        compiler_params=pltpu.CompilerParams(vmem_limit_bytes=FULL),
        cost_estimate=pl.CostEstimate(flops=6_000_000_000, bytes_accessed=4_000_000, transcendentals=0),
        name="conv_local",
    )(vol, ker, g)


def next_kernel(odd_ref, gn_ref, _, dw_ref, odd, grad, low, arrived):
    copies = [pltpu.make_async_copy(gn_ref, grad, arrived.at[B])]
    for b in range(B):
        copies.append(pltpu.make_async_copy(odd_ref.at[b], odd.at[b], arrived.at[b]))
    for copy in copies:
        copy.start()
    copies[0].wait()
    total = None
    for b in range(B):
        copies[1 + b].wait()
        back = jnp.dot(
            grad[b], columns(lambda k, y: odd[b, k, y]), preferred_element_type=F32
        )
        total = back if total is None else total + back
    for t in range(9):
        low[t * 32:(t + 1) * 32] = total[:, t * 128:(t + 1) * 128].astype(BF16)
    last = pltpu.make_async_copy(low, dw_ref.at[pl.ds(0, 288)], arrived.at[B + 1])
    last.start()
    last.wait()


def next_local(odd, gn, dw):
    return pl.pallas_call(
        next_kernel,
        in_specs=[pl.BlockSpec(memory_space=pltpu.HBM)] * 3,
        out_specs=pl.BlockSpec(memory_space=pltpu.HBM),
        out_shape=jax.ShapeDtypeStruct((ROWS, CIN), BF16),
        scratch_shapes=[
            pltpu.VMEM((B, 3, EDGE + 1, HALF, CIN), BF16),
            pltpu.VMEM((B, 32, 256), BF16),
            pltpu.VMEM((288, CIN), BF16),
            pltpu.SemaphoreType.DMA((B + 2,)),
        ],
        input_output_aliases={2: 0},
        compiler_params=pltpu.CompilerParams(vmem_limit_bytes=FULL),
        cost_estimate=pl.CostEstimate(flops=1_000_000_000, bytes_accessed=2_000_000, transcendentals=0),
        name="next_local",
    )(odd, gn, dw)


def pack_kernel(ker_ref, g_ref, out_ref, half, grad, cells, sent):
    core = lax.rem(lax.axis_index("space"), 2)
    fetch_half = pltpu.make_async_copy(ker_ref.at[pl.ds(core * 13, TAPS)], half, sent.at[8])
    fetch_grad = pltpu.make_async_copy(g_ref, grad, sent.at[9])
    fetch_half.start()
    fetch_grad.start()
    fetch_half.wait()
    copies = [
        pltpu.make_async_copy(half, out_ref.at[f, pl.ds(0, TAPS)], sent.at[f])
        for f in range(8)
    ]
    for copy in copies:
        copy.start()
    fetch_grad.wait()
    for b in range(B):
        whole = jnp.concatenate([grad[b], jnp.zeros((32, 128), BF16)], 1)
        lane = (b % 2) * 64
        for f in range(8):
            cells[f, b // 2, :, lane:lane + 64] = whole[:, 32 * f:32 * f + 64]
    last = pltpu.make_async_copy(cells, out_ref.at[:, pl.ds(TAPS, 2)], sent.at[10])
    last.start()
    for copy in copies:
        copy.wait()
    last.wait()


def pack(ker, g):
    return pl.pallas_call(
        pack_kernel,
        in_specs=[pl.BlockSpec(memory_space=pltpu.HBM)] * 2,
        out_specs=pl.BlockSpec(memory_space=pltpu.HBM),
        out_shape=jax.ShapeDtypeStruct((8, PACKED, 32, 128), BF16),
        scratch_shapes=[
            pltpu.VMEM((TAPS, 32, CIN), BF16),
            pltpu.VMEM((B, 32, 256), BF16),
            pltpu.VMEM((8, 2, 32, 128), BF16),
            pltpu.SemaphoreType.DMA((11,)),
        ],
        compiler_params=pltpu.CompilerParams(vmem_limit_bytes=FULL),
        name="pack",
    )(ker, g)


def input_grad_kernel(mine_ref, other_ref, next_ref, out_ref, halves, grads, mixed, paired):
    core = lax.rem(lax.axis_index("space"), 2)
    halves[core] = mine_ref[:, :TAPS]
    halves[1 - core] = other_ref[:, :TAPS]
    last = (iota((128, 256), 0) & 15) == 15
    for p, (ref, first) in enumerate(((mine_ref, TAPS), (next_ref, 0))):
        for two in range(B // 2):
            block = ref[:, first + two].reshape(256, 128).astype(F32)
            turned = jnp.transpose(block)
            later = jnp.where(last, 0.0, pltpu.roll(turned, 127, 0))
            for shift, value in enumerate((turned, later)):
                low = value.astype(BF16)
                for b in range(2):
                    for q in range(3):
                        start = b * 64 + q * 16
                        grads[p, shift, q, 2 * two + b] = low[start:start + 16]

    def lhs(p, qs, rs):
        rows = [grads[p, rs, qs + q, b] for q in range(2) for b in range(B)]
        return jnp.concatenate(rows, 0)

    def tap(i, j, k):
        t = i * 9 + j * 3 + k
        half, place = (0, t) if t < TAPS else (1, t - 13)
        return halves[half, :, place].reshape(256, CIN)

    choices = (((1, 0),), ((2, 0), (0, 1)))
    for py in range(2):
        for pz in range(2):
            total = jnp.zeros((128, 256), F32)
            extra = jnp.zeros((128, 128), F32)
            for j, qs in choices[py]:
                for k, rs in choices[pz]:
                    two = jnp.concatenate([tap(1, j, k), tap(2, j, k)], 1)
                    total += jnp.dot(lhs(0, qs, rs), two, preferred_element_type=F32)
                    extra += jnp.dot(lhs(1, qs, rs), tap(0, j, k), preferred_element_type=F32)
            values = (total[:, :128], total[:, 128:] + extra)
            for px in range(2):
                for q in range(2):
                    for b in range(B):
                        start = (q * B + b) * 16
                        mixed[px, b, pl.ds((2 * q + py) * 32 + pz, 16, stride=2), :] = (
                            values[px][start:start + 16]
                        )
    for b in range(B):
        for px in range(2):
            paired[b, pl.ds(px, CIN, stride=2), :] = jnp.transpose(mixed[px, b])
        out_ref[b] = paired[b].astype(BF16)


def input_grad_local(mine, other, following):
    return pl.pallas_call(
        input_grad_kernel,
        out_shape=jax.ShapeDtypeStruct((B, 2 * CIN, 128), BF16),
        scratch_shapes=[
            pltpu.VMEM((2, 8, TAPS, 32, CIN), BF16),
            pltpu.VMEM((2, 2, 3, B, HALF, 256), BF16),
            pltpu.VMEM((2, B, 128, CIN), F32),
            pltpu.VMEM((B, 2 * CIN, 128), F32),
        ],
        compiler_params=pltpu.CompilerParams(vmem_limit_bytes=24 * 1024 * 1024),
        cost_estimate=pl.CostEstimate(flops=2_000_000_000, bytes_accessed=3_000_000, transcendentals=0),
        name="input_grad_local",
    )(mine, other, following)


SMALL = pltpu.CompilerParams(vmem_limit_bytes=4 * 1024 * 1024)


def sum_kernel(parts_ref, out_ref):
    total = parts_ref[0].astype(F32)
    for i in range(1, 16):
        total = total + parts_ref[i].astype(F32)
    for i in range(16):
        out_ref[i] = total.astype(BF16)


def sum_and_copy(parts):
    return pl.pallas_call(
        sum_kernel,
        out_shape=jax.ShapeDtypeStruct(parts.shape, BF16),
        compiler_params=SMALL,
        name="sum_and_copy",
    )(parts)


def swap(values, axis):
    return lax.all_to_all(values, axis, split_axis=0, concat_axis=0, tiled=True)


def body(volume, kernel, out_grad):
    spaces = lax.axis_size("space")
    g = out_grad.reshape(B, 32, 256)
    ker = kernel.reshape(27, 32, CIN)
    to_previous = [(i + 1, i) for i in range(spaces - 1)]
    to_next = [(i, i + 1) for i in range(spaces - 1)]
    g_next = lax.ppermute(g, "space", to_previous)
    packed = pack(ker, g)
    vol = volume.reshape(B, CIN, 2, 8, 128).transpose(0, 1, 3, 2, 4).reshape(B, 2048, 128)
    mine = swap(packed, "filt")
    own, send, dw, odd = conv_local(vol, ker, g)
    dw = next_local(odd, g_next, dw)
    dw, mine = lax.optimization_barrier((dw, mine))
    came = lax.ppermute(send, "space", to_next)
    other = lax.ppermute(mine, "space", [(i, i ^ 1) for i in range(spaces)])
    following = lax.ppermute(mine[:, TAPS:], "space", to_previous)
    summed = swap(sum_and_copy(swap(dw.reshape(16, OWN, CIN), "space")), "space")
    output = (own + came).astype(BF16).reshape(B, 32, 1, 256)
    input_grad = input_grad_local(mine, other, following).reshape(B, CIN, 2, 128)
    summed, input_grad = lax.optimization_barrier((summed, input_grad))
    kernel_grad = summed.reshape(ROWS, CIN)[:864].astype(F32).reshape(3, 3, 3, 32, CIN)
    return (output, input_grad, kernel_grad)


def solution(mesh):
    return jax.shard_map(
        body,
        mesh=mesh,
        in_specs=(
            P(None, None, "space", None),
            P(None, None, None, "filt", None),
            P(None, "filt", "space", None),
        ),
        out_specs=(
            P(None, "filt", "space", None),
            P(None, None, "space", "filt"),
            P(None, None, None, "filt", None),
        ),
        check_vma=False,
    )
```

time: 62.4 us -> 57.7 us (0.925)
  waiting for transfers between devices: 16.2 us -> 10.6 us
  local copies, waits for them, and re-layouts: 2.4 us -> 0.67 us
  Pallas kernels: 13.6 us -> 15.2 us
  starting transfers between devices: 27.4 us -> 28.6 us
    ppermute x1, waiting for transfers between devices: 3.41 us -> 0.01 us  [body(): g_next = lax.ppermute(g, 'space', to_previous)]
    pallas_call x2 -> x3, Pallas kernels: 10.1 us -> 12.7 us  [the longest x1 8.06 us: conv_local(): pl.pallas_call(conv_kernel, grid=(B,), in_specs=[pl.BlockSpec(memory_spac...]
    all_to_all x3, waiting for transfers between devices: 12.8 us -> 10.6 us  [swap(): return lax.all_to_all(values, axis, split_axis=0, concat_axis=0, tiled=True)]
    unnamed x8, local copies, waits for them, and re-layouts: 2.37 us -> 0.64 us
    all_to_all x3, starting transfers between devices: 18.3 us -> 19.4 us  [swap(): return lax.all_to_all(values, axis, split_axis=0, concat_axis=0, tiled=True)]
    pallas_call x1, Pallas kernels: 1.74 us -> 0.73 us  [sum_and_copy(): pl.pallas_call(sum_kernel, out_shape=jax.ShapeDtypeStruct(parts.shape, BF...]
  transfers between devices with their start and end apart: 7 -> 7, of which waited for: 3 -> 3; matrix products, arithmetic and copies ran while one was open for 2% -> 1% of each run, Pallas kernels for 16% -> 23%
where the time goes in v3:
time: 57.7 us; the launch traced here: 57.3 us
  starting transfers between devices  28.6 us (50%)
  Pallas kernels  15.2 us (26%)
  waiting for transfers between devices  10.6 us (18%)
  other arithmetic  1.46 us (3%)
  between operations  0.74 us (1%)
  local copies, waits for them, and re-layouts  0.67 us (1%)
    all_to_all x3, starting transfers between devices, swap(): return lax.all_to_all(values, axis, split_axis=0, concat_axis=0, tiled=True)  19.4 us
    all_to_all x3, waiting for transfers between devices, swap(): return lax.all_to_all(values, axis, split_axis=0, concat_axis=0, tiled=True)  10.6 us
    pallas_call x1, Pallas kernels, conv_local(): pl.pallas_call(conv_kernel, grid=(B,), in_specs=[pl.BlockSpec(memory_spac...  8.06 us
    ppermute x1, starting transfers between devices, body(): came = lax.ppermute(send, 'space', to_next)  3.54 us
    ppermute x1, starting transfers between devices, body(): g_next = lax.ppermute(g, 'space', to_previous)  2.86 us
    pallas_call x1, Pallas kernels, next_local(): pl.pallas_call(next_kernel, in_specs=[pl.BlockSpec(memory_space=pltpu.HBM...  2.61 us
    pallas_call x1, Pallas kernels, pack(): pl.pallas_call(pack_kernel, in_specs=[pl.BlockSpec(memory_space=pltpu.HBM...  2.05 us
    ppermute x1, starting transfers between devices, body(): following = lax.ppermute(mine[:, TAPS:], 'space', to_previous)  1.92 us
  transfers between devices with their start and end apart: 7, of which 3 were waited for; matrix products, arithmetic and copies ran while one was open for 1% of the time, Pallas kernels for 23%

profile of v3, /device:TPU:1, one launch (start us, length us, event | category | flops | bytes accessed | tf_op | source)
XLA Modules:
  0.0 57.3 jit_solution(8559574222543977038)
XLA Ops:
  0.6 0.0 copy-start.1
  0.6 2.1 %pack.1 = bf16[8,16,32,128]{3,2,1,0:T(8,128)(2,1)} custom-call(bf16[27,32,128]{2,1,0:T(8,128)(2,1)} %bitcast.19, bf16[4,32,256]{2,1,0:T(8,128)(2,1)} %bitcast.21), custom_call_target="tpu_custom_call" | custom-call | tf_op jit(solution)/shard_map/pack/pallas_call | solution.py:215
  2.7 6.2 %all-to-all-start = ((bf16[8,16,32,128]{3,2,1,0:T(8,128)(2,1)}), bf16[8,16,32,128]{3,2,1,0:T(8,128)(2,1)S(1)}, u32[]{:S(2)}, u32[]{:S(2)}) async-start(bf16[8,16,32,128]{3,2,1,0:T(8,128)(2,1)} %pack.1), calls=%async_computation | async-start | bytes 2097152 | tf_op jit(solution)/shard_map/all_to_all | solution.py:318
  8.9 2.9 %collective-permute-start.1 = (bf16[4,32,256]{2,1,0:T(8,128)(2,1)S(1)}, bf16[4,32,256]{2,1,0:T(8,128)(2,1)S(1)}, u32[]{:S(2)}, u32[]{:S(2)}) collective-permute-start(bf16[4,32,256]{2,1,0:T(8,128)(2,1)S(1)} %bitcast.23), channel_id=1, source_target_pairs={{8,0},{16,8},{24,16},{32,24},{40,32},{48,40},{56,48},{64,56},{72,6... | collective-permute-start | bytes 196616 | tf_op jit(solution)/shard_map/ppermute | solution.py:327
  11.8 8.1 %conv_local.1 = (f32[4,32,256]{2,1,0:T(8,128)}, f32[4,32,256]{2,1,0:T(8,128)}, bf16[896,128]{1,0:T(8,128)(2,1)}, bf16[4,3,33,16,128]{4,3,2,1,0:T(8,128)(2,1)}) custom-call(bf16[4,2048,128]{2,1,0:T(8,128)(2,1)} %bitcast.24, bf16[27,32,128]{2,1,0:T(8,128)(2,1)} %bitcast.20, bf16[4,32,256]{2,1,0:T(8,128)(2,1)} %bitcast.22), custom_call_target="tpu_custom_call" | custom-call | flops 6000000000 | bytes 4000000 | tf_op jit(solution)/shard_map/conv_local/pallas_call | solution.py:120
  19.9 0.0 copy-start.2
  19.9 0.0 collective-permute-done.1.gn_ref
  19.9 0.0 copy-start.3
  19.9 0.6 %copy-done.3 = bf16[4,32,256]{2,1,0:T(8,128)(2,1)} copy-done((bf16[4,32,256]{2,1,0:T(8,128)(2,1)}, bf16[4,32,256]{2,1,0:T(8,128)(2,1)S(1)}, u32[]{:S(2)}) %copy-start.3) | copy-done | bytes 65560
  20.5 2.6 %next_local.1 = bf16[896,128]{1,0:T(8,128)(2,1)} custom-call(bf16[4,3,33,16,128]{4,3,2,1,0:T(8,128)(2,1)} %get-tuple-element.13.odd_ref, bf16[4,32,256]{2,1,0:T(8,128)(2,1)} %copy-done.3, bf16[896,128]{1,0:T(8,128)(2,1)} %get-tuple-element.14._), custom_call_target="tpu_custom_call", output_to_operand_aliasing={{}: (2, {})} | custom-call | flops 1000000000 | bytes 2000000 | tf_op jit(solution)/shard_map/next_local/pallas_call | solution.py:170
  23.1 1.6 %all-to-all-done.mine_ref = bf16[8,16,32,128]{3,2,1,0:T(8,128)(2,1)S(1)} async-done(((bf16[8,16,32,128]{3,2,1,0:T(8,128)(2,1)}), bf16[8,16,32,128]{3,2,1,0:T(8,128)(2,1)S(1)}, u32[]{:S(2)}, u32[]{:S(2)}) %all-to-all-start) | async-done | bytes 1048608 | tf_op jit(solution)/shard_map/all_to_all | solution.py:318
  24.7 0.8 %collective-permute-start.2 = (bf16[8,16,32,128]{3,2,1,0:T(8,128)(2,1)S(1)}, bf16[8,16,32,128]{3,2,1,0:T(8,128)(2,1)S(1)}, u32[]{:S(2)}, u32[]{:S(2)}) collective-permute-start(bf16[8,16,32,128]{3,2,1,0:T(8,128)(2,1)S(1)} %all-to-all-done.mine_ref), channel_id=1, source_target_pairs={{0,8},{8,0},{16,24},{24,16},{32,40},{40,32},{48,56},{56,48},{64,72... | collective-permute-start | bytes 3145736 | tf_op jit(solution)/shard_map/ppermute | solution.py:335
  25.6 7.6 %all-to-all-start.1 = ((bf16[16,56,128]{2,1,0:T(8,128)(2,1)}), bf16[16,56,128]{2,1,0:T(8,128)(2,1)S(1)}, u32[]{:S(2)}, u32[]{:S(2)}) async-start(bf16[16,56,128]{2,1,0:T(8,128)(2,1)} %bitcast.18), calls=%async_computation.1 | async-start | bytes 458752 | tf_op jit(solution)/shard_map/all_to_all | solution.py:318
  33.2 3.5 %collective-permute-start = (f32[4,32,256]{2,1,0:T(8,128)S(1)}, f32[4,32,256]{2,1,0:T(8,128)S(1)}, u32[]{:S(2)}, u32[]{:S(2)}) collective-permute-start(f32[4,32,256]{2,1,0:T(8,128)S(1)} %copy-done.2), channel_id=1, source_target_pairs={{0,8},{8,16},{16,24},{24,32},{32,40},{40,48},{48,56},{56,64},{64,7... | collective-permute-start | bytes 393224 | tf_op jit(solution)/shard_map/ppermute | solution.py:334
  36.8 1.9 %collective-permute-start.3 = (bf16[8,2,32,128]{3,2,1,0:T(8,128)(2,1)S(1)}, bf16[8,2,32,128]{3,2,1,0:T(8,128)(2,1)S(1)}, u32[]{:S(2)}, u32[]{:S(2)}) collective-permute-start(bf16[8,2,32,128]{3,2,1,0:T(8,128)(2,1)S(1)} %slice.6), channel_id=1, source_target_pairs={{8,0},{16,8},{24,16},{32,24},{40,32},{48,40},{56,48},{64,56},{72,6... | collective-permute-start | bytes 393224 | tf_op jit(solution)/shard_map/ppermute | solution.py:336
  38.7 3.0 %all-to-all-done.1.parts_ref = bf16[16,56,128]{2,1,0:T(8,128)(2,1)S(1)} async-done(((bf16[16,56,128]{2,1,0:T(8,128)(2,1)}), bf16[16,56,128]{2,1,0:T(8,128)(2,1)S(1)}, u32[]{:S(2)}, u32[]{:S(2)}) %all-to-all-start.1) | async-done | bytes 229408 | tf_op jit(solution)/shard_map/all_to_all | solution.py:318
  41.6 0.7 %sum_and_copy.1 = bf16[16,56,128]{2,1,0:T(8,128)(2,1)} custom-call(bf16[16,56,128]{2,1,0:T(8,128)(2,1)S(1)} %all-to-all-done.1.parts_ref), custom_call_target="tpu_custom_call" | custom-call | tf_op jit(solution)/shard_map/sum_and_copy/pallas_call | solution.py:309
  42.4 5.6 %all-to-all-start.2 = ((bf16[16,56,128]{2,1,0:T(8,128)(2,1)}), bf16[16,56,128]{2,1,0:T(8,128)(2,1)S(1)}, u32[]{:S(2)}, u32[]{:S(2)}) async-start(bf16[16,56,128]{2,1,0:T(8,128)(2,1)} %sum_and_copy.1), calls=%async_computation.2 | async-start | bytes 458752 | tf_op jit(solution)/shard_map/all_to_all | solution.py:318
  48.0 0.0 collective-permute-done
  48.0 0.6 %fusion = bf16[4,32,1,256]{3,1,2,0:T(8,128)(2,1)} fusion(f32[4,32,256]{2,1,0:T(8,128)S(1)} %copy-done, f32[4,32,256]{2,1,0:T(8,128)S(1)} %collective-permute-done), kind=kLoop, calls=%fused_computation.1 | loop fusion | flops 65536 | bytes 327680
  48.6 0.0 collective-permute-done.2.other_ref
  48.6 1.8 %input_grad_local.1 = bf16[4,256,128]{2,1,0:T(8,128)(2,1)} custom-call(bf16[8,16,32,128]{3,2,1,0:T(8,128)(2,1)S(1)} %all-to-all-done.mine_ref, bf16[8,16,32,128]{3,2,1,0:T(8,128)(2,1)S(1)} %collective-permute-done.2.other_ref, bf16[8,2,32,128]{3,2,1,0:T(8,128)(2,1)S(1)} %collective-permute-done.3.next_ref), custom_call_target="tpu_custom_call" | custom-call | flops 2000000000 | bytes 3000000 | tf_op jit(solution)/shard_map/input_grad_local/pallas_call | solution.py:282
  50.4 6.0 %all-to-all-done.2 = bf16[16,56,128]{2,1,0:T(8,128)(2,1)S(1)} async-done(((bf16[16,56,128]{2,1,0:T(8,128)(2,1)}), bf16[16,56,128]{2,1,0:T(8,128)(2,1)S(1)}, u32[]{:S(2)}, u32[]{:S(2)}) %all-to-all-start.2) | async-done | bytes 229408 | tf_op jit(solution)/shard_map/all_to_all | solution.py:318
  56.4 0.8 %convert.1 = f32[3,3,3,32,128]{4,3,2,1,0:T(8,128)} convert(bf16[3,3,3,32,128]{4,3,2,1,0:T(8,128)(2,1)S(1)} %bitcast.17) | non-fusion elementwise | flops 110592 | bytes 663552 | tf_op jit(solution)/shard_map/reshape | solution.py:341
  (7 shorter events, 0.0 us)
Async XLA Ops:
  0.6 8.3 %copy-start.1 = (bf16[4,32,1,256]{3,1,2,0:T(8,128)(2,1)S(1)}, bf16[4,32,1,256]{3,1,2,0:T(8,128)(2,1)}, u32[]{:S(2)}) copy-start(bf16[4,32,1,256]{3,1,2,0:T(8,128)(2,1)} %param.5) | copy-start | bytes 196612
  2.7 22.0 %all-to-all-start = ((bf16[8,16,32,128]{3,2,1,0:T(8,128)(2,1)}), bf16[8,16,32,128]{3,2,1,0:T(8,128)(2,1)S(1)}, u32[]{:S(2)}, u32[]{:S(2)}) async-start(bf16[8,16,32,128]{3,2,1,0:T(8,128)(2,1)} %pack.1), calls=%async_computation | async-start | bytes 2097152 | tf_op jit(solution)/shard_map/all_to_all | solution.py:318
  8.9 11.0 %collective-permute-start.1 = (bf16[4,32,256]{2,1,0:T(8,128)(2,1)S(1)}, bf16[4,32,256]{2,1,0:T(8,128)(2,1)S(1)}, u32[]{:S(2)}, u32[]{:S(2)}) collective-permute-start(bf16[4,32,256]{2,1,0:T(8,128)(2,1)S(1)} %bitcast.23), channel_id=1, source_target_pairs={{8,0},{16,8},{24,16},{32,24},{40,32},{48,40},{56,48},{64,56},{72,6... | collective-permute-start | bytes 196616 | tf_op jit(solution)/shard_map/ppermute | solution.py:327
  19.9 13.3 %copy-start.2 = (f32[4,32,256]{2,1,0:T(8,128)S(1)}, f32[4,32,256]{2,1,0:T(8,128)}, u32[]{:S(2)}) copy-start(f32[4,32,256]{2,1,0:T(8,128)} %get-tuple-element.12) | copy-start | bytes 393220
  19.9 0.6 %copy-start.3 = (bf16[4,32,256]{2,1,0:T(8,128)(2,1)}, bf16[4,32,256]{2,1,0:T(8,128)(2,1)S(1)}, u32[]{:S(2)}) copy-start(bf16[4,32,256]{2,1,0:T(8,128)(2,1)S(1)} %collective-permute-done.1.gn_ref) | copy-start | bytes 196612
  20.5 27.5 %copy-start = (f32[4,32,256]{2,1,0:T(8,128)S(1)}, f32[4,32,256]{2,1,0:T(8,128)}, u32[]{:S(2)}) copy-start(f32[4,32,256]{2,1,0:T(8,128)} %get-tuple-element.11) | copy-start | bytes 393220
  24.7 23.9 %collective-permute-start.2 = (bf16[8,16,32,128]{3,2,1,0:T(8,128)(2,1)S(1)}, bf16[8,16,32,128]{3,2,1,0:T(8,128)(2,1)S(1)}, u32[]{:S(2)}, u32[]{:S(2)}) collective-permute-start(bf16[8,16,32,128]{3,2,1,0:T(8,128)(2,1)S(1)} %all-to-all-done.mine_ref), channel_id=1, source_target_pairs={{0,8},{8,0},{16,24},{24,16},{32,40},{40,32},{48,56},{56,48},{64,72... | collective-permute-start | bytes 3145736 | tf_op jit(solution)/shard_map/ppermute | solution.py:335
  25.6 16.1 %all-to-all-start.1 = ((bf16[16,56,128]{2,1,0:T(8,128)(2,1)}), bf16[16,56,128]{2,1,0:T(8,128)(2,1)S(1)}, u32[]{:S(2)}, u32[]{:S(2)}) async-start(bf16[16,56,128]{2,1,0:T(8,128)(2,1)} %bitcast.18), calls=%async_computation.1 | async-start | bytes 458752 | tf_op jit(solution)/shard_map/all_to_all | solution.py:318
  33.2 14.8 %collective-permute-start = (f32[4,32,256]{2,1,0:T(8,128)S(1)}, f32[4,32,256]{2,1,0:T(8,128)S(1)}, u32[]{:S(2)}, u32[]{:S(2)}) collective-permute-start(f32[4,32,256]{2,1,0:T(8,128)S(1)} %copy-done.2), channel_id=1, source_target_pairs={{0,8},{8,16},{16,24},{24,32},{32,40},{40,48},{48,56},{56,64},{64,7... | collective-permute-start | bytes 393224 | tf_op jit(solution)/shard_map/ppermute | solution.py:334
  36.8 11.9 %collective-permute-start.3 = (bf16[8,2,32,128]{3,2,1,0:T(8,128)(2,1)S(1)}, bf16[8,2,32,128]{3,2,1,0:T(8,128)(2,1)S(1)}, u32[]{:S(2)}, u32[]{:S(2)}) collective-permute-start(bf16[8,2,32,128]{3,2,1,0:T(8,128)(2,1)S(1)} %slice.6), channel_id=1, source_target_pairs={{8,0},{16,8},{24,16},{32,24},{40,32},{48,40},{56,48},{64,56},{72,6... | collective-permute-start | bytes 393224 | tf_op jit(solution)/shard_map/ppermute | solution.py:336
  42.4 14.0 %all-to-all-start.2 = ((bf16[16,56,128]{2,1,0:T(8,128)(2,1)}), bf16[16,56,128]{2,1,0:T(8,128)(2,1)S(1)}, u32[]{:S(2)}, u32[]{:S(2)}) async-start(bf16[16,56,128]{2,1,0:T(8,128)(2,1)} %sum_and_copy.1), calls=%async_computation.2 | async-start | bytes 458752 | tf_op jit(solution)/shard_map/all_to_all | solution.py:318

commit v4 on v3

--- a/solution.py
+++ b/solution.py
@@ -15,8 +15,7 @@
 FULL = 63_000_000
 TAPS = 14
 PACKED = TAPS + 2
-ROWS = 896
-OWN = 56
+HELD = 432
 
 
 def iota(shape, axis):
@@ -31,7 +30,7 @@
     return jnp.concatenate(parts, 1)
 
 
-def conv_kernel(vol_ref, ker_ref, g_ref, own_ref, send_ref, dw_ref, odd_ref,
+def conv_kernel(vol_ref, ker_ref, g_ref, own_ref, send_ref, odd_ref, keep_ref, go_ref,
                 total, raw, arrived, ker_in, grads_in, perm, select, planes, cols):
     step = pl.program_id(0)
 
@@ -61,7 +60,6 @@
         wanted = (col == ((row >> 4) & 3) * 32 + depth) & (depth >= 0)
         select[...] = jnp.where(wanted, 1.0, 0.0).astype(BF16)
         total[...] = jnp.zeros_like(total)
-        dw_ref[...] = jnp.zeros_like(dw_ref)
         for k in range(3):
             planes[k, 0] = jnp.zeros((HALF, CIN), BF16)
 
@@ -111,7 +109,14 @@
 
     @pl.when(step == B - 1)
     def _():
-        dw_ref[288:864] = total[...].astype(BF16)
+        first = lax.rem(lax.axis_index("space"), 2) == 0
+        for chosen, low_ref, high_ref in ((first, keep_ref, go_ref), (~first, go_ref, keep_ref)):
+
+            @pl.when(chosen)
+            def _():
+                low_ref[:288] = jnp.zeros((288, CIN), F32)
+                low_ref[288:] = total[:144]
+                high_ref[...] = total[144:]
 
 
 def conv_local(vol, ker, g):
@@ -121,12 +126,13 @@
         conv_kernel,
         grid=(B,),
         in_specs=[pl.BlockSpec(memory_space=pltpu.HBM)] * 3,
-        out_specs=[per_sample(32, 256), per_sample(32, 256), whole(ROWS, CIN), per_sample(3, EDGE + 1, HALF, CIN)],
+        out_specs=[per_sample(32, 256), per_sample(32, 256), per_sample(3, EDGE + 1, HALF, CIN), whole(HELD, CIN), whole(HELD, CIN)],
         out_shape=[
             jax.ShapeDtypeStruct((B, 32, 256), F32),
             jax.ShapeDtypeStruct((B, 32, 256), F32),
-            jax.ShapeDtypeStruct((ROWS, CIN), BF16),
             jax.ShapeDtypeStruct((B, 3, EDGE + 1, HALF, CIN), BF16),
+            jax.ShapeDtypeStruct((HELD, CIN), F32),
+            jax.ShapeDtypeStruct((HELD, CIN), F32),
         ],
         scratch_shapes=[
             pltpu.VMEM((576, CIN), F32),
@@ -145,7 +151,7 @@
     )(vol, ker, g)
 
 
-def next_kernel(odd_ref, gn_ref, _, dw_ref, odd, grad, low, arrived):
+def next_kernel(odd_ref, gn_ref, _, __, keep_ref, go_ref, odd, grad, low, arrived):
     copies = [pltpu.make_async_copy(gn_ref, grad, arrived.at[B])]
     for b in range(B):
         copies.append(pltpu.make_async_copy(odd_ref.at[b], odd.at[b], arrived.at[b]))
@@ -160,29 +166,34 @@
         )
         total = back if total is None else total + back
     for t in range(9):
-        low[t * 32:(t + 1) * 32] = total[:, t * 128:(t + 1) * 128].astype(BF16)
-    last = pltpu.make_async_copy(low, dw_ref.at[pl.ds(0, 288)], arrived.at[B + 1])
-    last.start()
-    last.wait()
-
-
-def next_local(odd, gn, dw):
+        low[t * 32:(t + 1) * 32] = total[:, t * 128:(t + 1) * 128]
+    first = lax.rem(lax.axis_index("space"), 2) == 0
+    for chosen, ref in ((first, keep_ref), (~first, go_ref)):
+
+        @pl.when(chosen)
+        def _():
+            last = pltpu.make_async_copy(low, ref.at[pl.ds(0, 288)], arrived.at[B + 1])
+            last.start()
+            last.wait()
+
+
+def next_local(odd, gn, keep, go):
     return pl.pallas_call(
         next_kernel,
-        in_specs=[pl.BlockSpec(memory_space=pltpu.HBM)] * 3,
-        out_specs=pl.BlockSpec(memory_space=pltpu.HBM),
-        out_shape=jax.ShapeDtypeStruct((ROWS, CIN), BF16),
+        in_specs=[pl.BlockSpec(memory_space=pltpu.HBM)] * 4,
+        out_specs=[pl.BlockSpec(memory_space=pltpu.HBM)] * 2,
+        out_shape=[jax.ShapeDtypeStruct((HELD, CIN), F32)] * 2,
         scratch_shapes=[
             pltpu.VMEM((B, 3, EDGE + 1, HALF, CIN), BF16),
             pltpu.VMEM((B, 32, 256), BF16),
-            pltpu.VMEM((288, CIN), BF16),
+            pltpu.VMEM((288, CIN), F32),
             pltpu.SemaphoreType.DMA((B + 2,)),
         ],
-        input_output_aliases={2: 0},
+        input_output_aliases={2: 0, 3: 1},
         compiler_params=pltpu.CompilerParams(vmem_limit_bytes=FULL),
         cost_estimate=pl.CostEstimate(flops=1_000_000_000, bytes_accessed=2_000_000, transcendentals=0),
         name="next_local",
-    )(odd, gn, dw)
+    )(odd, gn, keep, go)
 
 
 def pack_kernel(ker_ref, g_ref, out_ref, half, grad, cells, sent):
@@ -297,21 +308,19 @@
 SMALL = pltpu.CompilerParams(vmem_limit_bytes=4 * 1024 * 1024)
 
 
-def sum_kernel(parts_ref, out_ref):
-    total = parts_ref[0].astype(F32)
-    for i in range(1, 16):
-        total = total + parts_ref[i].astype(F32)
-    for i in range(16):
-        out_ref[i] = total.astype(BF16)
-
-
-def sum_and_copy(parts):
-    return pl.pallas_call(
-        sum_kernel,
-        out_shape=jax.ShapeDtypeStruct(parts.shape, BF16),
+def place_kernel(mine_ref, theirs_ref, out_ref):
+    core = lax.rem(lax.axis_index("space"), 2)
+    out_ref[pl.ds(pl.multiple_of(core * HELD, 8), HELD)] = mine_ref[...]
+    out_ref[pl.ds(pl.multiple_of((1 - core) * HELD, 8), HELD)] = theirs_ref[...]
+
+
+def place(mine, theirs):
+    return pl.pallas_call(
+        place_kernel,
+        out_shape=jax.ShapeDtypeStruct((2 * HELD, CIN), F32),
         compiler_params=SMALL,
-        name="sum_and_copy",
-    )(parts)
+        name="place",
+    )(mine, theirs)
 
 
 def swap(values, axis):
@@ -328,17 +337,26 @@
     packed = pack(ker, g)
     vol = volume.reshape(B, CIN, 2, 8, 128).transpose(0, 1, 3, 2, 4).reshape(B, 2048, 128)
     mine = swap(packed, "filt")
-    own, send, dw, odd = conv_local(vol, ker, g)
-    dw = next_local(odd, g_next, dw)
-    dw, mine = lax.optimization_barrier((dw, mine))
+    own, send, odd, keep, go = conv_local(vol, ker, g)
+    keep, go = next_local(odd, g_next, keep, go)
+    keep, go, mine = lax.optimization_barrier((keep, go, mine))
+
+    def exchange(values, bits):
+        return lax.ppermute(values, "space", [(i, i ^ bits) for i in range(spaces)])
+
     came = lax.ppermute(send, "space", to_next)
-    other = lax.ppermute(mine, "space", [(i, i ^ 1) for i in range(spaces)])
+    other = exchange(mine, 1)
     following = lax.ppermute(mine[:, TAPS:], "space", to_previous)
-    summed = swap(sum_and_copy(swap(dw.reshape(16, OWN, CIN), "space")), "space")
+    pair = (keep + exchange(go, 1)).astype(BF16)
+    pair, following = lax.optimization_barrier((pair, following))
+    four = (pair.astype(F32) + exchange(pair, 8).astype(F32)).astype(BF16)
+    parts = [exchange(four, bits) for bits in (2, 4, 6)]
+    input_grad = input_grad_local(mine, other, following).reshape(B, CIN, 2, 128)
+    parts, input_grad = lax.optimization_barrier((parts, input_grad))
+    near, far, farther = (part.astype(F32) for part in parts)
+    held = (four.astype(F32) + near) + (far + farther)
+    kernel_grad = place(held, exchange(held, 1)).reshape(3, 3, 3, 32, CIN)
     output = (own + came).astype(BF16).reshape(B, 32, 1, 256)
-    input_grad = input_grad_local(mine, other, following).reshape(B, CIN, 2, 128)
-    summed, input_grad = lax.optimization_barrier((summed, input_grad))
-    kernel_grad = summed.reshape(ROWS, CIN)[:864].astype(F32).reshape(3, 3, 3, 32, CIN)
     return (output, input_grad, kernel_grad)
 
 

time: 57.7 us -> 52.9 us (0.917)
  starting transfers between devices: 28.6 us -> 24.5 us
  waiting for transfers between devices: 10.6 us -> 9.58 us
    all_to_all x3 -> x1, starting transfers between devices: 19.4 us -> 6.22 us  [swap(): return lax.all_to_all(values, axis, split_axis=0, concat_axis=0, tiled=True)]
    ppermute x1 -> x7, starting transfers between devices: 0.84 us -> 11 us  [exchange(): return lax.ppermute(values, 'space', [(i, i ^ bits) for i in range(spaces)])]
    all_to_all x3 -> x1, waiting for transfers between devices: 10.6 us -> 1.48 us  [swap(): return lax.all_to_all(values, axis, split_axis=0, concat_axis=0, tiled=True)]
    ppermute x1 -> x7, waiting for transfers between devices: 0.01 us -> 5.44 us  [exchange(): return lax.ppermute(values, 'space', [(i, i ^ bits) for i in range(spaces)])]
    ppermute x1, waiting for transfers between devices: 0.01 us -> 2.66 us  [body(): following = lax.ppermute(mine[:, TAPS:], 'space', to_previous)]
    ppermute x1, starting transfers between devices: 3.54 us -> 2.05 us  [body(): came = lax.ppermute(send, 'space', to_next)]
    convert_element_type x0 -> x2, other arithmetic: none -> 0.99 us  [the longest x1 0.96 us: body(): pair = (keep + exchange(go, 1)).astype(BF16)]
    reshape x1 -> x0, other arithmetic: 0.81 us -> none  [body(): summed.reshape(ROWS, CIN)[:864].astype(F32).reshape(3, 3, 3, 32, CIN)]
  transfers between devices with their start and end apart: 7 -> 11, of which waited for: 3 -> 7; matrix products, arithmetic and copies ran while one was open for 1% -> 3% of each run, Pallas kernels for 23% -> 24%
where the time goes in v4:
time: 52.9 us; the launch traced here: 52.6 us
  starting transfers between devices  24.5 us (46%)
  Pallas kernels  15.4 us (29%)
  waiting for transfers between devices  9.58 us (18%)
  other arithmetic  1.69 us (3%)
  between operations  0.74 us (1%)
  local copies, waits for them, and re-layouts  0.65 us (1%)
    ppermute x7, starting transfers between devices, exchange(): return lax.ppermute(values, 'space', [(i, i ^ bits) for i in range(spaces)])  11 us
    pallas_call x1, Pallas kernels, conv_local(): pl.pallas_call(conv_kernel, grid=(B,), in_specs=[pl.BlockSpec(memory_spac...  8.16 us
    all_to_all x1, starting transfers between devices, swap(): return lax.all_to_all(values, axis, split_axis=0, concat_axis=0, tiled=True)  6.22 us
    ppermute x7, waiting for transfers between devices, exchange(): return lax.ppermute(values, 'space', [(i, i ^ bits) for i in range(spaces)])  5.44 us
    ppermute x1, starting transfers between devices, body(): g_next = lax.ppermute(g, 'space', to_previous)  2.86 us
    ppermute x1, waiting for transfers between devices, body(): following = lax.ppermute(mine[:, TAPS:], 'space', to_previous)  2.66 us
    pallas_call x1, Pallas kernels, next_local(): pl.pallas_call(next_kernel, in_specs=[pl.BlockSpec(memory_space=pltpu.HBM...  2.64 us
    ppermute x1, starting transfers between devices, body(): following = lax.ppermute(mine[:, TAPS:], 'space', to_previous)  2.42 us
  transfers between devices with their start and end apart: 11, of which 7 were waited for; matrix products, arithmetic and copies ran while one was open for 3% of the time, Pallas kernels for 24%

profile of v4, /device:TPU:1, one launch (start us, length us, event | category | flops | bytes accessed | tf_op | source)
XLA Modules:
  0.0 52.6 jit_solution(13531120158899650611)
XLA Ops:
  0.6 2.0 %pack.1 = bf16[8,16,32,128]{3,2,1,0:T(8,128)(2,1)} custom-call(bf16[27,32,128]{2,1,0:T(8,128)(2,1)} %bitcast.14, bf16[4,32,256]{2,1,0:T(8,128)(2,1)} %bitcast.16), custom_call_target="tpu_custom_call" | custom-call | tf_op jit(solution)/shard_map/pack/pallas_call | solution.py:226
  2.7 6.2 %all-to-all-start = ((bf16[8,16,32,128]{3,2,1,0:T(8,128)(2,1)}), bf16[8,16,32,128]{3,2,1,0:T(8,128)(2,1)S(1)}, u32[]{:S(2)}, u32[]{:S(2)}) async-start(bf16[8,16,32,128]{3,2,1,0:T(8,128)(2,1)} %pack.1), calls=%async_computation | async-start | bytes 2097152 | tf_op jit(solution)/shard_map/all_to_all | solution.py:327
  8.9 2.9 %collective-permute-start.1 = (bf16[4,32,256]{2,1,0:T(8,128)(2,1)S(1)}, bf16[4,32,256]{2,1,0:T(8,128)(2,1)S(1)}, u32[]{:S(2)}, u32[]{:S(2)}) collective-permute-start(bf16[4,32,256]{2,1,0:T(8,128)(2,1)S(1)} %bitcast.18), channel_id=1, source_target_pairs={{8,0},{16,8},{24,16},{32,24},{40,32},{48,40},{56,48},{64,56},{72,6... | collective-permute-start | bytes 196616 | tf_op jit(solution)/shard_map/ppermute | solution.py:336
  11.8 8.2 %conv_local.1 = (f32[4,32,256]{2,1,0:T(8,128)}, f32[4,32,256]{2,1,0:T(8,128)}, bf16[4,3,33,16,128]{4,3,2,1,0:T(8,128)(2,1)}, f32[432,128]{1,0:T(8,128)}, f32[432,128]{1,0:T(8,128)}) custom-call(bf16[4,2048,128]{2,1,0:T(8,128)(2,1)} %bitcast.19, bf16[27,32,128]{2,1,0:T(8,128)(2,1)} %bitcast.15, bf16[4,32,256]{2,1,0:T(8,128)(2,1)} %bitcast.17), custom_call_target="tpu_custom_call" | custom-call | flops 6000000000 | bytes 4000000 | tf_op jit(solution)/shard_map/conv_local/pallas_call | solution.py:125
  20.0 0.6 %copy-done.3 = bf16[4,32,256]{2,1,0:T(8,128)(2,1)} copy-done((bf16[4,32,256]{2,1,0:T(8,128)(2,1)}, bf16[4,32,256]{2,1,0:T(8,128)(2,1)S(1)}, u32[]{:S(2)}) %copy-start.3) | copy-done | bytes 65560
  20.6 2.6 %next_local.1 = (f32[432,128]{1,0:T(8,128)}, f32[432,128]{1,0:T(8,128)}) custom-call(bf16[4,3,33,16,128]{4,3,2,1,0:T(8,128)(2,1)} %get-tuple-element.21.odd_ref, bf16[4,32,256]{2,1,0:T(8,128)(2,1)} %copy-done.3, f32[432,128]{1,0:T(8,128)} %get-tuple-element.22._, f32[432,128]{1,0:T(8,128)} %get-tuple-element.23.__), custom_call_target="tpu_custom_call", output_to_operand_aliasing={{0}: (2, {}), {1}: (3, {})} | custom-call | flops 1000000000 | bytes 2000000 | tf_op jit(solution)/shard_map/next_local/pallas_call | solution.py:181
  23.2 1.5 %all-to-all-done.mine_ref = bf16[8,16,32,128]{3,2,1,0:T(8,128)(2,1)S(1)} async-done(((bf16[8,16,32,128]{3,2,1,0:T(8,128)(2,1)}), bf16[8,16,32,128]{3,2,1,0:T(8,128)(2,1)S(1)}, u32[]{:S(2)}, u32[]{:S(2)}) %all-to-all-start) | async-done | bytes 1048608 | tf_op jit(solution)/shard_map/all_to_all | solution.py:327
  24.7 0.8 %collective-permute-start.8 = (bf16[8,16,32,128]{3,2,1,0:T(8,128)(2,1)S(1)}, bf16[8,16,32,128]{3,2,1,0:T(8,128)(2,1)S(1)}, u32[]{:S(2)}, u32[]{:S(2)}) collective-permute-start(bf16[8,16,32,128]{3,2,1,0:T(8,128)(2,1)S(1)} %all-to-all-done.mine_ref), channel_id=1, source_target_pairs={{0,8},{8,0},{16,24},{24,16},{32,40},{40,32},{48,56},{56,48},{64,72... | collective-permute-start | bytes 3145736 | tf_op jit(solution)/shard_map/ppermute | solution.py:345
  25.6 2.4 %collective-permute-start.3 = (bf16[8,2,32,128]{3,2,1,0:T(8,128)(2,1)S(1)}, bf16[8,2,32,128]{3,2,1,0:T(8,128)(2,1)S(1)}, u32[]{:S(2)}, u32[]{:S(2)}) collective-permute-start(bf16[8,2,32,128]{3,2,1,0:T(8,128)(2,1)S(1)} %slice.3), channel_id=1, source_target_pairs={{8,0},{16,8},{24,16},{32,24},{40,32},{48,40},{56,48},{64,56},{72,6... | collective-permute-start | bytes 393224 | tf_op jit(solution)/shard_map/ppermute | solution.py:349
  28.0 0.2 collective-permute-done.2
  28.2 1.0 %add_convert_fusion.1 = bf16[432,128]{1,0:T(8,128)(2,1)S(1)} fusion(f32[432,128]{1,0:T(8,128)} %get-tuple-element.26, f32[432,128]{1,0:T(8,128)S(1)} %collective-permute-done.2), kind=kLoop, calls=%fused_computation.2 | loop fusion | flops 110592 | bytes 552960 | tf_op jit(solution)/shard_map/convert_element_type | solution.py:350
  29.2 2.7 %collective-permute-done.3.next_ref = bf16[8,2,32,128]{3,2,1,0:T(8,128)(2,1)S(1)} collective-permute-done((bf16[8,2,32,128]{3,2,1,0:T(8,128)(2,1)S(1)}, bf16[8,2,32,128]{3,2,1,0:T(8,128)(2,1)S(1)}, u32[]{:S(2)}, u32[]{:S(2)}) %collective-permute-start.3) | collective-permute-done | bytes 131104 | tf_op jit(solution)/shard_map/ppermute | solution.py:349
  31.9 3.3 %collective-permute-start.4 = (bf16[432,128]{1,0:T(8,128)(2,1)S(1)}, bf16[432,128]{1,0:T(8,128)(2,1)S(1)}, u32[]{:S(2)}, u32[]{:S(2)}) collective-permute-start(bf16[432,128]{1,0:T(8,128)(2,1)S(1)} %add_convert_fusion.1), channel_id=1, source_target_pairs={{0,64},{8,72},{16,80},{24,88},{32,96},{40,104},{48,112},{56,120},{... | collective-permute-start | bytes 331784 | tf_op jit(solution)/shard_map/ppermute | solution.py:345
  35.2 2.1 %collective-permute-start = (f32[4,32,256]{2,1,0:T(8,128)S(1)}, f32[4,32,256]{2,1,0:T(8,128)S(1)}, u32[]{:S(2)}, u32[]{:S(2)}) collective-permute-start(f32[4,32,256]{2,1,0:T(8,128)S(1)} %copy-done.2), channel_id=1, source_target_pairs={{0,8},{8,16},{16,24},{24,32},{32,40},{40,48},{48,56},{56,64},{64,7... | collective-permute-start | bytes 393224 | tf_op jit(solution)/shard_map/ppermute | solution.py:347
  37.2 0.8 %collective-permute-done.4 = bf16[432,128]{1,0:T(8,128)(2,1)S(1)} collective-permute-done((bf16[432,128]{1,0:T(8,128)(2,1)S(1)}, bf16[432,128]{1,0:T(8,128)(2,1)S(1)}, u32[]{:S(2)}, u32[]{:S(2)}) %collective-permute-start.4) | collective-permute-done | bytes 110624 | tf_op jit(solution)/shard_map/ppermute | solution.py:345
  38.0 0.7 %collective-permute-start.5 = (bf16[432,128]{1,0:T(8,128)(2,1)S(1)}, bf16[432,128]{1,0:T(8,128)(2,1)S(1)}, u32[]{:S(2)}, u32[]{:S(2)}) collective-permute-start(bf16[432,128]{1,0:T(8,128)(2,1)S(1)} %add_convert_fusion), channel_id=1, source_target_pairs={{0,16},{8,24},{16,0},{24,8},{32,48},{40,56},{48,32},{56,40},{64,80... | collective-permute-start | bytes 331784 | tf_op jit(solution)/shard_map/ppermute | solution.py:345
  38.8 5.9 %collective-permute-start.6 = (bf16[432,128]{1,0:T(8,128)(2,1)S(1)}, bf16[432,128]{1,0:T(8,128)(2,1)S(1)}, u32[]{:S(2)}, u32[]{:S(2)}) collective-permute-start(bf16[432,128]{1,0:T(8,128)(2,1)S(1)} %add_convert_fusion), channel_id=1, source_target_pairs={{0,32},{8,40},{16,48},{24,56},{32,0},{40,8},{48,16},{56,24},{64,96... | collective-permute-start | bytes 331784 | tf_op jit(solution)/shard_map/ppermute | solution.py:345
  44.6 1.8 %input_grad_local.1 = bf16[4,256,128]{2,1,0:T(8,128)(2,1)} custom-call(bf16[8,16,32,128]{3,2,1,0:T(8,128)(2,1)S(1)} %all-to-all-done.mine_ref, bf16[8,16,32,128]{3,2,1,0:T(8,128)(2,1)S(1)} %collective-permute-done.8.other_ref, bf16[8,2,32,128]{3,2,1,0:T(8,128)(2,1)S(1)} %collective-permute-done.3.next_ref), custom_call_target="tpu_custom_call" | custom-call | flops 2000000000 | bytes 3000000 | tf_op jit(solution)/shard_map/input_grad_local/pallas_call | solution.py:293
  46.4 1.8 %collective-permute-done.6 = bf16[432,128]{1,0:T(8,128)(2,1)S(1)} collective-permute-done((bf16[432,128]{1,0:T(8,128)(2,1)S(1)}, bf16[432,128]{1,0:T(8,128)(2,1)S(1)}, u32[]{:S(2)}, u32[]{:S(2)}) %collective-permute-start.6) | collective-permute-done | bytes 110624 | tf_op jit(solution)/shard_map/ppermute | solution.py:345
  48.2 1.9 %collective-permute-done.7 = bf16[432,128]{1,0:T(8,128)(2,1)S(1)} collective-permute-done((bf16[432,128]{1,0:T(8,128)(2,1)S(1)}, bf16[432,128]{1,0:T(8,128)(2,1)S(1)}, u32[]{:S(2)}, u32[]{:S(2)}) %collective-permute-start.7) | collective-permute-done | bytes 110624 | tf_op jit(solution)/shard_map/ppermute | solution.py:345
  50.2 0.2 collective-permute-start.9
  50.5 0.6 %fusion = bf16[4,32,1,256]{3,1,2,0:T(8,128)(2,1)} fusion(f32[4,32,256]{2,1,0:T(8,128)S(1)} %copy-done, f32[4,32,256]{2,1,0:T(8,128)S(1)} %collective-permute-done), kind=kLoop, calls=%fused_computation.4 | loop fusion | flops 65536 | bytes 327680
  51.1 0.7 %collective-permute-done.9.theirs_ref = f32[432,128]{1,0:T(8,128)S(1)} collective-permute-done((f32[432,128]{1,0:T(8,128)S(1)}, f32[432,128]{1,0:T(8,128)S(1)}, u32[]{:S(2)}, u32[]{:S(2)}) %collective-permute-start.9) | collective-permute-done | bytes 221216 | tf_op jit(solution)/shard_map/ppermute | solution.py:345
  51.8 0.8 %place.1 = f32[864,128]{1,0:T(8,128)} custom-call(f32[432,128]{1,0:T(8,128)S(1)} %add_add_fusion.mine_ref, f32[432,128]{1,0:T(8,128)S(1)} %collective-permute-done.9.theirs_ref), custom_call_target="tpu_custom_call" | custom-call | tf_op jit(solution)/shard_map/place/pallas_call | solution.py:318
  (16 shorter events, 0.1 us)
Async XLA Ops:
  0.6 8.3 %copy-start.1 = (bf16[4,32,1,256]{3,1,2,0:T(8,128)(2,1)S(1)}, bf16[4,32,1,256]{3,1,2,0:T(8,128)(2,1)}, u32[]{:S(2)}) copy-start(bf16[4,32,1,256]{3,1,2,0:T(8,128)(2,1)} %param.5) | copy-start | bytes 196612
  2.7 22.0 %all-to-all-start = ((bf16[8,16,32,128]{3,2,1,0:T(8,128)(2,1)}), bf16[8,16,32,128]{3,2,1,0:T(8,128)(2,1)S(1)}, u32[]{:S(2)}, u32[]{:S(2)}) async-start(bf16[8,16,32,128]{3,2,1,0:T(8,128)(2,1)} %pack.1), calls=%async_computation | async-start | bytes 2097152 | tf_op jit(solution)/shard_map/all_to_all | solution.py:327
  8.9 11.0 %collective-permute-start.1 = (bf16[4,32,256]{2,1,0:T(8,128)(2,1)S(1)}, bf16[4,32,256]{2,1,0:T(8,128)(2,1)S(1)}, u32[]{:S(2)}, u32[]{:S(2)}) collective-permute-start(bf16[4,32,256]{2,1,0:T(8,128)(2,1)S(1)} %bitcast.18), channel_id=1, source_target_pairs={{8,0},{16,8},{24,16},{32,24},{40,32},{48,40},{56,48},{64,56},{72,6... | collective-permute-start | bytes 196616 | tf_op jit(solution)/shard_map/ppermute | solution.py:336
  20.0 0.6 %copy-start.3 = (bf16[4,32,256]{2,1,0:T(8,128)(2,1)}, bf16[4,32,256]{2,1,0:T(8,128)(2,1)S(1)}, u32[]{:S(2)}) copy-start(bf16[4,32,256]{2,1,0:T(8,128)(2,1)S(1)} %collective-permute-done.1.gn_ref) | copy-start | bytes 196612
  20.6 14.6 %copy-start.2 = (f32[4,32,256]{2,1,0:T(8,128)S(1)}, f32[4,32,256]{2,1,0:T(8,128)}, u32[]{:S(2)}) copy-start(f32[4,32,256]{2,1,0:T(8,128)} %get-tuple-element.20) | copy-start | bytes 393220
  24.7 19.9 %collective-permute-start.8 = (bf16[8,16,32,128]{3,2,1,0:T(8,128)(2,1)S(1)}, bf16[8,16,32,128]{3,2,1,0:T(8,128)(2,1)S(1)}, u32[]{:S(2)}, u32[]{:S(2)}) collective-permute-start(bf16[8,16,32,128]{3,2,1,0:T(8,128)(2,1)S(1)} %all-to-all-done.mine_ref), channel_id=1, source_target_pairs={{0,8},{8,0},{16,24},{24,16},{32,40},{40,32},{48,56},{56,48},{64,72... | collective-permute-start | bytes 3145736 | tf_op jit(solution)/shard_map/ppermute | solution.py:345
  25.6 2.7 %collective-permute-start.2 = (f32[432,128]{1,0:T(8,128)}, f32[432,128]{1,0:T(8,128)S(1)}, u32[]{:S(2)}, u32[]{:S(2)}) collective-permute-start(f32[432,128]{1,0:T(8,128)} %get-tuple-element.27), channel_id=1, source_target_pairs={{0,8},{8,0},{16,24},{24,16},{32,40},{40,32},{48,56},{56,48},{64,72... | collective-permute-start | bytes 663560 | tf_op jit(solution)/shard_map/ppermute | solution.py:345
  25.6 6.3 %collective-permute-start.3 = (bf16[8,2,32,128]{3,2,1,0:T(8,128)(2,1)S(1)}, bf16[8,2,32,128]{3,2,1,0:T(8,128)(2,1)S(1)}, u32[]{:S(2)}, u32[]{:S(2)}) collective-permute-start(bf16[8,2,32,128]{3,2,1,0:T(8,128)(2,1)S(1)} %slice.3), channel_id=1, source_target_pairs={{8,0},{16,8},{24,16},{32,24},{40,32},{48,40},{56,48},{64,56},{72,6... | collective-permute-start | bytes 393224 | tf_op jit(solution)/shard_map/ppermute | solution.py:349
  31.9 6.1 %collective-permute-start.4 = (bf16[432,128]{1,0:T(8,128)(2,1)S(1)}, bf16[432,128]{1,0:T(8,128)(2,1)S(1)}, u32[]{:S(2)}, u32[]{:S(2)}) collective-permute-start(bf16[432,128]{1,0:T(8,128)(2,1)S(1)} %add_convert_fusion.1), channel_id=1, source_target_pairs={{0,64},{8,72},{16,80},{24,88},{32,96},{40,104},{48,112},{56,120},{... | collective-permute-start | bytes 331784 | tf_op jit(solution)/shard_map/ppermute | solution.py:345
  35.2 15.3 %collective-permute-start = (f32[4,32,256]{2,1,0:T(8,128)S(1)}, f32[4,32,256]{2,1,0:T(8,128)S(1)}, u32[]{:S(2)}, u32[]{:S(2)}) collective-permute-start(f32[4,32,256]{2,1,0:T(8,128)S(1)} %copy-done.2), channel_id=1, source_target_pairs={{0,8},{8,16},{16,24},{24,32},{32,40},{40,48},{48,56},{56,64},{64,7... | collective-permute-start | bytes 393224 | tf_op jit(solution)/shard_map/ppermute | solution.py:347
  38.0 12.5 %copy-start = (f32[4,32,256]{2,1,0:T(8,128)S(1)}, f32[4,32,256]{2,1,0:T(8,128)}, u32[]{:S(2)}) copy-start(f32[4,32,256]{2,1,0:T(8,128)} %get-tuple-element.19) | copy-start | bytes 393220
  38.0 8.4 %collective-permute-start.5 = (bf16[432,128]{1,0:T(8,128)(2,1)S(1)}, bf16[432,128]{1,0:T(8,128)(2,1)S(1)}, u32[]{:S(2)}, u32[]{:S(2)}) collective-permute-start(bf16[432,128]{1,0:T(8,128)(2,1)S(1)} %add_convert_fusion), channel_id=1, source_target_pairs={{0,16},{8,24},{16,0},{24,8},{32,48},{40,56},{48,32},{56,40},{64,80... | collective-permute-start | bytes 331784 | tf_op jit(solution)/shard_map/ppermute | solution.py:345
  38.8 9.4 %collective-permute-start.6 = (bf16[432,128]{1,0:T(8,128)(2,1)S(1)}, bf16[432,128]{1,0:T(8,128)(2,1)S(1)}, u32[]{:S(2)}, u32[]{:S(2)}) collective-permute-start(bf16[432,128]{1,0:T(8,128)(2,1)S(1)} %add_convert_fusion), channel_id=1, source_target_pairs={{0,32},{8,40},{16,48},{24,56},{32,0},{40,8},{48,16},{56,24},{64,96... | collective-permute-start | bytes 331784 | tf_op jit(solution)/shard_map/ppermute | solution.py:345
  44.6 5.5 %collective-permute-start.7 = (bf16[432,128]{1,0:T(8,128)(2,1)S(1)}, bf16[432,128]{1,0:T(8,128)(2,1)S(1)}, u32[]{:S(2)}, u32[]{:S(2)}) collective-permute-start(bf16[432,128]{1,0:T(8,128)(2,1)S(1)} %add_convert_fusion), channel_id=1, source_target_pairs={{0,48},{8,56},{16,32},{24,40},{32,16},{40,24},{48,0},{56,8},{64,11... | collective-permute-start | bytes 331784 | tf_op jit(solution)/shard_map/ppermute | solution.py:345
  50.2 1.6 %collective-permute-start.9 = (f32[432,128]{1,0:T(8,128)S(1)}, f32[432,128]{1,0:T(8,128)S(1)}, u32[]{:S(2)}, u32[]{:S(2)}) collective-permute-start(f32[432,128]{1,0:T(8,128)S(1)} %add_add_fusion.mine_ref), channel_id=1, source_target_pairs={{0,8},{8,0},{16,24},{24,16},{32,40},{40,32},{48,56},{56,48},{64,72... | collective-permute-start | bytes 663560 | tf_op jit(solution)/shard_map/ppermute | solution.py:345

commit v5 on v2

v5 whole, which is shorter than its diff:
```python
import jax
import jax.numpy as jnp
from jax import lax
from jax.experimental import pallas as pl
from jax.experimental.pallas import tpu as pltpu
from jax.sharding import PartitionSpec as P

B = 4
CIN = 128
EDGE = 32
HALF = 16
F32 = jnp.float32
BF16 = jnp.bfloat16
NT = (((1,), (1,)), ((), ()))
FULL = 63_000_000
TAPS = 14
PACKED = TAPS + 4
HELD = 432


def iota(shape, axis):
    return lax.broadcasted_iota(jnp.int32, shape, axis)


def cut_cells(grad, cells):
    for b in range(B):
        whole = jnp.concatenate([grad[b], jnp.zeros((32, 128), BF16)], 1)
        lane = (b % 2) * 64
        for f in range(8):
            cells[f, b // 2, :, lane:lane + 64] = whole[:, 32 * f:32 * f + 64]


def prepare_kernel(vol_ref, ker_ref, g_ref, planes_ref, packed_ref,
                   raw, arrived, taps, grad, cells, sent, perm, select, cols):
    step = pl.program_id(0)
    core = lax.rem(lax.axis_index("space"), 2)

    def fetch(b):
        return pltpu.make_async_copy(vol_ref.at[b], raw.at[b], arrived.at[b])

    fetch_taps = pltpu.make_async_copy(ker_ref.at[pl.ds(core * 13, TAPS)], taps, arrived.at[B])
    fetch_grad = pltpu.make_async_copy(g_ref, grad, arrived.at[B + 1])
    copies = [
        pltpu.make_async_copy(taps, packed_ref.at[f, pl.ds(0, TAPS)], sent.at[f]) for f in range(8)
    ]
    copies.append(pltpu.make_async_copy(cells, packed_ref.at[:, pl.ds(TAPS, 2)], sent.at[8]))

    @pl.when(step == 0)
    def _():
        fetch(0).start()
        fetch_taps.start()
        fetch_grad.start()
        for b in range(1, B):
            fetch(b).start()
        row, col = iota((256, 256), 0), iota((256, 256), 1)
        source = (row & 15) * 16 + ((row >> 4) & 7) * 2 + (row >> 7)
        perm[...] = jnp.where(col == source, 1.0, 0.0).astype(BF16)
        row, col = iota((192, 128), 0), iota((192, 128), 1)
        depth = (row & 15) * 2 + (row >> 6) - 1
        wanted = (col == ((row >> 4) & 3) * 32 + depth) & (depth >= 0)
        select[...] = jnp.where(wanted, 1.0, 0.0).astype(BF16)

    @pl.when(step == 1)
    def _():
        fetch_taps.wait()
        for copy in copies[:8]:
            copy.start()
        fetch_grad.wait()
        cut_cells(grad, cells)
        copies[8].start()

    fetch(step).wait()
    wide = jnp.concatenate([raw[step, g * 256:(g + 1) * 256] for g in range(8)], 1)
    moved = jnp.dot(perm[...], wide, preferred_element_type=F32).astype(BF16)
    for lt in range(8):
        for x in range(2):
            start = (x * 8 + lt) * 16
            for g in range(8):
                cols[lt, x * 128 + g * 16:x * 128 + g * 16 + 16, :] = (
                    moved[start:start + 16, g * 128:(g + 1) * 128]
                )
    for x in range(2):
        for k in range(3):
            planes_ref[0, x, k, 0] = jnp.zeros((HALF, CIN), BF16)
    for lt in range(8):
        turned = lax.dot_general(select[...], cols[lt], NT, preferred_element_type=F32).astype(BF16)
        for k in range(3):
            for y in range(4):
                start = k * 64 + y * 16
                for x in range(2):
                    planes_ref[0, x, k, 1 + 4 * lt + y] = (
                        turned[start:start + 16, x * 128:(x + 1) * 128]
                    )

    @pl.when(step == B - 1)
    def _():
        for copy in copies:
            copy.wait()


def per_sample(*shape):
    return pl.BlockSpec((1,) + shape, lambda b: (b,) + (0,) * len(shape))


def whole_array(*shape):
    return pl.BlockSpec(shape, lambda b: (0,) * len(shape))


def prepare(vol, ker, g):
    return pl.pallas_call(
        prepare_kernel,
        grid=(B,),
        in_specs=[pl.BlockSpec(memory_space=pltpu.HBM)] * 3,
        out_specs=[per_sample(2, 3, EDGE + 1, HALF, CIN), pl.BlockSpec(memory_space=pltpu.HBM)],
        out_shape=[
            jax.ShapeDtypeStruct((B, 2, 3, EDGE + 1, HALF, CIN), BF16),
            jax.ShapeDtypeStruct((8, PACKED, 32, 128), BF16),
        ],
        scratch_shapes=[
            pltpu.VMEM((B, 2048, 128), BF16),
            pltpu.SemaphoreType.DMA((B + 2,)),
            pltpu.VMEM((TAPS, 32, CIN), BF16),
            pltpu.VMEM((B, 32, 256), BF16),
            pltpu.VMEM((8, 2, 32, 128), BF16),
            pltpu.SemaphoreType.DMA((9,)),
            pltpu.VMEM((256, 256), BF16),
            pltpu.VMEM((192, 128), BF16),
            pltpu.VMEM((8, 256, 128), BF16),
        ],
        compiler_params=pltpu.CompilerParams(vmem_limit_bytes=FULL),
        cost_estimate=pl.CostEstimate(flops=4_000_000_000, bytes_accessed=5_000_000, transcendentals=0),
        name="prepare",
    )(vol, ker, g)


def next_cells_kernel(gn_ref, _, packed_ref, cells, sent):
    cut_cells(gn_ref, cells)
    copy = pltpu.make_async_copy(cells, packed_ref.at[:, pl.ds(TAPS + 2, 2)], sent)
    copy.start()
    copy.wait()


def next_cells(gn, packed):
    return pl.pallas_call(
        next_cells_kernel,
        in_specs=[pl.BlockSpec(memory_space=pltpu.VMEM), pl.BlockSpec(memory_space=pltpu.HBM)],
        out_specs=pl.BlockSpec(memory_space=pltpu.HBM),
        out_shape=jax.ShapeDtypeStruct((8, PACKED, 32, 128), BF16),
        scratch_shapes=[pltpu.VMEM((8, 2, 32, 128), BF16), pltpu.SemaphoreType.DMA],
        input_output_aliases={1: 0},
        compiler_params=pltpu.CompilerParams(vmem_limit_bytes=FULL),
        name="next_cells",
    )(gn, packed)


def columns(plane):
    parts = []
    for j in range(3):
        for k in range(3):
            parts.append(jnp.concatenate([plane(k, 2 * q + j) for q in range(HALF)], 0))
    return jnp.concatenate(parts, 1)


def conv_kernel(planes_ref, ker_ref, g_ref, gn_ref, own_ref, send_ref, keep_ref, go_ref,
                total):
    step = pl.program_id(0)

    @pl.when(step == 0)
    def _():
        total[...] = jnp.zeros_like(total)

    def weights(i):
        return jnp.concatenate([ker_ref[i * 9 + t] for t in range(9)], 1)

    grad = g_ref[0]
    pair = jnp.concatenate([grad, gn_ref[0]], 0)
    even = columns(lambda k, y: planes_ref[0, 0, k, y])
    here = lax.dot_general(weights(1), even, NT, preferred_element_type=F32)
    back_even = jnp.dot(grad, even, preferred_element_type=F32)
    odd = columns(lambda k, y: planes_ref[0, 1, k, y])
    both = lax.dot_general(
        jnp.concatenate([weights(2), weights(0)], 0), odd, NT, preferred_element_type=F32
    )
    back_odd = jnp.dot(pair, odd, preferred_element_type=F32)
    own_ref[0] = here + both[:32]
    send_ref[0] = both[32:]
    for t in range(9):
        lanes = slice(t * 128, (t + 1) * 128)
        total[t * 32:(t + 1) * 32] += back_odd[32:, lanes]
        total[(9 + t) * 32:(10 + t) * 32] += back_even[:, lanes]
        total[(18 + t) * 32:(19 + t) * 32] += back_odd[:32, lanes]

    @pl.when(step == B - 1)
    def _():
        core = lax.rem(lax.axis_index("space"), 2)
        keep_ref[...] = total[pl.ds(pl.multiple_of(core * HELD, 8), HELD)]
        go_ref[...] = total[pl.ds(pl.multiple_of((1 - core) * HELD, 8), HELD)]


def conv_local(planes, ker, g, gn):
    return pl.pallas_call(
        conv_kernel,
        grid=(B,),
        in_specs=[
            per_sample(2, 3, EDGE + 1, HALF, CIN), whole_array(27, 32, CIN),
            per_sample(32, 256), per_sample(32, 256),
        ],
        out_specs=[
            per_sample(32, 256), per_sample(32, 256), whole_array(HELD, CIN), whole_array(HELD, CIN)
        ],
        out_shape=[
            jax.ShapeDtypeStruct((B, 32, 256), F32),
            jax.ShapeDtypeStruct((B, 32, 256), F32),
            jax.ShapeDtypeStruct((HELD, CIN), F32),
            jax.ShapeDtypeStruct((HELD, CIN), F32),
        ],
        scratch_shapes=[pltpu.VMEM((2 * HELD, CIN), F32)],
        compiler_params=pltpu.CompilerParams(vmem_limit_bytes=FULL),
        cost_estimate=pl.CostEstimate(flops=4_000_000_000, bytes_accessed=5_000_000, transcendentals=0),
        name="conv_local",
    )(planes, ker, g, gn)


def input_grad_kernel(mine_ref, other_ref, out_ref, halves, grads, mixed, paired):
    core = lax.rem(lax.axis_index("space"), 2)
    halves[core] = mine_ref[:, :TAPS]
    halves[1 - core] = other_ref[:, :TAPS]
    last = (iota((128, 256), 0) & 15) == 15
    for p in range(2):
        for two in range(B // 2):
            block = mine_ref[:, TAPS + 2 * p + two].reshape(256, 128).astype(F32)
            turned = jnp.transpose(block)
            later = jnp.where(last, 0.0, pltpu.roll(turned, 127, 0))
            for shift, value in enumerate((turned, later)):
                low = value.astype(BF16)
                for b in range(2):
                    for q in range(3):
                        start = b * 64 + q * 16
                        grads[p, shift, q, 2 * two + b] = low[start:start + 16]

    def lhs(p, qs, rs):
        rows = [grads[p, rs, qs + q, b] for q in range(2) for b in range(B)]
        return jnp.concatenate(rows, 0)

    def tap(i, j, k):
        t = i * 9 + j * 3 + k
        half, place = (0, t) if t < TAPS else (1, t - 13)
        return halves[half, :, place].reshape(256, CIN)

    choices = (((1, 0),), ((2, 0), (0, 1)))
    for py in range(2):
        for pz in range(2):
            total = jnp.zeros((128, 256), F32)
            extra = jnp.zeros((128, 128), F32)
            for j, qs in choices[py]:
                for k, rs in choices[pz]:
                    two = jnp.concatenate([tap(1, j, k), tap(2, j, k)], 1)
                    total += jnp.dot(lhs(0, qs, rs), two, preferred_element_type=F32)
                    extra += jnp.dot(lhs(1, qs, rs), tap(0, j, k), preferred_element_type=F32)
            values = (total[:, :128], total[:, 128:] + extra)
            for px in range(2):
                for q in range(2):
                    for b in range(B):
                        start = (q * B + b) * 16
                        mixed[px, b, pl.ds((2 * q + py) * 32 + pz, 16, stride=2), :] = (
                            values[px][start:start + 16]
                        )
    for b in range(B):
        for px in range(2):
            paired[b, pl.ds(px, CIN, stride=2), :] = jnp.transpose(mixed[px, b])
        out_ref[b] = paired[b].astype(BF16)


def input_grad_local(mine, other):
    return pl.pallas_call(
        input_grad_kernel,
        out_shape=jax.ShapeDtypeStruct((B, 2 * CIN, 128), BF16),
        scratch_shapes=[
            pltpu.VMEM((2, 8, TAPS, 32, CIN), BF16),
            pltpu.VMEM((2, 2, 3, B, HALF, 256), BF16),
            pltpu.VMEM((2, B, 128, CIN), F32),
            pltpu.VMEM((B, 2 * CIN, 128), F32),
        ],
        compiler_params=pltpu.CompilerParams(vmem_limit_bytes=24 * 1024 * 1024),
        cost_estimate=pl.CostEstimate(flops=2_000_000_000, bytes_accessed=3_000_000, transcendentals=0),
        name="input_grad_local",
    )(mine, other)


SMALL = pltpu.CompilerParams(vmem_limit_bytes=4 * 1024 * 1024)


def place_kernel(mine_ref, theirs_ref, out_ref):
    core = lax.rem(lax.axis_index("space"), 2)
    out_ref[pl.ds(pl.multiple_of(core * HELD, 8), HELD)] = mine_ref[...]
    out_ref[pl.ds(pl.multiple_of((1 - core) * HELD, 8), HELD)] = theirs_ref[...]


def place(mine, theirs):
    return pl.pallas_call(
        place_kernel,
        out_shape=jax.ShapeDtypeStruct((2 * HELD, CIN), F32),
        compiler_params=SMALL,
        name="place",
    )(mine, theirs)


def swap(values, axis):
    return lax.all_to_all(values, axis, split_axis=0, concat_axis=0, tiled=True)


def body(volume, kernel, out_grad):
    spaces = lax.axis_size("space")
    g = out_grad.reshape(B, 32, 256)
    ker = kernel.reshape(27, 32, CIN)
    to_previous = [(i + 1, i) for i in range(spaces - 1)]
    to_next = [(i, i + 1) for i in range(spaces - 1)]
    g_next = lax.ppermute(g, "space", to_previous)
    vol = volume.reshape(B, CIN, 2, 8, 128).transpose(0, 1, 3, 2, 4).reshape(B, 2048, 128)
    planes, packed = prepare(vol, ker, g)
    mine = swap(next_cells(g_next, packed), "filt")
    own, send, keep, go = conv_local(planes, ker, g, g_next)

    def exchange(values, bits):
        return lax.ppermute(values, "space", [(i, i ^ bits) for i in range(spaces)])

    came = lax.ppermute(send, "space", to_next)
    pair = (keep + exchange(go, 1)).astype(BF16)
    near, far, farther = (exchange(pair, bits).astype(F32) for bits in (2, 4, 6))
    row = ((pair.astype(F32) + near) + (far + farther)).astype(BF16)
    row, mine = lax.optimization_barrier((row, mine))
    other = exchange(mine, 1)
    across = exchange(row, 8)
    input_grad = input_grad_local(mine, other).reshape(B, CIN, 2, 128)
    across, input_grad = lax.optimization_barrier((across, input_grad))
    held = row.astype(F32) + across.astype(F32)
    kernel_grad = place(held, exchange(held, 1)).reshape(3, 3, 3, 32, CIN)
    output = (own + came).astype(BF16).reshape(B, 32, 1, 256)
    return (output, input_grad, kernel_grad)


def solution(mesh):
    return jax.shard_map(
        body,
        mesh=mesh,
        in_specs=(
            P(None, None, "space", None),
            P(None, None, None, "filt", None),
            P(None, "filt", "space", None),
        ),
        out_specs=(
            P(None, "filt", "space", None),
            P(None, None, "space", "filt"),
            P(None, None, None, "filt", None),
        ),
        check_vma=False,
    )
```

time: 62.4 us -> 49.7 us (0.80)
  the two profiles are of different devices: /device:TPU:1 before, /device:TPU:27 now
where the time goes in v5:
time: 49.7 us; the launch traced here: 49.3 us
  starting transfers between devices  19 us (38%)
  Pallas kernels  14.6 us (29%)
  waiting for transfers between devices  12.6 us (25%)
  other arithmetic  1.69 us (3%)
  between operations  0.75 us (2%)
  local copies, waits for them, and re-layouts  0.63 us (1%)
    ppermute x7, waiting for transfers between devices, exchange(): return lax.ppermute(values, 'space', [(i, i ^ bits) for i in range(spaces)])  10.9 us
    ppermute x1, starting transfers between devices, body(): came = lax.ppermute(send, 'space', to_next)  5.88 us
    all_to_all x1, starting transfers between devices, swap(): return lax.all_to_all(values, axis, split_axis=0, concat_axis=0, tiled=True)  5.64 us
    pallas_call x1, Pallas kernels, conv_local(): pl.pallas_call(conv_kernel, grid=(B,), in_specs=[per_sample(2, 3, EDGE +...  5.25 us
    pallas_call x1, Pallas kernels, prepare(): pl.pallas_call(prepare_kernel, grid=(B,), in_specs=[pl.BlockSpec(memory_s...  5.13 us
    ppermute x7, starting transfers between devices, exchange(): return lax.ppermute(values, 'space', [(i, i ^ bits) for i in range(spaces)])  4.93 us
    ppermute x1, starting transfers between devices, body(): g_next = lax.ppermute(g, 'space', to_previous)  2.59 us
    pallas_call x1, Pallas kernels, input_grad_local(): pl.pallas_call(input_grad_kernel, out_shape=jax.ShapeDtypeStruct((B, 2 *...  1.75 us
  transfers between devices with their start and end apart: 10, of which 6 were waited for; matrix products, arithmetic and copies ran while one was open for 3% of the time, Pallas kernels for 25%

profile of v5, /device:TPU:27, one launch (start us, length us, event | category | flops | bytes accessed | tf_op | source)
XLA Modules:
  0.0 49.3 jit_solution(7059056525739639306)
XLA Ops:
  0.6 2.6 %collective-permute-start = (bf16[4,32,256]{2,1,0:T(8,128)(2,1)}, bf16[4,32,256]{2,1,0:T(8,128)(2,1)S(1)}, u32[]{:S(2)}, u32[]{:S(2)}) collective-permute-start(bf16[4,32,256]{2,1,0:T(8,128)(2,1)} %bitcast.17), channel_id=1, source_target_pairs={{8,0},{16,8},{24,16},{32,24},{40,32},{48,40},{56,48},{64,56},{72,6... | collective-permute-start | bytes 196616 | tf_op jit(solution)/shard_map/ppermute | solution.py:318
  3.2 5.1 %prepare.1 = (bf16[4,2,3,33,16,128]{5,4,3,2,1,0:T(8,128)(2,1)}, bf16[8,18,32,128]{3,2,1,0:T(8,128)(2,1)}) custom-call(bf16[4,2048,128]{2,1,0:T(8,128)(2,1)} %bitcast.14, bf16[27,32,128]{2,1,0:T(8,128)(2,1)} %bitcast.15, bf16[4,32,256]{2,1,0:T(8,128)(2,1)} %bitcast.18), custom_call_target="tpu_custom_call" | custom-call | flops 4000000000 | bytes 5000000 | tf_op jit(solution)/shard_map/prepare/pallas_call | solution.py:110
  8.4 1.7 %collective-permute-done.gn_ref = bf16[4,32,256]{2,1,0:T(8,128)(2,1)S(1)} collective-permute-done((bf16[4,32,256]{2,1,0:T(8,128)(2,1)}, bf16[4,32,256]{2,1,0:T(8,128)(2,1)S(1)}, u32[]{:S(2)}, u32[]{:S(2)}) %collective-permute-start) | collective-permute-done | bytes 65568 | tf_op jit(solution)/shard_map/ppermute | solution.py:318
  10.0 0.6 %copy-done.1 = bf16[4,32,256]{2,1,0:T(8,128)(2,1)} copy-done((bf16[4,32,256]{2,1,0:T(8,128)(2,1)}, bf16[4,32,256]{2,1,0:T(8,128)(2,1)S(1)}, u32[]{:S(2)}) %copy-start.1) | copy-done | bytes 65560
  10.7 1.7 %next_cells.1 = bf16[8,18,32,128]{3,2,1,0:T(8,128)(2,1)} custom-call(bf16[4,32,256]{2,1,0:T(8,128)(2,1)} %copy-done.1, bf16[8,18,32,128]{3,2,1,0:T(8,128)(2,1)} %get-tuple-element.18._), custom_call_target="tpu_custom_call", output_to_operand_aliasing={{}: (1, {})} | custom-call | tf_op jit(solution)/shard_map/next_cells/pallas_call | solution.py:144
  12.3 5.6 %all-to-all-start = ((bf16[8,18,32,128]{3,2,1,0:T(8,128)(2,1)}), bf16[8,18,32,128]{3,2,1,0:T(8,128)(2,1)S(1)}, u32[]{:S(2)}, u32[]{:S(2)}) async-start(bf16[8,18,32,128]{3,2,1,0:T(8,128)(2,1)} %next_cells.1), calls=%async_computation | async-start | bytes 2359296 | tf_op jit(solution)/shard_map/all_to_all | solution.py:309
  18.0 5.2 %conv_local.1 = (f32[4,32,256]{2,1,0:T(8,128)}, f32[4,32,256]{2,1,0:T(8,128)}, f32[432,128]{1,0:T(8,128)}, f32[432,128]{1,0:T(8,128)}) custom-call(bf16[4,2,3,33,16,128]{5,4,3,2,1,0:T(8,128)(2,1)} %get-tuple-element.13.planes_ref, bf16[27,32,128]{2,1,0:T(8,128)(2,1)} %bitcast.16, bf16[4,32,256]{2,1,0:T(8,128)(2,1)} %bitcast.19, bf16[4,32,256]{2,1,0:T(8,128)(2,1)} %copy-done.1), custom_call_target="tpu_custom_call" | custom-call | flops 4000000000 | bytes 5000000 | tf_op jit(solution)/shard_map/conv_local/pallas_call | solution.py:201
  23.2 0.1 collective-permute-start.2
  23.3 1.7 %collective-permute-done.2 = f32[432,128]{1,0:T(8,128)S(1)} collective-permute-done((f32[432,128]{1,0:T(8,128)}, f32[432,128]{1,0:T(8,128)S(1)}, u32[]{:S(2)}, u32[]{:S(2)}) %collective-permute-start.2) | collective-permute-done | bytes 221216 | tf_op jit(solution)/shard_map/ppermute | solution.py:325
  25.0 1.0 %add_convert_fusion.1 = bf16[432,128]{1,0:T(8,128)(2,1)S(1)} fusion(f32[432,128]{1,0:T(8,128)} %get-tuple-element.16, f32[432,128]{1,0:T(8,128)S(1)} %collective-permute-done.2), kind=kLoop, calls=%fused_computation.2 | loop fusion | flops 110592 | bytes 552960 | tf_op jit(solution)/shard_map/convert_element_type | solution.py:328
  26.0 0.1 collective-permute-start.5
  26.1 0.8 %collective-permute-start.4 = (bf16[432,128]{1,0:T(8,128)(2,1)S(1)}, bf16[432,128]{1,0:T(8,128)(2,1)S(1)}, u32[]{:S(2)}, u32[]{:S(2)}) collective-permute-start(bf16[432,128]{1,0:T(8,128)(2,1)S(1)} %add_convert_fusion.1), channel_id=1, source_target_pairs={{0,32},{8,40},{16,48},{24,56},{32,0},{40,8},{48,16},{56,24},{64,96... | collective-permute-start | bytes 331784 | tf_op jit(solution)/shard_map/ppermute | solution.py:325
  26.8 2.5 %collective-permute-start.3 = (bf16[432,128]{1,0:T(8,128)(2,1)S(1)}, bf16[432,128]{1,0:T(8,128)(2,1)S(1)}, u32[]{:S(2)}, u32[]{:S(2)}) collective-permute-start(bf16[432,128]{1,0:T(8,128)(2,1)S(1)} %add_convert_fusion.1), channel_id=1, source_target_pairs={{0,16},{8,24},{16,0},{24,8},{32,48},{40,56},{48,32},{56,40},{64,80... | collective-permute-start | bytes 331784 | tf_op jit(solution)/shard_map/ppermute | solution.py:325
  29.3 5.0 %collective-permute-done.5 = bf16[432,128]{1,0:T(8,128)(2,1)S(1)} collective-permute-done((bf16[432,128]{1,0:T(8,128)(2,1)S(1)}, bf16[432,128]{1,0:T(8,128)(2,1)S(1)}, u32[]{:S(2)}, u32[]{:S(2)}) %collective-permute-start.5) | collective-permute-done | bytes 110624 | tf_op jit(solution)/shard_map/ppermute | solution.py:325
  34.3 0.1 collective-permute-done.3
  34.5 1.4 %collective-permute-start.7 = (bf16[8,18,32,128]{3,2,1,0:T(8,128)(2,1)S(1)}, bf16[8,18,32,128]{3,2,1,0:T(8,128)(2,1)S(1)}, u32[]{:S(2)}, u32[]{:S(2)}) collective-permute-start(bf16[8,18,32,128]{3,2,1,0:T(8,128)(2,1)S(1)} %all-to-all-done.mine_ref), channel_id=1, source_target_pairs={{0,8},{8,0},{16,24},{24,16},{32,40},{40,32},{48,56},{56,48},{64,72... | collective-permute-start | bytes 3538952 | tf_op jit(solution)/shard_map/ppermute | solution.py:325
  35.8 5.9 %collective-permute-start.1 = (f32[4,32,256]{2,1,0:T(8,128)}, f32[4,32,256]{2,1,0:T(8,128)S(1)}, u32[]{:S(2)}, u32[]{:S(2)}) collective-permute-start(f32[4,32,256]{2,1,0:T(8,128)} %get-tuple-element.15), channel_id=1, source_target_pairs={{0,8},{8,16},{16,24},{24,32},{32,40},{40,48},{48,56},{56,64},{64,7... | collective-permute-start | bytes 393224 | tf_op jit(solution)/shard_map/ppermute | solution.py:327
  41.7 0.1 collective-permute-start.6
  41.8 1.8 %input_grad_local.1 = bf16[4,256,128]{2,1,0:T(8,128)(2,1)} custom-call(bf16[8,18,32,128]{3,2,1,0:T(8,128)(2,1)S(1)} %all-to-all-done.mine_ref, bf16[8,18,32,128]{3,2,1,0:T(8,128)(2,1)S(1)} %collective-permute-done.7.other_ref), custom_call_target="tpu_custom_call" | custom-call | flops 2000000000 | bytes 3000000 | tf_op jit(solution)/shard_map/input_grad_local/pallas_call | solution.py:275
  43.6 3.3 %collective-permute-done.6 = bf16[432,128]{1,0:T(8,128)(2,1)S(1)} collective-permute-done((bf16[432,128]{1,0:T(8,128)(2,1)S(1)}, bf16[432,128]{1,0:T(8,128)(2,1)S(1)}, u32[]{:S(2)}, u32[]{:S(2)}) %collective-permute-start.6) | collective-permute-done | bytes 110624 | tf_op jit(solution)/shard_map/ppermute | solution.py:325
  46.9 0.1 collective-permute-start.8
  47.0 0.6 %fusion = bf16[4,32,1,256]{3,1,2,0:T(8,128)(2,1)} fusion(f32[4,32,256]{2,1,0:T(8,128)S(1)} %copy-done, f32[4,32,256]{2,1,0:T(8,128)S(1)} %collective-permute-done.1), kind=kLoop, calls=%fused_computation.4 | loop fusion | flops 65536 | bytes 327680
  47.7 0.8 %collective-permute-done.8.theirs_ref = f32[432,128]{1,0:T(8,128)S(1)} collective-permute-done((f32[432,128]{1,0:T(8,128)S(1)}, f32[432,128]{1,0:T(8,128)S(1)}, u32[]{:S(2)}, u32[]{:S(2)}) %collective-permute-start.8) | collective-permute-done | bytes 221216 | tf_op jit(solution)/shard_map/ppermute | solution.py:325
  48.5 0.8 %place.1 = f32[864,128]{1,0:T(8,128)} custom-call(f32[432,128]{1,0:T(8,128)S(1)} %convert_add_fusion.mine_ref, f32[432,128]{1,0:T(8,128)S(1)} %collective-permute-done.8.theirs_ref), custom_call_target="tpu_custom_call" | custom-call | tf_op jit(solution)/shard_map/place/pallas_call | solution.py:300
  (9 shorter events, 0.1 us)
Async XLA Ops:
  0.6 9.4 %collective-permute-start = (bf16[4,32,256]{2,1,0:T(8,128)(2,1)}, bf16[4,32,256]{2,1,0:T(8,128)(2,1)S(1)}, u32[]{:S(2)}, u32[]{:S(2)}) collective-permute-start(bf16[4,32,256]{2,1,0:T(8,128)(2,1)} %bitcast.17), channel_id=1, source_target_pairs={{8,0},{16,8},{24,16},{32,24},{40,32},{48,40},{56,48},{64,56},{72,6... | collective-permute-start | bytes 196616 | tf_op jit(solution)/shard_map/ppermute | solution.py:318
  10.0 0.6 %copy-start.1 = (bf16[4,32,256]{2,1,0:T(8,128)(2,1)}, bf16[4,32,256]{2,1,0:T(8,128)(2,1)S(1)}, u32[]{:S(2)}) copy-start(bf16[4,32,256]{2,1,0:T(8,128)(2,1)S(1)} %collective-permute-done.gn_ref) | copy-start | bytes 196612
  12.3 22.1 %all-to-all-start = ((bf16[8,18,32,128]{3,2,1,0:T(8,128)(2,1)}), bf16[8,18,32,128]{3,2,1,0:T(8,128)(2,1)S(1)}, u32[]{:S(2)}, u32[]{:S(2)}) async-start(bf16[8,18,32,128]{3,2,1,0:T(8,128)(2,1)} %next_cells.1), calls=%async_computation | async-start | bytes 2359296 | tf_op jit(solution)/shard_map/all_to_all | solution.py:309
  23.2 1.8 %collective-permute-start.2 = (f32[432,128]{1,0:T(8,128)}, f32[432,128]{1,0:T(8,128)S(1)}, u32[]{:S(2)}, u32[]{:S(2)}) collective-permute-start(f32[432,128]{1,0:T(8,128)} %get-tuple-element.17), channel_id=1, source_target_pairs={{0,8},{8,0},{16,24},{24,16},{32,40},{40,32},{48,56},{56,48},{64,72... | collective-permute-start | bytes 663560 | tf_op jit(solution)/shard_map/ppermute | solution.py:325
  26.0 8.3 %collective-permute-start.5 = (bf16[432,128]{1,0:T(8,128)(2,1)S(1)}, bf16[432,128]{1,0:T(8,128)(2,1)S(1)}, u32[]{:S(2)}, u32[]{:S(2)}) collective-permute-start(bf16[432,128]{1,0:T(8,128)(2,1)S(1)} %add_convert_fusion.1), channel_id=1, source_target_pairs={{0,48},{8,56},{16,32},{24,40},{32,16},{40,24},{48,0},{56,8},{64,11... | collective-permute-start | bytes 331784 | tf_op jit(solution)/shard_map/ppermute | solution.py:325
  26.1 8.2 %collective-permute-start.4 = (bf16[432,128]{1,0:T(8,128)(2,1)S(1)}, bf16[432,128]{1,0:T(8,128)(2,1)S(1)}, u32[]{:S(2)}, u32[]{:S(2)}) collective-permute-start(bf16[432,128]{1,0:T(8,128)(2,1)S(1)} %add_convert_fusion.1), channel_id=1, source_target_pairs={{0,32},{8,40},{16,48},{24,56},{32,0},{40,8},{48,16},{56,24},{64,96... | collective-permute-start | bytes 331784 | tf_op jit(solution)/shard_map/ppermute | solution.py:325
  26.8 7.6 %collective-permute-start.3 = (bf16[432,128]{1,0:T(8,128)(2,1)S(1)}, bf16[432,128]{1,0:T(8,128)(2,1)S(1)}, u32[]{:S(2)}, u32[]{:S(2)}) collective-permute-start(bf16[432,128]{1,0:T(8,128)(2,1)S(1)} %add_convert_fusion.1), channel_id=1, source_target_pairs={{0,16},{8,24},{16,0},{24,8},{32,48},{40,56},{48,32},{56,40},{64,80... | collective-permute-start | bytes 331784 | tf_op jit(solution)/shard_map/ppermute | solution.py:325
  34.5 7.3 %collective-permute-start.7 = (bf16[8,18,32,128]{3,2,1,0:T(8,128)(2,1)S(1)}, bf16[8,18,32,128]{3,2,1,0:T(8,128)(2,1)S(1)}, u32[]{:S(2)}, u32[]{:S(2)}) collective-permute-start(bf16[8,18,32,128]{3,2,1,0:T(8,128)(2,1)S(1)} %all-to-all-done.mine_ref), channel_id=1, source_target_pairs={{0,8},{8,0},{16,24},{24,16},{32,40},{40,32},{48,56},{56,48},{64,72... | collective-permute-start | bytes 3538952 | tf_op jit(solution)/shard_map/ppermute | solution.py:325
  35.8 11.2 %copy-start = (f32[4,32,256]{2,1,0:T(8,128)S(1)}, f32[4,32,256]{2,1,0:T(8,128)}, u32[]{:S(2)}) copy-start(f32[4,32,256]{2,1,0:T(8,128)} %get-tuple-element.14) | copy-start | bytes 393220
  35.8 11.2 %collective-permute-start.1 = (f32[4,32,256]{2,1,0:T(8,128)}, f32[4,32,256]{2,1,0:T(8,128)S(1)}, u32[]{:S(2)}, u32[]{:S(2)}) collective-permute-start(f32[4,32,256]{2,1,0:T(8,128)} %get-tuple-element.15), channel_id=1, source_target_pairs={{0,8},{8,16},{16,24},{24,32},{32,40},{40,48},{48,56},{56,64},{64,7... | collective-permute-start | bytes 393224 | tf_op jit(solution)/shard_map/ppermute | solution.py:327
  41.7 5.2 %collective-permute-start.6 = (bf16[432,128]{1,0:T(8,128)(2,1)S(1)}, bf16[432,128]{1,0:T(8,128)(2,1)S(1)}, u32[]{:S(2)}, u32[]{:S(2)}) collective-permute-start(bf16[432,128]{1,0:T(8,128)(2,1)S(1)} %add_convert_fusion), channel_id=1, source_target_pairs={{0,64},{8,72},{16,80},{24,88},{32,96},{40,104},{48,112},{56,120},{... | collective-permute-start | bytes 331784 | tf_op jit(solution)/shard_map/ppermute | solution.py:325
  46.9 1.6 %collective-permute-start.8 = (f32[432,128]{1,0:T(8,128)S(1)}, f32[432,128]{1,0:T(8,128)S(1)}, u32[]{:S(2)}, u32[]{:S(2)}) collective-permute-start(f32[432,128]{1,0:T(8,128)S(1)} %convert_add_fusion.mine_ref), channel_id=1, source_target_pairs={{0,8},{8,0},{16,24},{24,16},{32,40},{40,32},{48,56},{56,48},{64,72... | collective-permute-start | bytes 663560 | tf_op jit(solution)/shard_map/ppermute | solution.py:325

commit v6 on v5

--- a/solution.py
+++ b/solution.py
@@ -31,87 +31,72 @@
 
 
 def prepare_kernel(vol_ref, ker_ref, g_ref, planes_ref, packed_ref,
-                   raw, arrived, taps, grad, cells, sent, perm, select, cols):
-    step = pl.program_id(0)
+                   raw, arrived, taps, grad, cells, sent, perm, select, cols, planes):
     core = lax.rem(lax.axis_index("space"), 2)
-
-    def fetch(b):
-        return pltpu.make_async_copy(vol_ref.at[b], raw.at[b], arrived.at[b])
-
+    fetches = [pltpu.make_async_copy(vol_ref.at[b], raw.at[b], arrived.at[b]) for b in range(B)]
     fetch_taps = pltpu.make_async_copy(ker_ref.at[pl.ds(core * 13, TAPS)], taps, arrived.at[B])
     fetch_grad = pltpu.make_async_copy(g_ref, grad, arrived.at[B + 1])
     copies = [
         pltpu.make_async_copy(taps, packed_ref.at[f, pl.ds(0, TAPS)], sent.at[f]) for f in range(8)
     ]
     copies.append(pltpu.make_async_copy(cells, packed_ref.at[:, pl.ds(TAPS, 2)], sent.at[8]))
-
-    @pl.when(step == 0)
-    def _():
-        fetch(0).start()
-        fetch_taps.start()
-        fetch_grad.start()
-        for b in range(1, B):
-            fetch(b).start()
-        row, col = iota((256, 256), 0), iota((256, 256), 1)
-        source = (row & 15) * 16 + ((row >> 4) & 7) * 2 + (row >> 7)
-        perm[...] = jnp.where(col == source, 1.0, 0.0).astype(BF16)
-        row, col = iota((192, 128), 0), iota((192, 128), 1)
-        depth = (row & 15) * 2 + (row >> 6) - 1
-        wanted = (col == ((row >> 4) & 3) * 32 + depth) & (depth >= 0)
-        select[...] = jnp.where(wanted, 1.0, 0.0).astype(BF16)
-
-    @pl.when(step == 1)
-    def _():
-        fetch_taps.wait()
-        for copy in copies[:8]:
-            copy.start()
-        fetch_grad.wait()
-        cut_cells(grad, cells)
-        copies[8].start()
-
-    fetch(step).wait()
-    wide = jnp.concatenate([raw[step, g * 256:(g + 1) * 256] for g in range(8)], 1)
-    moved = jnp.dot(perm[...], wide, preferred_element_type=F32).astype(BF16)
-    for lt in range(8):
+    fetches[0].start()
+    fetch_taps.start()
+    fetch_grad.start()
+    for b in range(1, B):
+        fetches[b].start()
+    row, col = iota((256, 256), 0), iota((256, 256), 1)
+    source = (row & 15) * 16 + ((row >> 4) & 7) * 2 + (row >> 7)
+    perm[...] = jnp.where(col == source, 1.0, 0.0).astype(BF16)
+    row, col = iota((192, 128), 0), iota((192, 128), 1)
+    depth = (row & 15) * 2 + (row >> 6) - 1
+    wanted = (col == ((row >> 4) & 3) * 32 + depth) & (depth >= 0)
+    select[...] = jnp.where(wanted, 1.0, 0.0).astype(BF16)
+
+    for step in range(B):
+        fetches[step].wait()
+        wide = jnp.concatenate([raw[step, g * 256:(g + 1) * 256] for g in range(8)], 1)
+        moved = jnp.dot(perm[...], wide, preferred_element_type=F32).astype(BF16)
+        slot = step % 2
+        for lt in range(8):
+            for x in range(2):
+                start = (x * 8 + lt) * 16
+                for g in range(8):
+                    cols[slot, lt, x * 128 + g * 16:x * 128 + g * 16 + 16, :] = (
+                        moved[start:start + 16, g * 128:(g + 1) * 128]
+                    )
+        if step == 0:
+            fetch_taps.wait()
+            for copy in copies[:8]:
+                copy.start()
+            fetch_grad.wait()
+            cut_cells(grad, cells)
+            copies[8].start()
         for x in range(2):
-            start = (x * 8 + lt) * 16
-            for g in range(8):
-                cols[lt, x * 128 + g * 16:x * 128 + g * 16 + 16, :] = (
-                    moved[start:start + 16, g * 128:(g + 1) * 128]
-                )
-    for x in range(2):
-        for k in range(3):
-            planes_ref[0, x, k, 0] = jnp.zeros((HALF, CIN), BF16)
-    for lt in range(8):
-        turned = lax.dot_general(select[...], cols[lt], NT, preferred_element_type=F32).astype(BF16)
-        for k in range(3):
-            for y in range(4):
-                start = k * 64 + y * 16
-                for x in range(2):
-                    planes_ref[0, x, k, 1 + 4 * lt + y] = (
-                        turned[start:start + 16, x * 128:(x + 1) * 128]
-                    )
-
-    @pl.when(step == B - 1)
-    def _():
-        for copy in copies:
-            copy.wait()
-
-
-def per_sample(*shape):
-    return pl.BlockSpec((1,) + shape, lambda b: (b,) + (0,) * len(shape))
-
-
-def whole_array(*shape):
-    return pl.BlockSpec(shape, lambda b: (0,) * len(shape))
+            for k in range(3):
+                planes[step, x, k, 0] = jnp.zeros((HALF, CIN), BF16)
+        for lt in range(8):
+            turned = lax.dot_general(
+                select[...], cols[slot, lt], NT, preferred_element_type=F32
+            ).astype(BF16)
+            for k in range(3):
+                for y in range(4):
+                    start = k * 64 + y * 16
+                    for x in range(2):
+                        planes[step, x, k, 1 + 4 * lt + y] = (
+                            turned[start:start + 16, x * 128:(x + 1) * 128]
+                        )
+        copies.append(pltpu.make_async_copy(planes.at[step], planes_ref.at[step], sent.at[9 + step]))
+        copies[-1].start()
+    for copy in copies:
+        copy.wait()
 
 
 def prepare(vol, ker, g):
     return pl.pallas_call(
         prepare_kernel,
-        grid=(B,),
         in_specs=[pl.BlockSpec(memory_space=pltpu.HBM)] * 3,
-        out_specs=[per_sample(2, 3, EDGE + 1, HALF, CIN), pl.BlockSpec(memory_space=pltpu.HBM)],
+        out_specs=[pl.BlockSpec(memory_space=pltpu.HBM)] * 2,
         out_shape=[
             jax.ShapeDtypeStruct((B, 2, 3, EDGE + 1, HALF, CIN), BF16),
             jax.ShapeDtypeStruct((8, PACKED, 32, 128), BF16),
@@ -122,10 +107,11 @@
             pltpu.VMEM((TAPS, 32, CIN), BF16),
             pltpu.VMEM((B, 32, 256), BF16),
             pltpu.VMEM((8, 2, 32, 128), BF16),
-            pltpu.SemaphoreType.DMA((9,)),
+            pltpu.SemaphoreType.DMA((9 + B,)),
             pltpu.VMEM((256, 256), BF16),
             pltpu.VMEM((192, 128), BF16),
-            pltpu.VMEM((8, 256, 128), BF16),
+            pltpu.VMEM((2, 8, 256, 128), BF16),
+            pltpu.VMEM((B, 2, 3, EDGE + 1, HALF, CIN), BF16),
         ],
         compiler_params=pltpu.CompilerParams(vmem_limit_bytes=FULL),
         cost_estimate=pl.CostEstimate(flops=4_000_000_000, bytes_accessed=5_000_000, transcendentals=0),
@@ -162,59 +148,80 @@
 
 
 def conv_kernel(planes_ref, ker_ref, g_ref, gn_ref, own_ref, send_ref, keep_ref, go_ref,
-                total):
-    step = pl.program_id(0)
-
-    @pl.when(step == 0)
-    def _():
-        total[...] = jnp.zeros_like(total)
+                planes, ker, grads, own, send, total, arrived, sent):
+    fetch_planes = [
+        pltpu.make_async_copy(planes_ref.at[b], planes.at[b], arrived.at[b]) for b in range(B)
+    ]
+    others = [
+        pltpu.make_async_copy(ker_ref, ker, arrived.at[B]),
+        pltpu.make_async_copy(g_ref, grads.at[0], arrived.at[B + 1]),
+        pltpu.make_async_copy(gn_ref, grads.at[1], arrived.at[B + 2]),
+    ]
+    fetch_planes[0].start()
+    for copy in others + fetch_planes[1:]:
+        copy.start()
 
     def weights(i):
-        return jnp.concatenate([ker_ref[i * 9 + t] for t in range(9)], 1)
-
-    grad = g_ref[0]
-    pair = jnp.concatenate([grad, gn_ref[0]], 0)
-    even = columns(lambda k, y: planes_ref[0, 0, k, y])
-    here = lax.dot_general(weights(1), even, NT, preferred_element_type=F32)
-    back_even = jnp.dot(grad, even, preferred_element_type=F32)
-    odd = columns(lambda k, y: planes_ref[0, 1, k, y])
-    both = lax.dot_general(
-        jnp.concatenate([weights(2), weights(0)], 0), odd, NT, preferred_element_type=F32
-    )
-    back_odd = jnp.dot(pair, odd, preferred_element_type=F32)
-    own_ref[0] = here + both[:32]
-    send_ref[0] = both[32:]
-    for t in range(9):
-        lanes = slice(t * 128, (t + 1) * 128)
-        total[t * 32:(t + 1) * 32] += back_odd[32:, lanes]
-        total[(9 + t) * 32:(10 + t) * 32] += back_even[:, lanes]
-        total[(18 + t) * 32:(19 + t) * 32] += back_odd[:32, lanes]
-
-    @pl.when(step == B - 1)
-    def _():
-        core = lax.rem(lax.axis_index("space"), 2)
-        keep_ref[...] = total[pl.ds(pl.multiple_of(core * HELD, 8), HELD)]
-        go_ref[...] = total[pl.ds(pl.multiple_of((1 - core) * HELD, 8), HELD)]
+        return jnp.concatenate([ker[i * 9 + t] for t in range(9)], 1)
+
+    for copy in others:
+        copy.wait()
+    for step in range(B):
+        fetch_planes[step].wait()
+        grad = grads[0, step]
+        pair = jnp.concatenate([grad, grads[1, step]], 0)
+        even = columns(lambda k, y: planes[step, 0, k, y])
+        here = lax.dot_general(weights(1), even, NT, preferred_element_type=F32)
+        back_even = jnp.dot(grad, even, preferred_element_type=F32)
+        odd = columns(lambda k, y: planes[step, 1, k, y])
+        both = lax.dot_general(
+            jnp.concatenate([weights(2), weights(0)], 0), odd, NT, preferred_element_type=F32
+        )
+        back_odd = jnp.dot(pair, odd, preferred_element_type=F32)
+        own[step] = here + both[:32]
+        send[step] = both[32:]
+        for t in range(9):
+            lanes = slice(t * 128, (t + 1) * 128)
+            for first, value in (
+                (t, back_odd[32:, lanes]), (9 + t, back_even[:, lanes]), (18 + t, back_odd[:32, lanes])
+            ):
+                rows = slice(first * 32, first * 32 + 32)
+                total[rows] = value if step == 0 else total[rows] + value
+    core = lax.rem(lax.axis_index("space"), 2)
+    halves = [
+        total.at[pl.ds(pl.multiple_of(half * HELD, 8), HELD)] for half in (core, 1 - core)
+    ]
+    copies = [
+        pltpu.make_async_copy(source, target, sent.at[i])
+        for i, (source, target) in enumerate(zip([*halves, own, send], [keep_ref, go_ref, own_ref, send_ref]))
+    ]
+    for copy in copies:
+        copy.start()
+    for copy in copies:
+        copy.wait()
 
 
 def conv_local(planes, ker, g, gn):
     return pl.pallas_call(
         conv_kernel,
-        grid=(B,),
-        in_specs=[
-            per_sample(2, 3, EDGE + 1, HALF, CIN), whole_array(27, 32, CIN),
-            per_sample(32, 256), per_sample(32, 256),
-        ],
-        out_specs=[
-            per_sample(32, 256), per_sample(32, 256), whole_array(HELD, CIN), whole_array(HELD, CIN)
-        ],
+        in_specs=[pl.BlockSpec(memory_space=pltpu.HBM)] * 4,
+        out_specs=[pl.BlockSpec(memory_space=pltpu.HBM)] * 4,
         out_shape=[
             jax.ShapeDtypeStruct((B, 32, 256), F32),
             jax.ShapeDtypeStruct((B, 32, 256), F32),
             jax.ShapeDtypeStruct((HELD, CIN), F32),
             jax.ShapeDtypeStruct((HELD, CIN), F32),
         ],
-        scratch_shapes=[pltpu.VMEM((2 * HELD, CIN), F32)],
+        scratch_shapes=[
+            pltpu.VMEM((B, 2, 3, EDGE + 1, HALF, CIN), BF16),
+            pltpu.VMEM((27, 32, CIN), BF16),
+            pltpu.VMEM((2, B, 32, 256), BF16),
+            pltpu.VMEM((B, 32, 256), F32),
+            pltpu.VMEM((B, 32, 256), F32),
+            pltpu.VMEM((2 * HELD, CIN), F32),
+            pltpu.SemaphoreType.DMA((B + 3,)),
+            pltpu.SemaphoreType.DMA((4,)),
+        ],
         compiler_params=pltpu.CompilerParams(vmem_limit_bytes=FULL),
         cost_estimate=pl.CostEstimate(flops=4_000_000_000, bytes_accessed=5_000_000, transcendentals=0),
         name="conv_local",
@@ -324,11 +331,16 @@
     def exchange(values, bits):
         return lax.ppermute(values, "space", [(i, i ^ bits) for i in range(spaces)])
 
-    came = lax.ppermute(send, "space", to_next)
+    turn = spaces // 2
+    relayed = lax.ppermute(send, "space", [(turn - 1, spaces - 1)])
     pair = (keep + exchange(go, 1)).astype(BF16)
-    near, far, farther = (exchange(pair, bits).astype(F32) for bits in (2, 4, 6))
+    near, far, farther = (exchange(pair, bits).astype(F32) for bits in (4, 6, 2))
     row = ((pair.astype(F32) + near) + (far + farther)).astype(BF16)
-    row, mine = lax.optimization_barrier((row, mine))
+    row, mine, relayed = lax.optimization_barrier((row, mine, relayed))
+    passed = jnp.where(lax.axis_index("space") == spaces - 1, relayed, send)
+    came = lax.ppermute(
+        passed, "space", [(i, i + 1) for i in range(spaces - 1) if i != turn - 1] + [(spaces - 1, turn)]
+    )
     other = exchange(mine, 1)
     across = exchange(row, 8)
     input_grad = input_grad_local(mine, other).reshape(B, CIN, 2, 128)

time: 49.7 us -> 46.5 us (0.936)
  the two profiles are of different devices: /device:TPU:27 before, /device:TPU:1 now
where the time goes in v6:
time: 46.5 us; the launch traced here: 46.2 us
  starting transfers between devices  21.9 us (47%)
  Pallas kernels  14.3 us (31%)
  waiting for transfers between devices  6.93 us (15%)
  other arithmetic  1.71 us (4%)
  between operations  0.77 us (2%)
  local copies, waits for them, and re-layouts  0.63 us (1%)
    ppermute x7, starting transfers between devices, exchange(): return lax.ppermute(values, 'space', [(i, i ^ bits) for i in range(spaces)])  10.4 us
    ppermute x7, waiting for transfers between devices, exchange(): return lax.ppermute(values, 'space', [(i, i ^ bits) for i in range(spaces)])  6.92 us
    all_to_all x1, starting transfers between devices, swap(): return lax.all_to_all(values, axis, split_axis=0, concat_axis=0, tiled=True)  5.46 us
    pallas_call x1, Pallas kernels, conv_local(): pl.pallas_call(conv_kernel, in_specs=[pl.BlockSpec(memory_space=pltpu.HBM...  5.36 us
    pallas_call x1, Pallas kernels, prepare(): pl.pallas_call(prepare_kernel, in_specs=[pl.BlockSpec(memory_space=pltpu....  4.7 us
    ppermute x1, starting transfers between devices, body(): g_next = lax.ppermute(g, 'space', to_previous)  3.33 us
    ppermute x1, starting transfers between devices, body(): lax.ppermute(passed, 'space', [(i, i + 1) for i in range(spaces - 1) if i...  2.05 us
    pallas_call x1, Pallas kernels, input_grad_local(): pl.pallas_call(input_grad_kernel, out_shape=jax.ShapeDtypeStruct((B, 2 *...  1.75 us
  transfers between devices with their start and end apart: 11, of which 4 were waited for; matrix products, arithmetic and copies ran while one was open for 4% of the time, Pallas kernels for 26%

profile of v6, /device:TPU:1, one launch (start us, length us, event | category | flops | bytes accessed | tf_op | source)
XLA Modules:
  0.0 46.2 jit_solution(6024215116252667182)
XLA Ops:
  0.6 3.3 %collective-permute-start = (bf16[4,32,256]{2,1,0:T(8,128)(2,1)}, bf16[4,32,256]{2,1,0:T(8,128)(2,1)S(1)}, u32[]{:S(2)}, u32[]{:S(2)}) collective-permute-start(bf16[4,32,256]{2,1,0:T(8,128)(2,1)} %bitcast.17), channel_id=1, source_target_pairs={{8,0},{16,8},{24,16},{32,24},{40,32},{48,40},{56,48},{64,56},{72,6... | collective-permute-start | bytes 196616 | tf_op jit(solution)/shard_map/ppermute | solution.py:325
  4.0 4.7 %prepare.1 = (bf16[4,2,3,33,16,128]{5,4,3,2,1,0:T(8,128)(2,1)}, bf16[8,18,32,128]{3,2,1,0:T(8,128)(2,1)}) custom-call(bf16[4,2048,128]{2,1,0:T(8,128)(2,1)} %bitcast.14, bf16[27,32,128]{2,1,0:T(8,128)(2,1)} %bitcast.15, bf16[4,32,256]{2,1,0:T(8,128)(2,1)} %bitcast.18), custom_call_target="tpu_custom_call" | custom-call | flops 4000000000 | bytes 5000000 | tf_op jit(solution)/shard_map/prepare/pallas_call | solution.py:96
  8.7 0.6 %copy-done.2 = bf16[4,32,256]{2,1,0:T(8,128)(2,1)} copy-done((bf16[4,32,256]{2,1,0:T(8,128)(2,1)}, bf16[4,32,256]{2,1,0:T(8,128)(2,1)S(1)}, u32[]{:S(2)}) %copy-start.2) | copy-done | bytes 65560
  9.3 1.7 %next_cells.1 = bf16[8,18,32,128]{3,2,1,0:T(8,128)(2,1)} custom-call(bf16[4,32,256]{2,1,0:T(8,128)(2,1)} %copy-done.2, bf16[8,18,32,128]{3,2,1,0:T(8,128)(2,1)} %get-tuple-element.18._), custom_call_target="tpu_custom_call", output_to_operand_aliasing={{}: (1, {})} | custom-call | tf_op jit(solution)/shard_map/next_cells/pallas_call | solution.py:130
  11.0 5.5 %all-to-all-start = ((bf16[8,18,32,128]{3,2,1,0:T(8,128)(2,1)}), bf16[8,18,32,128]{3,2,1,0:T(8,128)(2,1)S(1)}, u32[]{:S(2)}, u32[]{:S(2)}) async-start(bf16[8,18,32,128]{3,2,1,0:T(8,128)(2,1)} %next_cells.1), calls=%async_computation | async-start | bytes 2359296 | tf_op jit(solution)/shard_map/all_to_all | solution.py:316
  16.5 5.4 %conv_local.1 = (f32[4,32,256]{2,1,0:T(8,128)}, f32[4,32,256]{2,1,0:T(8,128)}, f32[432,128]{1,0:T(8,128)}, f32[432,128]{1,0:T(8,128)}) custom-call(bf16[4,2,3,33,16,128]{5,4,3,2,1,0:T(8,128)(2,1)} %get-tuple-element.14.planes_ref, bf16[27,32,128]{2,1,0:T(8,128)(2,1)} %bitcast.16, bf16[4,32,256]{2,1,0:T(8,128)(2,1)} %bitcast.19, bf16[4,32,256]{2,1,0:T(8,128)(2,1)} %copy-done.2), custom_call_target="tpu_custom_call" | custom-call | flops 4000000000 | bytes 5000000 | tf_op jit(solution)/shard_map/conv_local/pallas_call | solution.py:205
  21.8 0.1 collective-permute-start.1
  21.9 1.7 %collective-permute-done.1 = f32[432,128]{1,0:T(8,128)S(1)} collective-permute-done((f32[432,128]{1,0:T(8,128)}, f32[432,128]{1,0:T(8,128)S(1)}, u32[]{:S(2)}, u32[]{:S(2)}) %collective-permute-start.1) | collective-permute-done | bytes 221216 | tf_op jit(solution)/shard_map/ppermute | solution.py:332
  23.6 1.0 %add_convert_fusion.1 = bf16[432,128]{1,0:T(8,128)(2,1)S(1)} fusion(f32[432,128]{1,0:T(8,128)} %get-tuple-element.16, f32[432,128]{1,0:T(8,128)S(1)} %collective-permute-done.1), kind=kLoop, calls=%fused_computation.2 | loop fusion | flops 110592 | bytes 552960 | tf_op jit(solution)/shard_map/convert_element_type | solution.py:336
  24.6 3.0 %collective-permute-start.2 = (bf16[432,128]{1,0:T(8,128)(2,1)S(1)}, bf16[432,128]{1,0:T(8,128)(2,1)S(1)}, u32[]{:S(2)}, u32[]{:S(2)}) collective-permute-start(bf16[432,128]{1,0:T(8,128)(2,1)S(1)} %add_convert_fusion.1), channel_id=1, source_target_pairs={{0,32},{8,40},{16,48},{24,56},{32,0},{40,8},{48,16},{56,24},{64,96... | collective-permute-start | bytes 331784 | tf_op jit(solution)/shard_map/ppermute | solution.py:332
  27.6 2.0 %collective-permute-start.3 = (bf16[432,128]{1,0:T(8,128)(2,1)S(1)}, bf16[432,128]{1,0:T(8,128)(2,1)S(1)}, u32[]{:S(2)}, u32[]{:S(2)}) collective-permute-start(bf16[432,128]{1,0:T(8,128)(2,1)S(1)} %add_convert_fusion.1), channel_id=1, source_target_pairs={{0,48},{8,56},{16,32},{24,40},{32,16},{40,24},{48,0},{56,8},{64,11... | collective-permute-start | bytes 331784 | tf_op jit(solution)/shard_map/ppermute | solution.py:332
  29.6 0.5 %collective-permute-start.4 = (bf16[432,128]{1,0:T(8,128)(2,1)S(1)}, bf16[432,128]{1,0:T(8,128)(2,1)S(1)}, u32[]{:S(2)}, u32[]{:S(2)}) collective-permute-start(bf16[432,128]{1,0:T(8,128)(2,1)S(1)} %add_convert_fusion.1), channel_id=1, source_target_pairs={{0,16},{8,24},{16,0},{24,8},{32,48},{40,56},{48,32},{56,40},{64,80... | collective-permute-start | bytes 331784 | tf_op jit(solution)/shard_map/ppermute | solution.py:332
  30.1 0.7 %collective-permute-start.5 = (f32[4,32,256]{2,1,0:T(8,128)}, f32[4,32,256]{2,1,0:T(8,128)S(1)}, u32[]{:S(2)}, u32[]{:S(2)}) collective-permute-start(f32[4,32,256]{2,1,0:T(8,128)} %get-tuple-element.19), channel_id=1, source_target_pairs={{56,120},{57,121},{58,122},{59,123},{60,124},{61,125},{62,126},{63... | collective-permute-start | bytes 393224 | tf_op jit(solution)/shard_map/ppermute | solution.py:335
  30.8 3.6 %collective-permute-done.3 = bf16[432,128]{1,0:T(8,128)(2,1)S(1)} collective-permute-done((bf16[432,128]{1,0:T(8,128)(2,1)S(1)}, bf16[432,128]{1,0:T(8,128)(2,1)S(1)}, u32[]{:S(2)}, u32[]{:S(2)}) %collective-permute-start.3) | collective-permute-done | bytes 110624 | tf_op jit(solution)/shard_map/ppermute | solution.py:332
  34.4 1.1 %collective-permute-done.4 = bf16[432,128]{1,0:T(8,128)(2,1)S(1)} collective-permute-done((bf16[432,128]{1,0:T(8,128)(2,1)S(1)}, bf16[432,128]{1,0:T(8,128)(2,1)S(1)}, u32[]{:S(2)}, u32[]{:S(2)}) %collective-permute-start.4) | collective-permute-done | bytes 110624 | tf_op jit(solution)/shard_map/ppermute | solution.py:332
  35.5 0.1 add_convert_fusion
  35.6 1.0 %collective-permute-start.8 = (bf16[8,18,32,128]{3,2,1,0:T(8,128)(2,1)S(1)}, bf16[8,18,32,128]{3,2,1,0:T(8,128)(2,1)S(1)}, u32[]{:S(2)}, u32[]{:S(2)}) collective-permute-start(bf16[8,18,32,128]{3,2,1,0:T(8,128)(2,1)S(1)} %all-to-all-done.mine_ref), channel_id=1, source_target_pairs={{0,8},{8,0},{16,24},{24,16},{32,40},{40,32},{48,56},{56,48},{64,72... | collective-permute-start | bytes 3538952 | tf_op jit(solution)/shard_map/ppermute | solution.py:332
  36.7 3.2 %collective-permute-start.7 = (bf16[432,128]{1,0:T(8,128)(2,1)S(1)}, bf16[432,128]{1,0:T(8,128)(2,1)S(1)}, u32[]{:S(2)}, u32[]{:S(2)}) collective-permute-start(bf16[432,128]{1,0:T(8,128)(2,1)S(1)} %add_convert_fusion), channel_id=1, source_target_pairs={{0,64},{8,72},{16,80},{24,88},{32,96},{40,104},{48,112},{56,120},{... | collective-permute-start | bytes 331784 | tf_op jit(solution)/shard_map/ppermute | solution.py:332
  39.9 2.1 %collective-permute-start.6 = (f32[4,32,256]{2,1,0:T(8,128)S(1)}, f32[4,32,256]{2,1,0:T(8,128)S(1)}, u32[]{:S(2)}, u32[]{:S(2)}) collective-permute-start(f32[4,32,256]{2,1,0:T(8,128)S(1)} %broadcast_select_fusion), channel_id=1, source_target_pairs={{0,8},{8,16},{16,24},{24,32},{32,40},{40,48},{48,56},{64,72},{72,8... | collective-permute-start | bytes 393224 | tf_op jit(solution)/shard_map/ppermute | solution.py:341
  42.0 1.8 %input_grad_local.1 = bf16[4,256,128]{2,1,0:T(8,128)(2,1)} custom-call(bf16[8,18,32,128]{3,2,1,0:T(8,128)(2,1)S(1)} %all-to-all-done.mine_ref, bf16[8,18,32,128]{3,2,1,0:T(8,128)(2,1)S(1)} %collective-permute-done.8.other_ref), custom_call_target="tpu_custom_call" | custom-call | flops 2000000000 | bytes 3000000 | tf_op jit(solution)/shard_map/input_grad_local/pallas_call | solution.py:282
  43.7 0.6 %collective-permute-start.9 = (f32[432,128]{1,0:T(8,128)S(1)}, f32[432,128]{1,0:T(8,128)S(1)}, u32[]{:S(2)}, u32[]{:S(2)}) collective-permute-start(f32[432,128]{1,0:T(8,128)S(1)} %convert_add_fusion.mine_ref), channel_id=1, source_target_pairs={{0,8},{8,0},{16,24},{24,16},{32,40},{40,32},{48,56},{56,48},{64,72... | collective-permute-start | bytes 663560 | tf_op jit(solution)/shard_map/ppermute | solution.py:332
  44.3 0.6 %fusion = bf16[4,32,1,256]{3,1,2,0:T(8,128)(2,1)} fusion(f32[4,32,256]{2,1,0:T(8,128)S(1)} %copy-done, f32[4,32,256]{2,1,0:T(8,128)S(1)} %collective-permute-done.6), kind=kLoop, calls=%fused_computation.4 | loop fusion | flops 65536 | bytes 327680
  45.0 0.5 collective-permute-done.9.theirs_ref
  45.4 0.8 %place.1 = f32[864,128]{1,0:T(8,128)} custom-call(f32[432,128]{1,0:T(8,128)S(1)} %convert_add_fusion.mine_ref, f32[432,128]{1,0:T(8,128)S(1)} %collective-permute-done.9.theirs_ref), custom_call_target="tpu_custom_call" | custom-call | tf_op jit(solution)/shard_map/place/pallas_call | solution.py:307
  (14 shorter events, 0.1 us)
Async XLA Ops:
  0.6 8.1 %collective-permute-start = (bf16[4,32,256]{2,1,0:T(8,128)(2,1)}, bf16[4,32,256]{2,1,0:T(8,128)(2,1)S(1)}, u32[]{:S(2)}, u32[]{:S(2)}) collective-permute-start(bf16[4,32,256]{2,1,0:T(8,128)(2,1)} %bitcast.17), channel_id=1, source_target_pairs={{8,0},{16,8},{24,16},{32,24},{40,32},{48,40},{56,48},{64,56},{72,6... | collective-permute-start | bytes 196616 | tf_op jit(solution)/shard_map/ppermute | solution.py:325
  8.7 0.6 %copy-start.2 = (bf16[4,32,256]{2,1,0:T(8,128)(2,1)}, bf16[4,32,256]{2,1,0:T(8,128)(2,1)S(1)}, u32[]{:S(2)}) copy-start(bf16[4,32,256]{2,1,0:T(8,128)(2,1)S(1)} %collective-permute-done.gn_ref) | copy-start | bytes 196612
  11.0 24.6 %all-to-all-start = ((bf16[8,18,32,128]{3,2,1,0:T(8,128)(2,1)}), bf16[8,18,32,128]{3,2,1,0:T(8,128)(2,1)S(1)}, u32[]{:S(2)}, u32[]{:S(2)}) async-start(bf16[8,18,32,128]{3,2,1,0:T(8,128)(2,1)} %next_cells.1), calls=%async_computation | async-start | bytes 2359296 | tf_op jit(solution)/shard_map/all_to_all | solution.py:316
  21.8 18.0 %copy-start.1 = (f32[4,32,256]{2,1,0:T(8,128)S(1)}, f32[4,32,256]{2,1,0:T(8,128)}, u32[]{:S(2)}) copy-start(f32[4,32,256]{2,1,0:T(8,128)} %get-tuple-element.19) | copy-start | bytes 393220
  21.8 1.8 %collective-permute-start.1 = (f32[432,128]{1,0:T(8,128)}, f32[432,128]{1,0:T(8,128)S(1)}, u32[]{:S(2)}, u32[]{:S(2)}) collective-permute-start(f32[432,128]{1,0:T(8,128)} %get-tuple-element.17), channel_id=1, source_target_pairs={{0,8},{8,0},{16,24},{24,16},{32,40},{40,32},{48,56},{56,48},{64,72... | collective-permute-start | bytes 663560 | tf_op jit(solution)/shard_map/ppermute | solution.py:332
  24.6 6.2 %collective-permute-start.2 = (bf16[432,128]{1,0:T(8,128)(2,1)S(1)}, bf16[432,128]{1,0:T(8,128)(2,1)S(1)}, u32[]{:S(2)}, u32[]{:S(2)}) collective-permute-start(bf16[432,128]{1,0:T(8,128)(2,1)S(1)} %add_convert_fusion.1), channel_id=1, source_target_pairs={{0,32},{8,40},{16,48},{24,56},{32,0},{40,8},{48,16},{56,24},{64,96... | collective-permute-start | bytes 331784 | tf_op jit(solution)/shard_map/ppermute | solution.py:332
  27.6 6.8 %collective-permute-start.3 = (bf16[432,128]{1,0:T(8,128)(2,1)S(1)}, bf16[432,128]{1,0:T(8,128)(2,1)S(1)}, u32[]{:S(2)}, u32[]{:S(2)}) collective-permute-start(bf16[432,128]{1,0:T(8,128)(2,1)S(1)} %add_convert_fusion.1), channel_id=1, source_target_pairs={{0,48},{8,56},{16,32},{24,40},{32,16},{40,24},{48,0},{56,8},{64,11... | collective-permute-start | bytes 331784 | tf_op jit(solution)/shard_map/ppermute | solution.py:332
  29.6 6.0 %collective-permute-start.4 = (bf16[432,128]{1,0:T(8,128)(2,1)S(1)}, bf16[432,128]{1,0:T(8,128)(2,1)S(1)}, u32[]{:S(2)}, u32[]{:S(2)}) collective-permute-start(bf16[432,128]{1,0:T(8,128)(2,1)S(1)} %add_convert_fusion.1), channel_id=1, source_target_pairs={{0,16},{8,24},{16,0},{24,8},{32,48},{40,56},{48,32},{56,40},{64,80... | collective-permute-start | bytes 331784 | tf_op jit(solution)/shard_map/ppermute | solution.py:332
  30.1 5.5 %collective-permute-start.5 = (f32[4,32,256]{2,1,0:T(8,128)}, f32[4,32,256]{2,1,0:T(8,128)S(1)}, u32[]{:S(2)}, u32[]{:S(2)}) collective-permute-start(f32[4,32,256]{2,1,0:T(8,128)} %get-tuple-element.19), channel_id=1, source_target_pairs={{56,120},{57,121},{58,122},{59,123},{60,124},{61,125},{62,126},{63... | collective-permute-start | bytes 393224 | tf_op jit(solution)/shard_map/ppermute | solution.py:335
  35.6 6.3 %collective-permute-start.8 = (bf16[8,18,32,128]{3,2,1,0:T(8,128)(2,1)S(1)}, bf16[8,18,32,128]{3,2,1,0:T(8,128)(2,1)S(1)}, u32[]{:S(2)}, u32[]{:S(2)}) collective-permute-start(bf16[8,18,32,128]{3,2,1,0:T(8,128)(2,1)S(1)} %all-to-all-done.mine_ref), channel_id=1, source_target_pairs={{0,8},{8,0},{16,24},{24,16},{32,40},{40,32},{48,56},{56,48},{64,72... | collective-permute-start | bytes 3538952 | tf_op jit(solution)/shard_map/ppermute | solution.py:332
  36.7 7.0 %collective-permute-start.7 = (bf16[432,128]{1,0:T(8,128)(2,1)S(1)}, bf16[432,128]{1,0:T(8,128)(2,1)S(1)}, u32[]{:S(2)}, u32[]{:S(2)}) collective-permute-start(bf16[432,128]{1,0:T(8,128)(2,1)S(1)} %add_convert_fusion), channel_id=1, source_target_pairs={{0,64},{8,72},{16,80},{24,88},{32,96},{40,104},{48,112},{56,120},{... | collective-permute-start | bytes 331784 | tf_op jit(solution)/shard_map/ppermute | solution.py:332
  39.9 4.5 %copy-start = (f32[4,32,256]{2,1,0:T(8,128)S(1)}, f32[4,32,256]{2,1,0:T(8,128)}, u32[]{:S(2)}) copy-start(f32[4,32,256]{2,1,0:T(8,128)} %get-tuple-element.15) | copy-start | bytes 393220
  39.9 4.4 %collective-permute-start.6 = (f32[4,32,256]{2,1,0:T(8,128)S(1)}, f32[4,32,256]{2,1,0:T(8,128)S(1)}, u32[]{:S(2)}, u32[]{:S(2)}) collective-permute-start(f32[4,32,256]{2,1,0:T(8,128)S(1)} %broadcast_select_fusion), channel_id=1, source_target_pairs={{0,8},{8,16},{16,24},{24,32},{32,40},{40,48},{48,56},{64,72},{72,8... | collective-permute-start | bytes 393224 | tf_op jit(solution)/shard_map/ppermute | solution.py:341
  43.7 1.7 %collective-permute-start.9 = (f32[432,128]{1,0:T(8,128)S(1)}, f32[432,128]{1,0:T(8,128)S(1)}, u32[]{:S(2)}, u32[]{:S(2)}) collective-permute-start(f32[432,128]{1,0:T(8,128)S(1)} %convert_add_fusion.mine_ref), channel_id=1, source_target_pairs={{0,8},{8,0},{16,24},{24,16},{32,40},{40,32},{48,56},{56,48},{64,72... | collective-permute-start | bytes 663560 | tf_op jit(solution)/shard_map/ppermute | solution.py:332

commit v7 on v6

--- a/solution.py
+++ b/solution.py
@@ -333,21 +333,19 @@
 
     turn = spaces // 2
     relayed = lax.ppermute(send, "space", [(turn - 1, spaces - 1)])
+    came = lax.ppermute(send, "space", [(i, i + 1) for i in range(spaces - 1) if i != turn - 1])
     pair = (keep + exchange(go, 1)).astype(BF16)
-    near, far, farther = (exchange(pair, bits).astype(F32) for bits in (4, 6, 2))
+    near, far, farther = (exchange(pair, bits).astype(F32) for bits in (2, 6, 4))
     row = ((pair.astype(F32) + near) + (far + farther)).astype(BF16)
-    row, mine, relayed = lax.optimization_barrier((row, mine, relayed))
-    passed = jnp.where(lax.axis_index("space") == spaces - 1, relayed, send)
-    came = lax.ppermute(
-        passed, "space", [(i, i + 1) for i in range(spaces - 1) if i != turn - 1] + [(spaces - 1, turn)]
-    )
+    row, mine, relayed, came = lax.optimization_barrier((row, mine, relayed, came))
+    turned = lax.ppermute(relayed, "space", [(spaces - 1, turn)])
     other = exchange(mine, 1)
     across = exchange(row, 8)
     input_grad = input_grad_local(mine, other).reshape(B, CIN, 2, 128)
     across, input_grad = lax.optimization_barrier((across, input_grad))
     held = row.astype(F32) + across.astype(F32)
     kernel_grad = place(held, exchange(held, 1)).reshape(3, 3, 3, 32, CIN)
-    output = (own + came).astype(BF16).reshape(B, 32, 1, 256)
+    output = (own + came + turned).astype(BF16).reshape(B, 32, 1, 256)
     return (output, input_grad, kernel_grad)
 
 

time: 46.5 us -> 46.2 us (level)
  waiting for transfers between devices: 6.93 us -> 4.52 us
  starting transfers between devices: 21.9 us -> 24 us
    ppermute x7, waiting for transfers between devices: 6.92 us -> 4.33 us  [exchange(): return lax.ppermute(values, 'space', [(i, i ^ bits) for i in range(spaces)])]
    ppermute x1 -> x2, starting transfers between devices: 2.05 us -> 4.13 us  [the longest x1 3.47 us: body(): lax.ppermute(send, 'space', [(i, i + 1) for i in range(spaces - 1) if i !...]
  transfers between devices with their start and end apart: 11 -> 12, of which waited for: 4 -> 6; matrix products, arithmetic and copies ran while one was open for 4% -> 4% of each run, Pallas kernels for 26% -> 26%
where the time goes in v7:
time: 46.2 us; the launch traced here: 45.9 us
  starting transfers between devices  24 us (52%)
  Pallas kernels  14.3 us (31%)
  waiting for transfers between devices  4.52 us (10%)
  other arithmetic  1.7 us (4%)
  between operations  0.75 us (2%)
  local copies, waits for them, and re-layouts  0.63 us (1%)
    ppermute x7, starting transfers between devices, exchange(): return lax.ppermute(values, 'space', [(i, i ^ bits) for i in range(spaces)])  10.4 us
    all_to_all x1, starting transfers between devices, swap(): return lax.all_to_all(values, axis, split_axis=0, concat_axis=0, tiled=True)  5.46 us
    pallas_call x1, Pallas kernels, conv_local(): pl.pallas_call(conv_kernel, in_specs=[pl.BlockSpec(memory_space=pltpu.HBM...  5.36 us
    pallas_call x1, Pallas kernels, prepare(): pl.pallas_call(prepare_kernel, in_specs=[pl.BlockSpec(memory_space=pltpu....  4.7 us
    ppermute x7, waiting for transfers between devices, exchange(): return lax.ppermute(values, 'space', [(i, i ^ bits) for i in range(spaces)])  4.33 us
    ppermute x1, starting transfers between devices, body(): lax.ppermute(send, 'space', [(i, i + 1) for i in range(spaces - 1) if i !...  3.47 us
    ppermute x1, starting transfers between devices, body(): g_next = lax.ppermute(g, 'space', to_previous)  3.33 us
    pallas_call x1, Pallas kernels, input_grad_local(): pl.pallas_call(input_grad_kernel, out_shape=jax.ShapeDtypeStruct((B, 2 *...  1.75 us
  transfers between devices with their start and end apart: 12, of which 6 were waited for; matrix products, arithmetic and copies ran while one was open for 4% of the time, Pallas kernels for 26%

profile of v7, /device:TPU:1, one launch (start us, length us, event | category | flops | bytes accessed | tf_op | source)
XLA Modules:
  0.0 45.9 jit_solution(4885935603415381486)
XLA Ops:
  0.6 3.3 %collective-permute-start = (bf16[4,32,256]{2,1,0:T(8,128)(2,1)}, bf16[4,32,256]{2,1,0:T(8,128)(2,1)S(1)}, u32[]{:S(2)}, u32[]{:S(2)}) collective-permute-start(bf16[4,32,256]{2,1,0:T(8,128)(2,1)} %bitcast.17), channel_id=1, source_target_pairs={{8,0},{16,8},{24,16},{32,24},{40,32},{48,40},{56,48},{64,56},{72,6... | collective-permute-start | bytes 196616 | tf_op jit(solution)/shard_map/ppermute | solution.py:325
  4.0 4.7 %prepare.1 = (bf16[4,2,3,33,16,128]{5,4,3,2,1,0:T(8,128)(2,1)}, bf16[8,18,32,128]{3,2,1,0:T(8,128)(2,1)}) custom-call(bf16[4,2048,128]{2,1,0:T(8,128)(2,1)} %bitcast.14, bf16[27,32,128]{2,1,0:T(8,128)(2,1)} %bitcast.15, bf16[4,32,256]{2,1,0:T(8,128)(2,1)} %bitcast.18), custom_call_target="tpu_custom_call" | custom-call | flops 4000000000 | bytes 5000000 | tf_op jit(solution)/shard_map/prepare/pallas_call | solution.py:96
  8.7 0.6 %copy-done.1 = bf16[4,32,256]{2,1,0:T(8,128)(2,1)} copy-done((bf16[4,32,256]{2,1,0:T(8,128)(2,1)}, bf16[4,32,256]{2,1,0:T(8,128)(2,1)S(1)}, u32[]{:S(2)}) %copy-start.1) | copy-done | bytes 65560
  9.3 1.7 %next_cells.1 = bf16[8,18,32,128]{3,2,1,0:T(8,128)(2,1)} custom-call(bf16[4,32,256]{2,1,0:T(8,128)(2,1)} %copy-done.1, bf16[8,18,32,128]{3,2,1,0:T(8,128)(2,1)} %get-tuple-element.19._), custom_call_target="tpu_custom_call", output_to_operand_aliasing={{}: (1, {})} | custom-call | tf_op jit(solution)/shard_map/next_cells/pallas_call | solution.py:130
  11.0 5.5 %all-to-all-start = ((bf16[8,18,32,128]{3,2,1,0:T(8,128)(2,1)}), bf16[8,18,32,128]{3,2,1,0:T(8,128)(2,1)S(1)}, u32[]{:S(2)}, u32[]{:S(2)}) async-start(bf16[8,18,32,128]{3,2,1,0:T(8,128)(2,1)} %next_cells.1), calls=%async_computation | async-start | bytes 2359296 | tf_op jit(solution)/shard_map/all_to_all | solution.py:316
  16.5 5.4 %conv_local.1 = (f32[4,32,256]{2,1,0:T(8,128)}, f32[4,32,256]{2,1,0:T(8,128)}, f32[432,128]{1,0:T(8,128)}, f32[432,128]{1,0:T(8,128)}) custom-call(bf16[4,2,3,33,16,128]{5,4,3,2,1,0:T(8,128)(2,1)} %get-tuple-element.15.planes_ref, bf16[27,32,128]{2,1,0:T(8,128)(2,1)} %bitcast.16, bf16[4,32,256]{2,1,0:T(8,128)(2,1)} %bitcast.19, bf16[4,32,256]{2,1,0:T(8,128)(2,1)} %copy-done.1), custom_call_target="tpu_custom_call" | custom-call | flops 4000000000 | bytes 5000000 | tf_op jit(solution)/shard_map/conv_local/pallas_call | solution.py:205
  21.9 1.7 %collective-permute-done.1 = f32[432,128]{1,0:T(8,128)S(1)} collective-permute-done((f32[432,128]{1,0:T(8,128)}, f32[432,128]{1,0:T(8,128)S(1)}, u32[]{:S(2)}, u32[]{:S(2)}) %collective-permute-start.1) | collective-permute-done | bytes 221216 | tf_op jit(solution)/shard_map/ppermute | solution.py:332
  23.6 1.0 %add_convert_fusion.1 = bf16[432,128]{1,0:T(8,128)(2,1)S(1)} fusion(f32[432,128]{1,0:T(8,128)} %get-tuple-element.17, f32[432,128]{1,0:T(8,128)S(1)} %collective-permute-done.1), kind=kLoop, calls=%fused_computation.2 | loop fusion | flops 110592 | bytes 552960 | tf_op jit(solution)/shard_map/convert_element_type | solution.py:337
  24.6 3.0 %collective-permute-start.4 = (bf16[432,128]{1,0:T(8,128)(2,1)S(1)}, bf16[432,128]{1,0:T(8,128)(2,1)S(1)}, u32[]{:S(2)}, u32[]{:S(2)}) collective-permute-start(bf16[432,128]{1,0:T(8,128)(2,1)S(1)} %add_convert_fusion.1), channel_id=1, source_target_pairs={{0,32},{8,40},{16,48},{24,56},{32,0},{40,8},{48,16},{56,24},{64,96... | collective-permute-start | bytes 331784 | tf_op jit(solution)/shard_map/ppermute | solution.py:332
  27.6 2.0 %collective-permute-start.3 = (bf16[432,128]{1,0:T(8,128)(2,1)S(1)}, bf16[432,128]{1,0:T(8,128)(2,1)S(1)}, u32[]{:S(2)}, u32[]{:S(2)}) collective-permute-start(bf16[432,128]{1,0:T(8,128)(2,1)S(1)} %add_convert_fusion.1), channel_id=1, source_target_pairs={{0,48},{8,56},{16,32},{24,40},{32,16},{40,24},{48,0},{56,8},{64,11... | collective-permute-start | bytes 331784 | tf_op jit(solution)/shard_map/ppermute | solution.py:332
  29.6 0.5 %collective-permute-start.2 = (bf16[432,128]{1,0:T(8,128)(2,1)S(1)}, bf16[432,128]{1,0:T(8,128)(2,1)S(1)}, u32[]{:S(2)}, u32[]{:S(2)}) collective-permute-start(bf16[432,128]{1,0:T(8,128)(2,1)S(1)} %add_convert_fusion.1), channel_id=1, source_target_pairs={{0,16},{8,24},{16,0},{24,8},{32,48},{40,56},{48,32},{56,40},{64,80... | collective-permute-start | bytes 331784 | tf_op jit(solution)/shard_map/ppermute | solution.py:332
  30.1 3.5 %collective-permute-start.6 = (f32[4,32,256]{2,1,0:T(8,128)}, f32[4,32,256]{2,1,0:T(8,128)S(1)}, u32[]{:S(2)}, u32[]{:S(2)}) collective-permute-start(f32[4,32,256]{2,1,0:T(8,128)} %get-tuple-element.20), channel_id=1, source_target_pairs={{0,8},{8,16},{16,24},{24,32},{32,40},{40,48},{48,56},{64,72},{72,8... | collective-permute-start | bytes 393224 | tf_op jit(solution)/shard_map/ppermute | solution.py:336
  33.5 0.7 %collective-permute-start.5 = (f32[4,32,256]{2,1,0:T(8,128)}, f32[4,32,256]{2,1,0:T(8,128)S(1)}, u32[]{:S(2)}, u32[]{:S(2)}) collective-permute-start(f32[4,32,256]{2,1,0:T(8,128)} %get-tuple-element.20), channel_id=1, source_target_pairs={{56,120},{57,121},{58,122},{59,123},{60,124},{61,125},{62,126},{63... | collective-permute-start | bytes 393224 | tf_op jit(solution)/shard_map/ppermute | solution.py:335
  34.4 1.1 %collective-permute-done.2 = bf16[432,128]{1,0:T(8,128)(2,1)S(1)} collective-permute-done((bf16[432,128]{1,0:T(8,128)(2,1)S(1)}, bf16[432,128]{1,0:T(8,128)(2,1)S(1)}, u32[]{:S(2)}, u32[]{:S(2)}) %collective-permute-start.2) | collective-permute-done | bytes 110624 | tf_op jit(solution)/shard_map/ppermute | solution.py:332
  35.6 0.2 collective-permute-done.6
  35.8 0.9 %collective-permute-start.9 = (bf16[8,18,32,128]{3,2,1,0:T(8,128)(2,1)S(1)}, bf16[8,18,32,128]{3,2,1,0:T(8,128)(2,1)S(1)}, u32[]{:S(2)}, u32[]{:S(2)}) collective-permute-start(bf16[8,18,32,128]{3,2,1,0:T(8,128)(2,1)S(1)} %all-to-all-done.mine_ref), channel_id=1, source_target_pairs={{0,8},{8,0},{16,24},{24,16},{32,40},{40,32},{48,56},{56,48},{64,72... | collective-permute-start | bytes 3538952 | tf_op jit(solution)/shard_map/ppermute | solution.py:332
  36.7 3.2 %collective-permute-start.8 = (bf16[432,128]{1,0:T(8,128)(2,1)S(1)}, bf16[432,128]{1,0:T(8,128)(2,1)S(1)}, u32[]{:S(2)}, u32[]{:S(2)}) collective-permute-start(bf16[432,128]{1,0:T(8,128)(2,1)S(1)} %add_convert_fusion), channel_id=1, source_target_pairs={{0,64},{8,72},{16,80},{24,88},{32,96},{40,104},{48,112},{56,120},{... | collective-permute-start | bytes 331784 | tf_op jit(solution)/shard_map/ppermute | solution.py:332
  39.9 0.7 %collective-permute-start.7 = (f32[4,32,256]{2,1,0:T(8,128)S(1)}, f32[4,32,256]{2,1,0:T(8,128)S(1)}, u32[]{:S(2)}, u32[]{:S(2)}) collective-permute-start(f32[4,32,256]{2,1,0:T(8,128)S(1)} %collective-permute-done.5), channel_id=1, source_target_pairs={{120,64},{121,65},{122,66},{123,67},{124,68},{125,69},{126,70},{12... | collective-permute-start | bytes 393224 | tf_op jit(solution)/shard_map/ppermute | solution.py:341
  40.5 1.8 %input_grad_local.1 = bf16[4,256,128]{2,1,0:T(8,128)(2,1)} custom-call(bf16[8,18,32,128]{3,2,1,0:T(8,128)(2,1)S(1)} %all-to-all-done.mine_ref, bf16[8,18,32,128]{3,2,1,0:T(8,128)(2,1)S(1)} %collective-permute-done.9.other_ref), custom_call_target="tpu_custom_call" | custom-call | flops 2000000000 | bytes 3000000 | tf_op jit(solution)/shard_map/input_grad_local/pallas_call | solution.py:282
  42.3 0.9 %collective-permute-done.8 = bf16[432,128]{1,0:T(8,128)(2,1)S(1)} collective-permute-done((bf16[432,128]{1,0:T(8,128)(2,1)S(1)}, bf16[432,128]{1,0:T(8,128)(2,1)S(1)}, u32[]{:S(2)}, u32[]{:S(2)}) %collective-permute-start.8) | collective-permute-done | bytes 110624 | tf_op jit(solution)/shard_map/ppermute | solution.py:332
  43.2 0.7 %collective-permute-start.10 = (f32[432,128]{1,0:T(8,128)S(1)}, f32[432,128]{1,0:T(8,128)S(1)}, u32[]{:S(2)}, u32[]{:S(2)}) collective-permute-start(f32[432,128]{1,0:T(8,128)S(1)} %convert_add_fusion.mine_ref), channel_id=1, source_target_pairs={{0,8},{8,0},{16,24},{24,16},{32,40},{40,32},{48,56},{56,48},{64,72... | collective-permute-start | bytes 663560 | tf_op jit(solution)/shard_map/ppermute | solution.py:332
  44.0 0.7 %fusion = bf16[4,32,1,256]{3,1,2,0:T(8,128)(2,1)} fusion(f32[4,32,256]{2,1,0:T(8,128)S(1)} %collective-permute-done.7, f32[4,32,256]{2,1,0:T(8,128)S(1)} %copy-done, f32[4,32,256]{2,1,0:T(8,128)S(1)} %collective-permute-done.6), kind=kLoop, calls=%fused_computation.4 | loop fusion | flops 98304 | bytes 458752
  44.6 0.4 collective-permute-done.10.theirs_ref
  45.1 0.8 %place.1 = f32[864,128]{1,0:T(8,128)} custom-call(f32[432,128]{1,0:T(8,128)S(1)} %convert_add_fusion.mine_ref, f32[432,128]{1,0:T(8,128)S(1)} %collective-permute-done.10.theirs_ref), custom_call_target="tpu_custom_call" | custom-call | tf_op jit(solution)/shard_map/place/pallas_call | solution.py:307
  (13 shorter events, 0.3 us)
Async XLA Ops:
  0.6 8.1 %collective-permute-start = (bf16[4,32,256]{2,1,0:T(8,128)(2,1)}, bf16[4,32,256]{2,1,0:T(8,128)(2,1)S(1)}, u32[]{:S(2)}, u32[]{:S(2)}) collective-permute-start(bf16[4,32,256]{2,1,0:T(8,128)(2,1)} %bitcast.17), channel_id=1, source_target_pairs={{8,0},{16,8},{24,16},{32,24},{40,32},{48,40},{56,48},{64,56},{72,6... | collective-permute-start | bytes 196616 | tf_op jit(solution)/shard_map/ppermute | solution.py:325
  8.7 0.6 %copy-start.1 = (bf16[4,32,256]{2,1,0:T(8,128)(2,1)}, bf16[4,32,256]{2,1,0:T(8,128)(2,1)S(1)}, u32[]{:S(2)}) copy-start(bf16[4,32,256]{2,1,0:T(8,128)(2,1)S(1)} %collective-permute-done.gn_ref) | copy-start | bytes 196612
  11.0 24.8 %all-to-all-start = ((bf16[8,18,32,128]{3,2,1,0:T(8,128)(2,1)}), bf16[8,18,32,128]{3,2,1,0:T(8,128)(2,1)S(1)}, u32[]{:S(2)}, u32[]{:S(2)}) async-start(bf16[8,18,32,128]{3,2,1,0:T(8,128)(2,1)} %next_cells.1), calls=%async_computation | async-start | bytes 2359296 | tf_op jit(solution)/shard_map/all_to_all | solution.py:316
  21.8 1.8 %collective-permute-start.1 = (f32[432,128]{1,0:T(8,128)}, f32[432,128]{1,0:T(8,128)S(1)}, u32[]{:S(2)}, u32[]{:S(2)}) collective-permute-start(f32[432,128]{1,0:T(8,128)} %get-tuple-element.18), channel_id=1, source_target_pairs={{0,8},{8,0},{16,24},{24,16},{32,40},{40,32},{48,56},{56,48},{64,72... | collective-permute-start | bytes 663560 | tf_op jit(solution)/shard_map/ppermute | solution.py:332
  24.6 9.7 %collective-permute-start.4 = (bf16[432,128]{1,0:T(8,128)(2,1)S(1)}, bf16[432,128]{1,0:T(8,128)(2,1)S(1)}, u32[]{:S(2)}, u32[]{:S(2)}) collective-permute-start(bf16[432,128]{1,0:T(8,128)(2,1)S(1)} %add_convert_fusion.1), channel_id=1, source_target_pairs={{0,32},{8,40},{16,48},{24,56},{32,0},{40,8},{48,16},{56,24},{64,96... | collective-permute-start | bytes 331784 | tf_op jit(solution)/shard_map/ppermute | solution.py:332
  27.6 6.8 %collective-permute-start.3 = (bf16[432,128]{1,0:T(8,128)(2,1)S(1)}, bf16[432,128]{1,0:T(8,128)(2,1)S(1)}, u32[]{:S(2)}, u32[]{:S(2)}) collective-permute-start(bf16[432,128]{1,0:T(8,128)(2,1)S(1)} %add_convert_fusion.1), channel_id=1, source_target_pairs={{0,48},{8,56},{16,32},{24,40},{32,16},{40,24},{48,0},{56,8},{64,11... | collective-permute-start | bytes 331784 | tf_op jit(solution)/shard_map/ppermute | solution.py:332
  29.6 6.0 %collective-permute-start.2 = (bf16[432,128]{1,0:T(8,128)(2,1)S(1)}, bf16[432,128]{1,0:T(8,128)(2,1)S(1)}, u32[]{:S(2)}, u32[]{:S(2)}) collective-permute-start(bf16[432,128]{1,0:T(8,128)(2,1)S(1)} %add_convert_fusion.1), channel_id=1, source_target_pairs={{0,16},{8,24},{16,0},{24,8},{32,48},{40,56},{48,32},{56,40},{64,80... | collective-permute-start | bytes 331784 | tf_op jit(solution)/shard_map/ppermute | solution.py:332
  30.1 5.7 %collective-permute-start.6 = (f32[4,32,256]{2,1,0:T(8,128)}, f32[4,32,256]{2,1,0:T(8,128)S(1)}, u32[]{:S(2)}, u32[]{:S(2)}) collective-permute-start(f32[4,32,256]{2,1,0:T(8,128)} %get-tuple-element.20), channel_id=1, source_target_pairs={{0,8},{8,16},{16,24},{24,32},{32,40},{40,48},{48,56},{64,72},{72,8... | collective-permute-start | bytes 393224 | tf_op jit(solution)/shard_map/ppermute | solution.py:336
  33.5 2.2 %collective-permute-start.5 = (f32[4,32,256]{2,1,0:T(8,128)}, f32[4,32,256]{2,1,0:T(8,128)S(1)}, u32[]{:S(2)}, u32[]{:S(2)}) collective-permute-start(f32[4,32,256]{2,1,0:T(8,128)} %get-tuple-element.20), channel_id=1, source_target_pairs={{56,120},{57,121},{58,122},{59,123},{60,124},{61,125},{62,126},{63... | collective-permute-start | bytes 393224 | tf_op jit(solution)/shard_map/ppermute | solution.py:335
  35.6 8.4 %copy-start = (f32[4,32,256]{2,1,0:T(8,128)S(1)}, f32[4,32,256]{2,1,0:T(8,128)}, u32[]{:S(2)}) copy-start(f32[4,32,256]{2,1,0:T(8,128)} %get-tuple-element.16) | copy-start | bytes 393220
  35.8 4.7 %collective-permute-start.9 = (bf16[8,18,32,128]{3,2,1,0:T(8,128)(2,1)S(1)}, bf16[8,18,32,128]{3,2,1,0:T(8,128)(2,1)S(1)}, u32[]{:S(2)}, u32[]{:S(2)}) collective-permute-start(bf16[8,18,32,128]{3,2,1,0:T(8,128)(2,1)S(1)} %all-to-all-done.mine_ref), channel_id=1, source_target_pairs={{0,8},{8,0},{16,24},{24,16},{32,40},{40,32},{48,56},{56,48},{64,72... | collective-permute-start | bytes 3538952 | tf_op jit(solution)/shard_map/ppermute | solution.py:332
  36.7 6.5 %collective-permute-start.8 = (bf16[432,128]{1,0:T(8,128)(2,1)S(1)}, bf16[432,128]{1,0:T(8,128)(2,1)S(1)}, u32[]{:S(2)}, u32[]{:S(2)}) collective-permute-start(bf16[432,128]{1,0:T(8,128)(2,1)S(1)} %add_convert_fusion), channel_id=1, source_target_pairs={{0,64},{8,72},{16,80},{24,88},{32,96},{40,104},{48,112},{56,120},{... | collective-permute-start | bytes 331784 | tf_op jit(solution)/shard_map/ppermute | solution.py:332
  39.9 4.1 %collective-permute-start.7 = (f32[4,32,256]{2,1,0:T(8,128)S(1)}, f32[4,32,256]{2,1,0:T(8,128)S(1)}, u32[]{:S(2)}, u32[]{:S(2)}) collective-permute-start(f32[4,32,256]{2,1,0:T(8,128)S(1)} %collective-permute-done.5), channel_id=1, source_target_pairs={{120,64},{121,65},{122,66},{123,67},{124,68},{125,69},{126,70},{12... | collective-permute-start | bytes 393224 | tf_op jit(solution)/shard_map/ppermute | solution.py:341
  43.2 1.8 %collective-permute-start.10 = (f32[432,128]{1,0:T(8,128)S(1)}, f32[432,128]{1,0:T(8,128)S(1)}, u32[]{:S(2)}, u32[]{:S(2)}) collective-permute-start(f32[432,128]{1,0:T(8,128)S(1)} %convert_add_fusion.mine_ref), channel_id=1, source_target_pairs={{0,8},{8,0},{16,24},{24,16},{32,40},{40,32},{48,56},{56,48},{64,72... | collective-permute-start | bytes 663560 | tf_op jit(solution)/shard_map/ppermute | solution.py:332

commit v8 on v7

--- a/solution.py
+++ b/solution.py
@@ -147,81 +147,68 @@
     return jnp.concatenate(parts, 1)
 
 
+def per_sample(*shape):
+    return pl.BlockSpec((1,) + shape, lambda b: (b,) + (0,) * len(shape))
+
+
+def whole_array(*shape):
+    return pl.BlockSpec(shape, lambda b: (0,) * len(shape))
+
+
 def conv_kernel(planes_ref, ker_ref, g_ref, gn_ref, own_ref, send_ref, keep_ref, go_ref,
-                planes, ker, grads, own, send, total, arrived, sent):
-    fetch_planes = [
-        pltpu.make_async_copy(planes_ref.at[b], planes.at[b], arrived.at[b]) for b in range(B)
-    ]
-    others = [
-        pltpu.make_async_copy(ker_ref, ker, arrived.at[B]),
-        pltpu.make_async_copy(g_ref, grads.at[0], arrived.at[B + 1]),
-        pltpu.make_async_copy(gn_ref, grads.at[1], arrived.at[B + 2]),
-    ]
-    fetch_planes[0].start()
-    for copy in others + fetch_planes[1:]:
-        copy.start()
+                total):
+    step = pl.program_id(0)
+
+    @pl.when(step == 0)
+    def _():
+        total[...] = jnp.zeros_like(total)
 
     def weights(i):
-        return jnp.concatenate([ker[i * 9 + t] for t in range(9)], 1)
-
-    for copy in others:
-        copy.wait()
-    for step in range(B):
-        fetch_planes[step].wait()
-        grad = grads[0, step]
-        pair = jnp.concatenate([grad, grads[1, step]], 0)
-        even = columns(lambda k, y: planes[step, 0, k, y])
-        here = lax.dot_general(weights(1), even, NT, preferred_element_type=F32)
-        back_even = jnp.dot(grad, even, preferred_element_type=F32)
-        odd = columns(lambda k, y: planes[step, 1, k, y])
-        both = lax.dot_general(
-            jnp.concatenate([weights(2), weights(0)], 0), odd, NT, preferred_element_type=F32
-        )
-        back_odd = jnp.dot(pair, odd, preferred_element_type=F32)
-        own[step] = here + both[:32]
-        send[step] = both[32:]
-        for t in range(9):
-            lanes = slice(t * 128, (t + 1) * 128)
-            for first, value in (
-                (t, back_odd[32:, lanes]), (9 + t, back_even[:, lanes]), (18 + t, back_odd[:32, lanes])
-            ):
-                rows = slice(first * 32, first * 32 + 32)
-                total[rows] = value if step == 0 else total[rows] + value
-    core = lax.rem(lax.axis_index("space"), 2)
-    halves = [
-        total.at[pl.ds(pl.multiple_of(half * HELD, 8), HELD)] for half in (core, 1 - core)
-    ]
-    copies = [
-        pltpu.make_async_copy(source, target, sent.at[i])
-        for i, (source, target) in enumerate(zip([*halves, own, send], [keep_ref, go_ref, own_ref, send_ref]))
-    ]
-    for copy in copies:
-        copy.start()
-    for copy in copies:
-        copy.wait()
+        return jnp.concatenate([ker_ref[i * 9 + t] for t in range(9)], 1)
+
+    grad = g_ref[0]
+    pair = jnp.concatenate([grad, gn_ref[0]], 0)
+    even = columns(lambda k, y: planes_ref[0, 0, k, y])
+    here = lax.dot_general(weights(1), even, NT, preferred_element_type=F32)
+    back_even = jnp.dot(grad, even, preferred_element_type=F32)
+    odd = columns(lambda k, y: planes_ref[0, 1, k, y])
+    both = lax.dot_general(
+        jnp.concatenate([weights(2), weights(0)], 0), odd, NT, preferred_element_type=F32
+    )
+    back_odd = jnp.dot(pair, odd, preferred_element_type=F32)
+    own_ref[0] = here + both[:32]
+    send_ref[0] = both[32:]
+    for t in range(9):
+        lanes = slice(t * 128, (t + 1) * 128)
+        total[t * 32:(t + 1) * 32] += back_odd[32:, lanes]
+        total[(9 + t) * 32:(10 + t) * 32] += back_even[:, lanes]
+        total[(18 + t) * 32:(19 + t) * 32] += back_odd[:32, lanes]
+
+    @pl.when(step == B - 1)
+    def _():
+        core = lax.rem(lax.axis_index("space"), 2)
+        keep_ref[...] = total[pl.ds(pl.multiple_of(core * HELD, 8), HELD)]
+        go_ref[...] = total[pl.ds(pl.multiple_of((1 - core) * HELD, 8), HELD)]
 
 
 def conv_local(planes, ker, g, gn):
     return pl.pallas_call(
         conv_kernel,
-        in_specs=[pl.BlockSpec(memory_space=pltpu.HBM)] * 4,
-        out_specs=[pl.BlockSpec(memory_space=pltpu.HBM)] * 4,
+        grid=(B,),
+        in_specs=[
+            per_sample(2, 3, EDGE + 1, HALF, CIN), whole_array(27, 32, CIN),
+            per_sample(32, 256), per_sample(32, 256),
+        ],
+        out_specs=[
+            per_sample(32, 256), per_sample(32, 256), whole_array(HELD, CIN), whole_array(HELD, CIN)
+        ],
         out_shape=[
             jax.ShapeDtypeStruct((B, 32, 256), F32),
             jax.ShapeDtypeStruct((B, 32, 256), F32),
             jax.ShapeDtypeStruct((HELD, CIN), F32),
             jax.ShapeDtypeStruct((HELD, CIN), F32),
         ],
-        scratch_shapes=[
-            pltpu.VMEM((B, 2, 3, EDGE + 1, HALF, CIN), BF16),
-            pltpu.VMEM((27, 32, CIN), BF16),
-            pltpu.VMEM((2, B, 32, 256), BF16),
-            pltpu.VMEM((B, 32, 256), F32),
-            pltpu.VMEM((B, 32, 256), F32),
-            pltpu.VMEM((2 * HELD, CIN), F32),
-            pltpu.SemaphoreType.DMA((B + 3,)),
-            pltpu.SemaphoreType.DMA((4,)),
-        ],
+        scratch_shapes=[pltpu.VMEM((2 * HELD, CIN), F32)],
         compiler_params=pltpu.CompilerParams(vmem_limit_bytes=FULL),
         cost_estimate=pl.CostEstimate(flops=4_000_000_000, bytes_accessed=5_000_000, transcendentals=0),
         name="conv_local",

time: 46.2 us -> 46.1 us (level)
  no operation moved by 1% of the time
where the time goes in v8:
time: 46.1 us; the launch traced here: 45.7 us
  starting transfers between devices  24 us (52%)
  Pallas kernels  14.2 us (31%)
  waiting for transfers between devices  4.52 us (10%)
  other arithmetic  1.7 us (4%)
  between operations  0.75 us (2%)
  local copies, waits for them, and re-layouts  0.63 us (1%)
    ppermute x7, starting transfers between devices, exchange(): return lax.ppermute(values, 'space', [(i, i ^ bits) for i in range(spaces)])  10.4 us
    all_to_all x1, starting transfers between devices, swap(): return lax.all_to_all(values, axis, split_axis=0, concat_axis=0, tiled=True)  5.46 us
    pallas_call x1, Pallas kernels, conv_local(): pl.pallas_call(conv_kernel, grid=(B,), in_specs=[per_sample(2, 3, EDGE +...  5.25 us
    pallas_call x1, Pallas kernels, prepare(): pl.pallas_call(prepare_kernel, in_specs=[pl.BlockSpec(memory_space=pltpu....  4.7 us
    ppermute x7, waiting for transfers between devices, exchange(): return lax.ppermute(values, 'space', [(i, i ^ bits) for i in range(spaces)])  4.33 us
    ppermute x1, starting transfers between devices, body(): lax.ppermute(send, 'space', [(i, i + 1) for i in range(spaces - 1) if i !...  3.47 us
    ppermute x1, starting transfers between devices, body(): g_next = lax.ppermute(g, 'space', to_previous)  3.33 us
    pallas_call x1, Pallas kernels, input_grad_local(): pl.pallas_call(input_grad_kernel, out_shape=jax.ShapeDtypeStruct((B, 2 *...  1.75 us
  transfers between devices with their start and end apart: 12, of which 6 were waited for; matrix products, arithmetic and copies ran while one was open for 4% of the time, Pallas kernels for 26%

profile of v8, /device:TPU:1, one launch (start us, length us, event | category | flops | bytes accessed | tf_op | source)
XLA Modules:
  0.0 45.7 jit_solution(17527690294503496701)
XLA Ops:
  0.6 3.3 %collective-permute-start = (bf16[4,32,256]{2,1,0:T(8,128)(2,1)}, bf16[4,32,256]{2,1,0:T(8,128)(2,1)S(1)}, u32[]{:S(2)}, u32[]{:S(2)}) collective-permute-start(bf16[4,32,256]{2,1,0:T(8,128)(2,1)} %bitcast.17), channel_id=1, source_target_pairs={{8,0},{16,8},{24,16},{32,24},{40,32},{48,40},{56,48},{64,56},{72,6... | collective-permute-start | bytes 196616 | tf_op jit(solution)/shard_map/ppermute | solution.py:312
  4.0 4.7 %prepare.1 = (bf16[4,2,3,33,16,128]{5,4,3,2,1,0:T(8,128)(2,1)}, bf16[8,18,32,128]{3,2,1,0:T(8,128)(2,1)}) custom-call(bf16[4,2048,128]{2,1,0:T(8,128)(2,1)} %bitcast.14, bf16[27,32,128]{2,1,0:T(8,128)(2,1)} %bitcast.15, bf16[4,32,256]{2,1,0:T(8,128)(2,1)} %bitcast.18), custom_call_target="tpu_custom_call" | custom-call | flops 4000000000 | bytes 5000000 | tf_op jit(solution)/shard_map/prepare/pallas_call | solution.py:96
  8.7 0.6 %copy-done.1 = bf16[4,32,256]{2,1,0:T(8,128)(2,1)} copy-done((bf16[4,32,256]{2,1,0:T(8,128)(2,1)}, bf16[4,32,256]{2,1,0:T(8,128)(2,1)S(1)}, u32[]{:S(2)}) %copy-start.1) | copy-done | bytes 65560
  9.3 1.7 %next_cells.1 = bf16[8,18,32,128]{3,2,1,0:T(8,128)(2,1)} custom-call(bf16[4,32,256]{2,1,0:T(8,128)(2,1)} %copy-done.1, bf16[8,18,32,128]{3,2,1,0:T(8,128)(2,1)} %get-tuple-element.19._), custom_call_target="tpu_custom_call", output_to_operand_aliasing={{}: (1, {})} | custom-call | tf_op jit(solution)/shard_map/next_cells/pallas_call | solution.py:130
  11.0 5.5 %all-to-all-start = ((bf16[8,18,32,128]{3,2,1,0:T(8,128)(2,1)}), bf16[8,18,32,128]{3,2,1,0:T(8,128)(2,1)S(1)}, u32[]{:S(2)}, u32[]{:S(2)}) async-start(bf16[8,18,32,128]{3,2,1,0:T(8,128)(2,1)} %next_cells.1), calls=%async_computation | async-start | bytes 2359296 | tf_op jit(solution)/shard_map/all_to_all | solution.py:303
  16.5 5.3 %conv_local.1 = (f32[4,32,256]{2,1,0:T(8,128)}, f32[4,32,256]{2,1,0:T(8,128)}, f32[432,128]{1,0:T(8,128)}, f32[432,128]{1,0:T(8,128)}) custom-call(bf16[4,2,3,33,16,128]{5,4,3,2,1,0:T(8,128)(2,1)} %get-tuple-element.15.planes_ref, bf16[27,32,128]{2,1,0:T(8,128)(2,1)} %bitcast.16, bf16[4,32,256]{2,1,0:T(8,128)(2,1)} %bitcast.19, bf16[4,32,256]{2,1,0:T(8,128)(2,1)} %copy-done.1), custom_call_target="tpu_custom_call" | custom-call | flops 4000000000 | bytes 5000000 | tf_op jit(solution)/shard_map/conv_local/pallas_call | solution.py:195
  21.8 1.7 %collective-permute-done.1 = f32[432,128]{1,0:T(8,128)S(1)} collective-permute-done((f32[432,128]{1,0:T(8,128)}, f32[432,128]{1,0:T(8,128)S(1)}, u32[]{:S(2)}, u32[]{:S(2)}) %collective-permute-start.1) | collective-permute-done | bytes 221216 | tf_op jit(solution)/shard_map/ppermute | solution.py:319
  23.5 1.0 %add_convert_fusion.1 = bf16[432,128]{1,0:T(8,128)(2,1)S(1)} fusion(f32[432,128]{1,0:T(8,128)} %get-tuple-element.17, f32[432,128]{1,0:T(8,128)S(1)} %collective-permute-done.1), kind=kLoop, calls=%fused_computation.2 | loop fusion | flops 110592 | bytes 552960 | tf_op jit(solution)/shard_map/convert_element_type | solution.py:324
  24.4 3.0 %collective-permute-start.4 = (bf16[432,128]{1,0:T(8,128)(2,1)S(1)}, bf16[432,128]{1,0:T(8,128)(2,1)S(1)}, u32[]{:S(2)}, u32[]{:S(2)}) collective-permute-start(bf16[432,128]{1,0:T(8,128)(2,1)S(1)} %add_convert_fusion.1), channel_id=1, source_target_pairs={{0,32},{8,40},{16,48},{24,56},{32,0},{40,8},{48,16},{56,24},{64,96... | collective-permute-start | bytes 331784 | tf_op jit(solution)/shard_map/ppermute | solution.py:319
  27.4 2.0 %collective-permute-start.3 = (bf16[432,128]{1,0:T(8,128)(2,1)S(1)}, bf16[432,128]{1,0:T(8,128)(2,1)S(1)}, u32[]{:S(2)}, u32[]{:S(2)}) collective-permute-start(bf16[432,128]{1,0:T(8,128)(2,1)S(1)} %add_convert_fusion.1), channel_id=1, source_target_pairs={{0,48},{8,56},{16,32},{24,40},{32,16},{40,24},{48,0},{56,8},{64,11... | collective-permute-start | bytes 331784 | tf_op jit(solution)/shard_map/ppermute | solution.py:319
  29.5 0.5 %collective-permute-start.2 = (bf16[432,128]{1,0:T(8,128)(2,1)S(1)}, bf16[432,128]{1,0:T(8,128)(2,1)S(1)}, u32[]{:S(2)}, u32[]{:S(2)}) collective-permute-start(bf16[432,128]{1,0:T(8,128)(2,1)S(1)} %add_convert_fusion.1), channel_id=1, source_target_pairs={{0,16},{8,24},{16,0},{24,8},{32,48},{40,56},{48,32},{56,40},{64,80... | collective-permute-start | bytes 331784 | tf_op jit(solution)/shard_map/ppermute | solution.py:319
  29.9 3.5 %collective-permute-start.6 = (f32[4,32,256]{2,1,0:T(8,128)}, f32[4,32,256]{2,1,0:T(8,128)S(1)}, u32[]{:S(2)}, u32[]{:S(2)}) collective-permute-start(f32[4,32,256]{2,1,0:T(8,128)} %get-tuple-element.20), channel_id=1, source_target_pairs={{0,8},{8,16},{16,24},{24,32},{32,40},{40,48},{48,56},{64,72},{72,8... | collective-permute-start | bytes 393224 | tf_op jit(solution)/shard_map/ppermute | solution.py:323
  33.4 0.7 %collective-permute-start.5 = (f32[4,32,256]{2,1,0:T(8,128)}, f32[4,32,256]{2,1,0:T(8,128)S(1)}, u32[]{:S(2)}, u32[]{:S(2)}) collective-permute-start(f32[4,32,256]{2,1,0:T(8,128)} %get-tuple-element.20), channel_id=1, source_target_pairs={{56,120},{57,121},{58,122},{59,123},{60,124},{61,125},{62,126},{63... | collective-permute-start | bytes 393224 | tf_op jit(solution)/shard_map/ppermute | solution.py:322
  34.3 1.1 %collective-permute-done.2 = bf16[432,128]{1,0:T(8,128)(2,1)S(1)} collective-permute-done((bf16[432,128]{1,0:T(8,128)(2,1)S(1)}, bf16[432,128]{1,0:T(8,128)(2,1)S(1)}, u32[]{:S(2)}, u32[]{:S(2)}) %collective-permute-start.2) | collective-permute-done | bytes 110624 | tf_op jit(solution)/shard_map/ppermute | solution.py:319
  35.5 0.2 collective-permute-done.6
  35.7 0.9 %collective-permute-start.9 = (bf16[8,18,32,128]{3,2,1,0:T(8,128)(2,1)S(1)}, bf16[8,18,32,128]{3,2,1,0:T(8,128)(2,1)S(1)}, u32[]{:S(2)}, u32[]{:S(2)}) collective-permute-start(bf16[8,18,32,128]{3,2,1,0:T(8,128)(2,1)S(1)} %all-to-all-done.mine_ref), channel_id=1, source_target_pairs={{0,8},{8,0},{16,24},{24,16},{32,40},{40,32},{48,56},{56,48},{64,72... | collective-permute-start | bytes 3538952 | tf_op jit(solution)/shard_map/ppermute | solution.py:319
  36.5 3.2 %collective-permute-start.8 = (bf16[432,128]{1,0:T(8,128)(2,1)S(1)}, bf16[432,128]{1,0:T(8,128)(2,1)S(1)}, u32[]{:S(2)}, u32[]{:S(2)}) collective-permute-start(bf16[432,128]{1,0:T(8,128)(2,1)S(1)} %add_convert_fusion), channel_id=1, source_target_pairs={{0,64},{8,72},{16,80},{24,88},{32,96},{40,104},{48,112},{56,120},{... | collective-permute-start | bytes 331784 | tf_op jit(solution)/shard_map/ppermute | solution.py:319
  39.7 0.7 %collective-permute-start.7 = (f32[4,32,256]{2,1,0:T(8,128)S(1)}, f32[4,32,256]{2,1,0:T(8,128)S(1)}, u32[]{:S(2)}, u32[]{:S(2)}) collective-permute-start(f32[4,32,256]{2,1,0:T(8,128)S(1)} %collective-permute-done.5), channel_id=1, source_target_pairs={{120,64},{121,65},{122,66},{123,67},{124,68},{125,69},{126,70},{12... | collective-permute-start | bytes 393224 | tf_op jit(solution)/shard_map/ppermute | solution.py:328
  40.4 1.8 %input_grad_local.1 = bf16[4,256,128]{2,1,0:T(8,128)(2,1)} custom-call(bf16[8,18,32,128]{3,2,1,0:T(8,128)(2,1)S(1)} %all-to-all-done.mine_ref, bf16[8,18,32,128]{3,2,1,0:T(8,128)(2,1)S(1)} %collective-permute-done.9.other_ref), custom_call_target="tpu_custom_call" | custom-call | flops 2000000000 | bytes 3000000 | tf_op jit(solution)/shard_map/input_grad_local/pallas_call | solution.py:269
  42.2 0.9 %collective-permute-done.8 = bf16[432,128]{1,0:T(8,128)(2,1)S(1)} collective-permute-done((bf16[432,128]{1,0:T(8,128)(2,1)S(1)}, bf16[432,128]{1,0:T(8,128)(2,1)S(1)}, u32[]{:S(2)}, u32[]{:S(2)}) %collective-permute-start.8) | collective-permute-done | bytes 110624 | tf_op jit(solution)/shard_map/ppermute | solution.py:319
  43.1 0.7 %collective-permute-start.10 = (f32[432,128]{1,0:T(8,128)S(1)}, f32[432,128]{1,0:T(8,128)S(1)}, u32[]{:S(2)}, u32[]{:S(2)}) collective-permute-start(f32[432,128]{1,0:T(8,128)S(1)} %convert_add_fusion.mine_ref), channel_id=1, source_target_pairs={{0,8},{8,0},{16,24},{24,16},{32,40},{40,32},{48,56},{56,48},{64,72... | collective-permute-start | bytes 663560 | tf_op jit(solution)/shard_map/ppermute | solution.py:319
  43.8 0.7 %fusion = bf16[4,32,1,256]{3,1,2,0:T(8,128)(2,1)} fusion(f32[4,32,256]{2,1,0:T(8,128)S(1)} %collective-permute-done.7, f32[4,32,256]{2,1,0:T(8,128)S(1)} %copy-done, f32[4,32,256]{2,1,0:T(8,128)S(1)} %collective-permute-done.6), kind=kLoop, calls=%fused_computation.4 | loop fusion | flops 98304 | bytes 458752
  44.5 0.4 collective-permute-done.10.theirs_ref
  44.9 0.8 %place.1 = f32[864,128]{1,0:T(8,128)} custom-call(f32[432,128]{1,0:T(8,128)S(1)} %convert_add_fusion.mine_ref, f32[432,128]{1,0:T(8,128)S(1)} %collective-permute-done.10.theirs_ref), custom_call_target="tpu_custom_call" | custom-call | tf_op jit(solution)/shard_map/place/pallas_call | solution.py:294
  (13 shorter events, 0.3 us)
Async XLA Ops:
  0.6 8.1 %collective-permute-start = (bf16[4,32,256]{2,1,0:T(8,128)(2,1)}, bf16[4,32,256]{2,1,0:T(8,128)(2,1)S(1)}, u32[]{:S(2)}, u32[]{:S(2)}) collective-permute-start(bf16[4,32,256]{2,1,0:T(8,128)(2,1)} %bitcast.17), channel_id=1, source_target_pairs={{8,0},{16,8},{24,16},{32,24},{40,32},{48,40},{56,48},{64,56},{72,6... | collective-permute-start | bytes 196616 | tf_op jit(solution)/shard_map/ppermute | solution.py:312
  8.7 0.6 %copy-start.1 = (bf16[4,32,256]{2,1,0:T(8,128)(2,1)}, bf16[4,32,256]{2,1,0:T(8,128)(2,1)S(1)}, u32[]{:S(2)}) copy-start(bf16[4,32,256]{2,1,0:T(8,128)(2,1)S(1)} %collective-permute-done.gn_ref) | copy-start | bytes 196612
  11.0 24.7 %all-to-all-start = ((bf16[8,18,32,128]{3,2,1,0:T(8,128)(2,1)}), bf16[8,18,32,128]{3,2,1,0:T(8,128)(2,1)S(1)}, u32[]{:S(2)}, u32[]{:S(2)}) async-start(bf16[8,18,32,128]{3,2,1,0:T(8,128)(2,1)} %next_cells.1), calls=%async_computation | async-start | bytes 2359296 | tf_op jit(solution)/shard_map/all_to_all | solution.py:303
  21.7 1.8 %collective-permute-start.1 = (f32[432,128]{1,0:T(8,128)}, f32[432,128]{1,0:T(8,128)S(1)}, u32[]{:S(2)}, u32[]{:S(2)}) collective-permute-start(f32[432,128]{1,0:T(8,128)} %get-tuple-element.18), channel_id=1, source_target_pairs={{0,8},{8,0},{16,24},{24,16},{32,40},{40,32},{48,56},{56,48},{64,72... | collective-permute-start | bytes 663560 | tf_op jit(solution)/shard_map/ppermute | solution.py:319
  24.4 9.7 %collective-permute-start.4 = (bf16[432,128]{1,0:T(8,128)(2,1)S(1)}, bf16[432,128]{1,0:T(8,128)(2,1)S(1)}, u32[]{:S(2)}, u32[]{:S(2)}) collective-permute-start(bf16[432,128]{1,0:T(8,128)(2,1)S(1)} %add_convert_fusion.1), channel_id=1, source_target_pairs={{0,32},{8,40},{16,48},{24,56},{32,0},{40,8},{48,16},{56,24},{64,96... | collective-permute-start | bytes 331784 | tf_op jit(solution)/shard_map/ppermute | solution.py:319
  27.4 6.8 %collective-permute-start.3 = (bf16[432,128]{1,0:T(8,128)(2,1)S(1)}, bf16[432,128]{1,0:T(8,128)(2,1)S(1)}, u32[]{:S(2)}, u32[]{:S(2)}) collective-permute-start(bf16[432,128]{1,0:T(8,128)(2,1)S(1)} %add_convert_fusion.1), channel_id=1, source_target_pairs={{0,48},{8,56},{16,32},{24,40},{32,16},{40,24},{48,0},{56,8},{64,11... | collective-permute-start | bytes 331784 | tf_op jit(solution)/shard_map/ppermute | solution.py:319
  29.5 6.0 %collective-permute-start.2 = (bf16[432,128]{1,0:T(8,128)(2,1)S(1)}, bf16[432,128]{1,0:T(8,128)(2,1)S(1)}, u32[]{:S(2)}, u32[]{:S(2)}) collective-permute-start(bf16[432,128]{1,0:T(8,128)(2,1)S(1)} %add_convert_fusion.1), channel_id=1, source_target_pairs={{0,16},{8,24},{16,0},{24,8},{32,48},{40,56},{48,32},{56,40},{64,80... | collective-permute-start | bytes 331784 | tf_op jit(solution)/shard_map/ppermute | solution.py:319
  29.9 5.7 %collective-permute-start.6 = (f32[4,32,256]{2,1,0:T(8,128)}, f32[4,32,256]{2,1,0:T(8,128)S(1)}, u32[]{:S(2)}, u32[]{:S(2)}) collective-permute-start(f32[4,32,256]{2,1,0:T(8,128)} %get-tuple-element.20), channel_id=1, source_target_pairs={{0,8},{8,16},{16,24},{24,32},{32,40},{40,48},{48,56},{64,72},{72,8... | collective-permute-start | bytes 393224 | tf_op jit(solution)/shard_map/ppermute | solution.py:323
  33.4 2.2 %collective-permute-start.5 = (f32[4,32,256]{2,1,0:T(8,128)}, f32[4,32,256]{2,1,0:T(8,128)S(1)}, u32[]{:S(2)}, u32[]{:S(2)}) collective-permute-start(f32[4,32,256]{2,1,0:T(8,128)} %get-tuple-element.20), channel_id=1, source_target_pairs={{56,120},{57,121},{58,122},{59,123},{60,124},{61,125},{62,126},{63... | collective-permute-start | bytes 393224 | tf_op jit(solution)/shard_map/ppermute | solution.py:322
  35.5 8.4 %copy-start = (f32[4,32,256]{2,1,0:T(8,128)S(1)}, f32[4,32,256]{2,1,0:T(8,128)}, u32[]{:S(2)}) copy-start(f32[4,32,256]{2,1,0:T(8,128)} %get-tuple-element.16) | copy-start | bytes 393220
  35.7 4.7 %collective-permute-start.9 = (bf16[8,18,32,128]{3,2,1,0:T(8,128)(2,1)S(1)}, bf16[8,18,32,128]{3,2,1,0:T(8,128)(2,1)S(1)}, u32[]{:S(2)}, u32[]{:S(2)}) collective-permute-start(bf16[8,18,32,128]{3,2,1,0:T(8,128)(2,1)S(1)} %all-to-all-done.mine_ref), channel_id=1, source_target_pairs={{0,8},{8,0},{16,24},{24,16},{32,40},{40,32},{48,56},{56,48},{64,72... | collective-permute-start | bytes 3538952 | tf_op jit(solution)/shard_map/ppermute | solution.py:319
  36.5 6.5 %collective-permute-start.8 = (bf16[432,128]{1,0:T(8,128)(2,1)S(1)}, bf16[432,128]{1,0:T(8,128)(2,1)S(1)}, u32[]{:S(2)}, u32[]{:S(2)}) collective-permute-start(bf16[432,128]{1,0:T(8,128)(2,1)S(1)} %add_convert_fusion), channel_id=1, source_target_pairs={{0,64},{8,72},{16,80},{24,88},{32,96},{40,104},{48,112},{56,120},{... | collective-permute-start | bytes 331784 | tf_op jit(solution)/shard_map/ppermute | solution.py:319
  39.7 4.1 %collective-permute-start.7 = (f32[4,32,256]{2,1,0:T(8,128)S(1)}, f32[4,32,256]{2,1,0:T(8,128)S(1)}, u32[]{:S(2)}, u32[]{:S(2)}) collective-permute-start(f32[4,32,256]{2,1,0:T(8,128)S(1)} %collective-permute-done.5), channel_id=1, source_target_pairs={{120,64},{121,65},{122,66},{123,67},{124,68},{125,69},{126,70},{12... | collective-permute-start | bytes 393224 | tf_op jit(solution)/shard_map/ppermute | solution.py:328
  43.1 1.8 %collective-permute-start.10 = (f32[432,128]{1,0:T(8,128)S(1)}, f32[432,128]{1,0:T(8,128)S(1)}, u32[]{:S(2)}, u32[]{:S(2)}) collective-permute-start(f32[432,128]{1,0:T(8,128)S(1)} %convert_add_fusion.mine_ref), channel_id=1, source_target_pairs={{0,8},{8,0},{16,24},{24,16},{32,40},{40,32},{48,56},{56,48},{64,72... | collective-permute-start | bytes 663560 | tf_op jit(solution)/shard_map/ppermute | solution.py:319
